TPU v7x, 32 devices: a whole 2x2x4 slice. The times are simulated.
32 devices in a mesh: row: 16 (over z, y, core), col: 2 (over x).
Axes of the slice: x: 2, y: 2, z: 4, core: 2. Of those that a mesh axis runs over, the one named last changes fastest.
Arguments:
- fine_matrix: bfloat16 [4096, 1536], P('row', 'col'), may hold values from -0.75 to 0.75
- fine_columns: int32 [64, 24], P('row'), may hold values from 0 to 63, as said below
- fine_counts: int32 [64], P('row'), may hold values from 12 to 24, as said below
- prolong: bfloat16 [4096, 128], P('row'), may hold values from -6 to 6
- prolong_columns: int32 [64, 2], P('row'), may hold values from 0 to 31
- restrict_rows: bfloat16 [2048, 256], P('row'), may hold values from -0.375 to 0.375
- coarse_pattern: int32 [16, 48], P('row'), may hold values from -1 to 31, as said below
Outputs:
- coarse_operator: float32 [2048, 3072], P('row', 'col')
Inputs may be any that keep to these rules, and one draw needn't show every extreme that they name: Only the first fine_counts[i] block slots of fine brick i are live. `fine_columns`: at most 4 block slots of each fine brick couple to a brick more than 8 bricks away, counting cyclically over the 64 bricks. `coarse_pattern`: each row holds distinct coarse brick numbers and -1 in slots left empty; every coarse brick reached by a live product of the slab is listed.
All inputs are finite; a program needn't handle non-finite values.
Results may differ from a plain program's by a relative error of at most 0.00035.
Values may be sent and summed in bfloat16 or wider, within the bound.
No kernel may reach another device: no remote copies, remote signals or barrier semaphores. Data moves between devices by JAX's collectives and lax.ppermute only.
A program may use at most 64 MiB of HBM per device.

v0:
```python
import jax
import jax.numpy as jnp
from jax import lax
from jax.sharding import PartitionSpec as P

BRICK = 64
P_SLOTS = 2


def make_folder(targets, totals, pieces):
    piece_blocks, piece_columns = pieces
    arrived = piece_columns.shape[0]
    matches = targets[:, None] == jnp.arange(arrived, dtype=jnp.int32)[None, :]
    gathered = jnp.einsum(
        "mn,nbc->mbc",
        matches.astype(jnp.bfloat16),
        piece_blocks,
        preferred_element_type=jnp.float32,
    )
    picked = totals[1] + jnp.sum(
        jnp.where(matches[:, :, None], piece_columns[None, :, :], 0), axis=1
    )
    return (gathered, picked)


def local(
    fine_matrix, fine_columns, fine_counts, prolong, prolong_columns, restrict_rows, coarse_pattern
):
    bricks = fine_counts.shape[0]
    share_width = fine_matrix.shape[1] // BRICK
    col_index = lax.axis_index("col")
    owned_first = col_index * share_width
    live_slots = (owned_first + jnp.arange(share_width, dtype=jnp.int32))[None, :] < fine_counts[
        :, None
    ]
    blocks = prolong.reshape(bricks, BRICK, P_SLOTS * BRICK)
    targets = lax.dynamic_slice_in_dim(fine_columns, owned_first, share_width, 1).reshape(-1)
    empty_sel = (
        jnp.zeros((targets.shape[0], BRICK, P_SLOTS * BRICK), jnp.float32),
        jnp.zeros((targets.shape[0], P_SLOTS), jnp.int32),
    )
    chosen, reached = make_folder(
        targets,
        empty_sel,
        (
            lax.all_gather(blocks, "row", axis=0, tiled=True),
            lax.all_gather(prolong_columns, "row", axis=0, tiled=True),
        ),
    )
    chosen = chosen.astype(jnp.bfloat16).reshape(bricks, share_width, BRICK, P_SLOTS * BRICK)
    reached = reached.reshape(bricks, share_width, P_SLOTS)
    a_blocks = fine_matrix.reshape(bricks, BRICK, share_width, BRICK)
    products = jnp.einsum("iakb,ikbc->ikac", a_blocks, chosen, preferred_element_type=jnp.float32)
    products = products.reshape(bricks, share_width, BRICK, P_SLOTS, BRICK)
    pattern = coarse_pattern[0]
    matches = (
        (reached[:, :, :, None] == pattern[None, None, None, :]) & live_slots[:, :, None, None]
    ).astype(jnp.float32)
    partial_value = jnp.einsum(
        "ikqs,ikaqc->iasc", matches, products, precision=lax.Precision.HIGHEST
    )
    partial_value = partial_value.reshape(bricks * BRICK, pattern.shape[0] * BRICK)
    restrict = restrict_rows.astype(jnp.float32)
    owned_sums = lax.psum_scatter(partial_value, "col", scatter_dimension=1, tiled=True)
    return jnp.dot(restrict, owned_sums, precision=lax.Precision.HIGHEST)


def solution(mesh):
    return jax.shard_map(
        local,
        mesh=mesh,
        in_specs=(
            P("row", "col"),
            P("row", None),
            P("row"),
            P("row", None),
            P("row", None),
            P("row", None),
            P("row", None),
        ),
        out_specs=P("row", "col"),
        check_vma=False,
    )
```

profile of v0, /device:TPU:0, one launch (start us, length us, event | category | flops | bytes accessed | tf_op | source)
XLA Modules:
  0.0 123.4 jit_solution(1021751907928465593)
XLA Ops:
  6.5 0.0 copy-start
  6.5 0.0 all-gather.3.cloned.1.call-start
  6.5 0.7 all-gather.3.cloned.1.call-update
  7.3 0.0 reduce-scatter.2.cloned.1.call-start
  7.3 0.8 constant_dynamic-slice_fusion
  8.1 0.1 eq.36
  8.2 23.3 %all-gather = s32[16,4,2]{1,2,0:T(2,128)S(1)} all-gather(s32[1,4,2]{1,2,0:T(2,128)} %bitcast.34), channel_id=1, replica_groups=mesh['row'=16,'col'=2] {'row'}, dimensions={0}, use_global_device_ids=true | all-gather | bytes 544 | tf_op jit(solution)/shard_map/all_gather | solution.py:47
  31.5 0.1 reshape.80
  31.6 0.1 iota_compare_fusion
  31.7 0.1 select_reduce_fusion
  31.8 0.1 eq.40
  31.9 1.7 %reshape.84 = bf16[4,64,12,64]{3,2,1,0:T(8,128)(2,1)S(1)} reshape(bf16[256,768]{1,0:T(8,128)(2,1)} %param.7) | data formatting | bytes 786432 | tf_op jit(solution)/shard_map/reshape | solution.py:52
  33.6 0.7 broadcast_compare_fusion
  34.3 15.9 %all-gather.3.cloned.1.call-done = bf16[64,64,128]{2,1,0:T(8,128)(2,1)} async-done(((bf16[4,64,128]{2,1,0:T(8,128)(2,1)}), bf16[64,64,128]{2,1,0:T(8,128)(2,1)}) %all-gather.3.cloned.1.call-update) | async-done | bytes 1048592 | tf_op jit(solution)/shard_map/all_gather | solution.py:46
  50.2 2.1 %convolution_convert_fusion = bf16[48,64,128]{2,0,1:T(8,128)(2,1)S(1)} fusion(bf16[64,64,128]{2,1,0:T(8,128)(2,1)} %all-gather.3.cloned.1.call-done, s32[48]{0:T(128)S(1)} %eq.36), kind=kOutput, calls=%fused_computation.5 | convolution fusion | flops 50727936 | bytes 1835200 | tf_op jit(solution)/shard_map/mn,nbc->mbc/dot_general | solution.py:14
  52.3 0.2 copy.34
  52.5 1.5 %convolution_bitcast_fusion.1 = f32[4,12,64,128]{3,2,1,0:T(8,128)} fusion(bf16[4,12,64,128]{3,2,1,0:T(8,128)(2,1)S(1)} %bitcast.32, bf16[4,64,12,64]{3,2,1,0:T(8,128)(2,1)S(1)} %reshape.84), kind=kOutput, calls=%fused_computation.4 | convolution fusion | flops 50331648 | bytes 2752512 | tf_op jit(solution)/shard_map/iakb,ikbc->ikac/dot_general | solution.py:53
  54.0 0.0 copy-start.1
  54.1 3.2 %reshape.77 = f32[4,12,64,2,64]{4,3,2,1,0:T(2,128)S(1)} reshape(f32[4,12,64,128]{3,2,1,0:T(8,128)} %convolution_bitcast_fusion.1) | data formatting | bytes 3145728 | tf_op jit(solution)/shard_map/reshape | solution.py:54
  57.3 0.0 copy-done.1
  57.3 7.1 %fusion.2 = f32[4,64,48,64]{3,2,1,0:T(8,128)} fusion(f32[4,12,64,2,64]{4,3,2,1,0:T(2,128)S(1)} %reshape.77, s32[48]{0:T(128)S(1)} %bitcast.35, s32[4,12,2]{1,2,0:T(2,128)S(1)} %copy.38, pred[4,12]{1,0:T(4,128)(4,1)S(1)} %broadcast_compare_fusion), kind=kOutput, calls=%fused_computation.2 | convolution fusion | flops 226501632 | bytes 4719216 | tf_op jit(solution)/shard_map/ikqs,ikaqc->iasc/dot_general | solution.py:59
  64.4 5.8 %reshape.78 = f32[256,3072]{1,0:T(8,128)} reshape(f32[4,64,48,64]{3,2,1,0:T(8,128)} %fusion.2) | data formatting | bytes 6291456 | tf_op jit(solution)/shard_map/reshape | solution.py:62
  70.2 0.0 reduce-scatter.2.cloned.1.call-update
  70.2 42.4 %reduce-scatter.2.cloned.1.call-done = f32[256,1536]{1,0:T(8,128)} async-done(((f32[256,3072]{1,0:T(8,128)}), f32[256,1536]{1,0:T(8,128)}) %reduce-scatter.2.cloned.1.call-update) | async-done | bytes 1572880 | tf_op jit(solution)/shard_map/reduce_scatter | solution.py:64
  112.6 0.0 copy-done
  112.6 2.8 %convolution_bitcast_fusion = f32[128,1536]{0,1:T(8,128)S(1)} fusion(f32[256,1536]{1,0:T(8,128)} %reduce-scatter.2.cloned.1.call-done, bf16[128,256]{1,0:T(8,128)(2,1)S(1)} %copy-done), kind=kOutput, calls=%fused_computation.3 | convolution fusion | flops 603979776 | bytes 2424832 | tf_op jit(solution)/shard_map/dot_general | solution.py:65
  115.4 1.1 copy.40
  (3 shorter events, 0.0 us)
Async XLA Ops:
  6.5 106.1 %copy-start = (bf16[128,256]{1,0:T(8,128)(2,1)S(1)}, bf16[128,256]{1,0:T(8,128)(2,1)}, u32[]{:S(2)}) copy-start(bf16[128,256]{1,0:T(8,128)(2,1)} %param.12) | copy-start | bytes 196612
  6.5 43.7 %all-gather.3.cloned.1.call-start = ((), (), s32[]{:S(2)}) async-start(), calls=%async_computation.1 | async-start | bytes 1114112 | tf_op jit(solution)/shard_map/all_gather | solution.py:46
  7.3 105.4 %reduce-scatter.2.cloned.1.call-start = ((), (), s32[]{:S(2)}) async-start(), calls=%async_computation.2 | async-start | bytes 4718592 | tf_op jit(solution)/shard_map/reduce_scatter | solution.py:64
  54.0 3.2 %copy-start.1 = (s32[1,48]{1,0:T(1,128)S(1)}, s32[1,48]{1,0:T(1,128)}, u32[]{:S(2)}) copy-start(s32[1,48]{1,0:T(1,128)} %param.13) | copy-start | bytes 580
Sparse Core Ops, SparseCore 0:
  9.5 40.6 all-gather.2
  70.3 42.2 reduce-scatter.1
where the time goes:
time: 124 us; the launch traced here: 123 us
  waiting for transfers between devices  59.1 us (48%)
  blocking collectives  23.3 us (19%)
  matrix products  13.5 us (11%)
  between operations  13.5 us (11%)
  local copies, waits for them, and re-layouts  13.1 us (11%)
    reduce_scatter x1, waiting for transfers between devices, local(): lax.psum_scatter(partial_value, 'col', scatter_dimension=1, tiled=True)  42.4 us
    all_gather x1, blocking collectives, local(): lax.all_gather(prolong_columns, 'row', axis=0, tiled=True)  23.3 us
    all_gather x1, waiting for transfers between devices, local(): lax.all_gather(blocks, 'row', axis=0, tiled=True)  15.9 us
    dot_general x1, matrix products, local(): jnp.einsum('ikqs,ikaqc->iasc', matches, products, precision=lax.Precision...  7.08 us
    reshape x1, local copies, waits for them, and re-layouts, local(): partial_value.reshape(bricks * BRICK, pattern.shape[0] * BRICK)  5.8 us
    reshape x1, local copies, waits for them, and re-layouts, local(): products = products.reshape(bricks, share_width, BRICK, P_SLOTS, BRICK)  3.22 us
    dot_general x1, matrix products, local(): return jnp.dot(restrict, owned_sums, precision=lax.Precision.HIGHEST)  2.82 us
  transfers between devices with their start and end apart: 2, of which 2 were waited for; matrix products, arithmetic and copies ran while one was open for 3% of the time, Pallas kernels for 0%

commit v1 on v0

v1 whole, which is shorter than its diff:
```python
import functools

import jax
import jax.numpy as jnp
from jax import lax
from jax.experimental import pallas as pl
from jax.experimental.pallas import tpu as pltpu
from jax.sharding import PartitionSpec as P

BRICK = 64
P_SLOTS = 2
DIGIT = 128
LANES = 128
EXTRA = 16


def pack_kernel(columns_ref, prolong_ref, packed_ref):
    rows = prolong_ref.shape[0]
    packed_ref[:rows, :] = prolong_ref[...]
    row = lax.broadcasted_iota(jnp.int32, (EXTRA, LANES), 0)
    lane = lax.broadcasted_iota(jnp.int32, (EXTRA, LANES), 1)
    digits = jnp.zeros((EXTRA, LANES), jnp.int32)
    for brick in range(columns_ref.shape[0]):
        for q in range(P_SLOTS):
            value = columns_ref[brick, q]
            here = lane == brick * P_SLOTS + q
            digits = jnp.where(here & (row == 0), value % DIGIT, digits)
            digits = jnp.where(here & (row == 1), value // DIGIT, digits)
    packed_ref[rows:, :] = digits.astype(jnp.float32).astype(jnp.bfloat16)


def pack(prolong, prolong_columns):
    return pl.pallas_call(
        pack_kernel,
        out_shape=jax.ShapeDtypeStruct((prolong.shape[0] + EXTRA, LANES), jnp.bfloat16),
        in_specs=[
            pl.BlockSpec(memory_space=pltpu.SMEM),
            pl.BlockSpec(memory_space=pltpu.VMEM),
        ],
        out_specs=pl.BlockSpec(memory_space=pltpu.VMEM),
        name="pack",
    )(prolong_columns, prolong)


def swap(block, axis, size, mask):
    return lax.ppermute(block, axis, [(i, i ^ mask) for i in range(size)])


def gather_row(packed, size):
    if size & (size - 1) or size < 8 or size > 32:
        return [lax.all_gather(packed, "row", axis=0, tiled=True)], False
    pieces = {0: packed}
    for mask in (8, 12, 4, 16, 20, 24, 28):
        if mask < size:
            pieces[mask] = swap(packed, "row", size, mask)
    for mask in sorted(pieces):
        pieces[mask | 2] = swap(pieces[mask], "row", size, 2)
    for mask in sorted(pieces):
        pieces[mask | 1] = swap(pieces[mask], "row", size, 1)
    return [pieces[mask] for mask in range(size)], True


def operator_kernel(
    slabs, by_xor, columns_ref, counts_ref, pattern_ref, restrict_ref, *refs, cols, parts
):
    fines = refs[:cols]
    pieces = refs[cols : cols + parts]
    out_ref, held_ref, seen_ref, reached_ref, slot_ref, sums_ref, sem = refs[cols + parts :]
    bricks, slots = columns_ref.shape
    share = slots // cols
    owned = pattern_ref.shape[1] // cols
    rows = bricks * BRICK + EXTRA
    row_index = lax.axis_index("row")
    col_index = lax.axis_index("col")

    if parts > 1:
        for at, piece in enumerate(pieces):
            held_ref[at * rows : (at + 1) * rows, :] = piece[...]
        source = held_ref
    else:
        source = pieces[0]
    for at in range(slabs):
        first = at * rows + bricks * BRICK
        digits = source[first : first + EXTRA, :].astype(jnp.float32)
        seen_ref[at : at + 1, :] = (digits[0:1, :] + DIGIT * digits[1:2, :]).astype(jnp.int32)
    move = pltpu.make_async_copy(seen_ref, reached_ref, sem)
    move.start()

    owned_first = col_index * owned
    for s in range(owned * cols):
        mine = s - owned_first
        mine = jnp.where((mine >= 0) & (mine < owned), mine, owned)
        slot_ref[pattern_ref[0, s] + 1] = mine
    sums_ref[...] = jnp.zeros_like(sums_ref)
    left = lax.broadcasted_iota(jnp.int32, (BRICK, LANES), 1) < BRICK
    nothing = jnp.zeros((BRICK, LANES), jnp.bfloat16)
    move.wait()

    for i in range(bricks):
        for part in range(cols):
            part_first = (col_index ^ part) * share if cols > 1 else 0
            for pair in range(share // 2):
                blocks, where_to = [], []
                for half in range(2):
                    k = part_first + pair * 2 + half
                    brick = columns_ref[i, k]
                    slab = lax.div(brick, bricks)
                    inner = brick - slab * bricks
                    if by_xor:
                        slab = slab ^ row_index
                    start = pl.multiple_of(slab * rows + inner * BRICK, 16)
                    blocks.append(source[pl.ds(start, BRICK), :])
                    live = k < counts_ref[i]
                    for q in range(P_SLOTS):
                        coarse = reached_ref[slab, inner * P_SLOTS + q]
                        where_to.append(jnp.where(live, slot_ref[coarse + 1], owned))
                right = jnp.concatenate(
                    [
                        jnp.concatenate([blocks[0], nothing], axis=1),
                        jnp.concatenate([nothing, blocks[1]], axis=1),
                    ],
                    axis=0,
                )
                a = fines[part][i * BRICK : (i + 1) * BRICK, pair * LANES : (pair + 1) * LANES]
                product = jnp.dot(a, right, preferred_element_type=jnp.float32)
                for half in range(2):
                    block = product[:, half * LANES : (half + 1) * LANES]
                    sums_ref[i, where_to[half * 2]] += jnp.where(left, block, 0.0)
                    sums_ref[i, where_to[half * 2 + 1]] += jnp.where(left, 0.0, block)

    restrict = restrict_ref[...]
    for pair in range(owned // 2):
        high, low = [], []
        for i in range(bricks):
            even, odd = sums_ref[i, 2 * pair], sums_ref[i, 2 * pair + 1]
            total = jnp.where(left, even, odd) + pltpu.roll(
                jnp.where(left, odd, even), BRICK, 1
            )
            top = total.astype(jnp.bfloat16)
            high.append(top)
            low.append((total - top.astype(jnp.float32)).astype(jnp.bfloat16))
        high = jnp.concatenate(high, axis=0)
        low = jnp.concatenate(low, axis=0)
        out_ref[:, pair * LANES : (pair + 1) * LANES] = jnp.dot(
            restrict, high, preferred_element_type=jnp.float32
        ) + jnp.dot(restrict, low, preferred_element_type=jnp.float32)


def local(
    slabs,
    cols,
    fine_matrix,
    fine_columns,
    fine_counts,
    prolong,
    prolong_columns,
    restrict_rows,
    coarse_pattern,
):
    bricks = fine_counts.shape[0]
    owned = coarse_pattern.shape[1] // cols
    coarse = restrict_rows.shape[0] // BRICK * slabs
    packed = pack(prolong, prolong_columns)
    pieces, by_xor = gather_row(packed, slabs)
    fines = [fine_matrix] + [swap(fine_matrix, "col", cols, d) for d in range(1, cols)]
    rows = packed.shape[0]
    smem = pl.BlockSpec(memory_space=pltpu.SMEM)
    vmem = pl.BlockSpec(memory_space=pltpu.VMEM)
    held_rows = slabs * rows if len(pieces) > 1 else 16
    return pl.pallas_call(
        functools.partial(operator_kernel, slabs, by_xor, cols=cols, parts=len(pieces)),
        out_shape=jax.ShapeDtypeStruct((restrict_rows.shape[0], owned * BRICK), jnp.float32),
        in_specs=[smem] * 3 + [vmem] * (1 + cols + len(pieces)),
        out_specs=vmem,
        scratch_shapes=[
            pltpu.VMEM((held_rows, LANES), jnp.bfloat16),
            pltpu.VMEM((slabs, LANES), jnp.int32),
            pltpu.SMEM((slabs, LANES), jnp.int32),
            pltpu.SMEM((coarse + 1,), jnp.int32),
            pltpu.VMEM((bricks, owned + 1, BRICK, LANES), jnp.float32),
            pltpu.SemaphoreType.DMA,
        ],
        compiler_params=pltpu.CompilerParams(vmem_limit_bytes=32 * 1024 * 1024),
        name="operator",
    )(fine_columns, fine_counts, coarse_pattern, restrict_rows, *fines, *pieces)


def solution(mesh):
    return jax.shard_map(
        functools.partial(local, mesh.shape["row"], mesh.shape["col"]),
        mesh=mesh,
        in_specs=(
            P("row", "col"),
            P("row", None),
            P("row"),
            P("row", None),
            P("row", None),
            P("row", None),
            P("row", None),
        ),
        out_specs=P("row", "col"),
        check_vma=False,
    )
```

time: 124 us -> 32.2 us (0.26)
  waiting for transfers between devices: 59.1 us -> 8.3 us
  blocking collectives: 23.3 us -> 0 us
  starting transfers between devices: 0.04 us -> 14.4 us
  matrix products: 13.5 us -> 0 us
  between operations: 13.5 us -> 0.05 us
  local copies, waits for them, and re-layouts: 13.1 us -> 3.21 us
  Pallas kernels: 0 us -> 6.04 us
    reduce_scatter x1 -> x0, waiting for transfers between devices: 42.4 us -> none  [local(): lax.psum_scatter(partial_value, 'col', scatter_dimension=1, tiled=True)]
    all_gather x1 -> x0, blocking collectives: 23.3 us -> none  [local(): lax.all_gather(prolong_columns, 'row', axis=0, tiled=True)]
    all_gather x1 -> x0, waiting for transfers between devices: 15.9 us -> none  [local(): lax.all_gather(blocks, 'row', axis=0, tiled=True)]
    ppermute x0 -> x16, starting transfers between devices: none -> 14.4 us  [swap(): return lax.ppermute(block, axis, [(i, i ^ mask) for i in range(size)])]
    dot_general x4 -> x0, matrix products: 13.5 us -> none  [the longest x1 7.08 us: local(): jnp.einsum('ikqs,ikaqc->iasc', matches, products, precision=lax.Precision...]
    reshape x3 -> x0, local copies, waits for them, and re-layouts: 10.7 us -> none  [the longest x1 5.8 us: local(): partial_value.reshape(bricks * BRICK, pattern.shape[0] * BRICK)]
    ppermute x0 -> x16, waiting for transfers between devices: none -> 8.3 us  [swap(): return lax.ppermute(block, axis, [(i, i ^ mask) for i in range(size)])]
    pallas_call x0 -> x2, Pallas kernels: none -> 6.04 us  [the longest x1 4.45 us: local(): pl.pallas_call(functools.partial(operator_kernel, slabs, by_xor, cols=col...]
  transfers between devices with their start and end apart: 2 -> 16, of which waited for: 2 -> 7; matrix products, arithmetic and copies ran while one was open for 3% -> 4% of each run, Pallas kernels for 0% -> 5%
where the time goes in v1:
time: 32.2 us; the launch traced here: 31.9 us
  starting transfers between devices  14.4 us (45%)
  waiting for transfers between devices  8.3 us (26%)
  Pallas kernels  6.04 us (19%)
  local copies, waits for them, and re-layouts  3.21 us (10%)
    ppermute x16, starting transfers between devices, swap(): return lax.ppermute(block, axis, [(i, i ^ mask) for i in range(size)])  14.4 us
    ppermute x16, waiting for transfers between devices, swap(): return lax.ppermute(block, axis, [(i, i ^ mask) for i in range(size)])  8.3 us
    pallas_call x1, Pallas kernels, local(): pl.pallas_call(functools.partial(operator_kernel, slabs, by_xor, cols=col...  4.45 us
    unnamed x13, local copies, waits for them, and re-layouts  3.21 us
    pallas_call x1, Pallas kernels, pack(): pl.pallas_call(pack_kernel, out_shape=jax.ShapeDtypeStruct((prolong.shape...  1.59 us
  transfers between devices with their start and end apart: 16, of which 7 were waited for; matrix products, arithmetic and copies ran while one was open for 4% of the time, Pallas kernels for 5%

profile of v1, /device:TPU:0, one launch (start us, length us, event | category | flops | bytes accessed | tf_op | source)
XLA Modules:
  0.0 31.9 jit_solution(18152788656745841957)
XLA Ops:
  0.0 2.9 %collective-permute-start = (bf16[256,768]{1,0:T(8,128)(2,1)}, bf16[256,768]{1,0:T(8,128)(2,1)S(1)}, u32[]{:S(2)}, u32[]{:S(2)}) collective-permute-start(bf16[256,768]{1,0:T(8,128)(2,1)} %refs_0_.1), channel_id=1, source_target_pairs={{0,1},{1,0},{2,3},{3,2},{4,5},{5,4},{6,7},{7,6},{8,9},{9,8},{10,11... | collective-permute-start | bytes 1179656 | tf_op jit(solution)/shard_map/ppermute | solution.py:46
  2.9 1.3 %copy.8.columns_ref = s32[4,2]{1,0:T(4,128)} copy(s32[4,2]{0,1:T(2,128)} %param.11) | data formatting | bytes 64 | tf_op args[4]
  4.3 0.0 copy-start.2
  4.3 0.0 copy-start.3
  4.3 0.0 copy-start.4
  4.3 0.0 copy-start.5
  4.3 1.6 %pack.1.refs_2_ = bf16[272,128]{1,0:T(8,128)(2,1)} custom-call(s32[4,2]{1,0:T(4,128)} %copy.8.columns_ref, bf16[256,128]{1,0:T(8,128)(2,1)} %prolong_ref.1), custom_call_target="tpu_custom_call" | custom-call | tf_op jit(solution)/shard_map/pack/pallas_call | solution.py:33
  5.9 3.6 %collective-permute-start.12 = (bf16[272,128]{1,0:T(8,128)(2,1)}, bf16[272,128]{1,0:T(8,128)(2,1)S(1)}, u32[]{:S(2)}, u32[]{:S(2)}) collective-permute-start(bf16[272,128]{1,0:T(8,128)(2,1)} %pack.1.refs_2_), channel_id=1, source_target_pairs={{0,24},{2,26},{4,28},{6,30},{8,16},{10,18},{12,20},{14,22},{16,8},... | collective-permute-start | bytes 208904 | tf_op jit(solution)/shard_map/ppermute | solution.py:46
  9.5 0.0 collective-permute-start.8
  9.5 0.8 %collective-permute-start.4 = (bf16[272,128]{1,0:T(8,128)(2,1)}, bf16[272,128]{1,0:T(8,128)(2,1)S(1)}, u32[]{:S(2)}, u32[]{:S(2)}) collective-permute-start(bf16[272,128]{1,0:T(8,128)(2,1)} %pack.1.refs_2_), channel_id=1, source_target_pairs={{0,8},{2,10},{4,12},{6,14},{8,0},{10,2},{12,4},{14,6},{16,24},{18,... | collective-permute-start | bytes 208904 | tf_op jit(solution)/shard_map/ppermute | solution.py:46
  10.3 1.5 %collective-permute-start.2 = (bf16[272,128]{1,0:T(8,128)(2,1)}, bf16[272,128]{1,0:T(8,128)(2,1)S(1)}, u32[]{:S(2)}, u32[]{:S(2)}) collective-permute-start(bf16[272,128]{1,0:T(8,128)(2,1)} %pack.1.refs_2_), channel_id=1, source_target_pairs={{0,4},{2,6},{4,0},{6,2},{8,12},{10,14},{12,8},{14,10},{16,20},{18,... | collective-permute-start | bytes 208904 | tf_op jit(solution)/shard_map/ppermute | solution.py:46
  11.8 1.3 %collective-permute-done.12.refs_14_ = bf16[272,128]{1,0:T(8,128)(2,1)S(1)} collective-permute-done((bf16[272,128]{1,0:T(8,128)(2,1)}, bf16[272,128]{1,0:T(8,128)(2,1)S(1)}, u32[]{:S(2)}, u32[]{:S(2)}) %collective-permute-start.12) | collective-permute-done | bytes 69664 | tf_op jit(solution)/shard_map/ppermute | solution.py:46
  13.0 0.0 collective-permute-start.1
  13.0 2.3 %collective-permute-done.8.refs_10_ = bf16[272,128]{1,0:T(8,128)(2,1)S(1)} collective-permute-done((bf16[272,128]{1,0:T(8,128)(2,1)}, bf16[272,128]{1,0:T(8,128)(2,1)S(1)}, u32[]{:S(2)}, u32[]{:S(2)}) %collective-permute-start.8) | collective-permute-done | bytes 69664 | tf_op jit(solution)/shard_map/ppermute | solution.py:46
  15.4 1.5 %collective-permute-start.14 = (bf16[272,128]{1,0:T(8,128)(2,1)S(1)}, bf16[272,128]{1,0:T(8,128)(2,1)S(1)}, u32[]{:S(2)}, u32[]{:S(2)}) collective-permute-start(bf16[272,128]{1,0:T(8,128)(2,1)S(1)} %collective-permute-done.12.refs_14_), channel_id=1, source_target_pairs={{0,4},{2,6},{4,0},{6,2},{8,12},{10,14},{12,8},{14,10},{16,20},{18,... | collective-permute-start | bytes 208904 | tf_op jit(solution)/shard_map/ppermute | solution.py:46
  16.9 0.0 collective-permute-done.4.refs_6_
  16.9 0.0 collective-permute-start.13
  16.9 0.0 collective-permute-done.2.refs_4_
  16.9 0.6 %collective-permute-start.10 = (bf16[272,128]{1,0:T(8,128)(2,1)S(1)}, bf16[272,128]{1,0:T(8,128)(2,1)S(1)}, u32[]{:S(2)}, u32[]{:S(2)}) collective-permute-start(bf16[272,128]{1,0:T(8,128)(2,1)S(1)} %collective-permute-done.8.refs_10_), channel_id=1, source_target_pairs={{0,4},{2,6},{4,0},{6,2},{8,12},{10,14},{12,8},{14,10},{16,20},{18,... | collective-permute-start | bytes 208904 | tf_op jit(solution)/shard_map/ppermute | solution.py:46
  17.5 0.0 collective-permute-done.1.refs_3_
  17.5 0.2 collective-permute-start.9
  17.6 2.0 %collective-permute-done.14.refs_16_ = bf16[272,128]{1,0:T(8,128)(2,1)S(1)} collective-permute-done((bf16[272,128]{1,0:T(8,128)(2,1)S(1)}, bf16[272,128]{1,0:T(8,128)(2,1)S(1)}, u32[]{:S(2)}, u32[]{:S(2)}) %collective-permute-start.14) | collective-permute-done | bytes 69664 | tf_op jit(solution)/shard_map/ppermute | solution.py:46
  19.7 2.2 %collective-permute-start.6 = (bf16[272,128]{1,0:T(8,128)(2,1)S(1)}, bf16[272,128]{1,0:T(8,128)(2,1)S(1)}, u32[]{:S(2)}, u32[]{:S(2)}) collective-permute-start(bf16[272,128]{1,0:T(8,128)(2,1)S(1)} %collective-permute-done.4.refs_6_), channel_id=1, source_target_pairs={{0,4},{2,6},{4,0},{6,2},{8,12},{10,14},{12,8},{14,10},{16,20},{18,... | collective-permute-start | bytes 208904 | tf_op jit(solution)/shard_map/ppermute | solution.py:46
  21.9 0.0 collective-permute-done.13.refs_15_
  21.9 0.0 collective-permute-start.5
  21.9 0.1 collective-permute-done.10.refs_12_
  21.9 0.5 %collective-permute-start.3 = (bf16[272,128]{1,0:T(8,128)(2,1)S(1)}, bf16[272,128]{1,0:T(8,128)(2,1)S(1)}, u32[]{:S(2)}, u32[]{:S(2)}) collective-permute-start(bf16[272,128]{1,0:T(8,128)(2,1)S(1)} %collective-permute-done.2.refs_4_), channel_id=1, source_target_pairs={{0,2},{2,0},{4,6},{6,4},{8,10},{10,8},{12,14},{14,12},{16,18},{18,... | collective-permute-start | bytes 208904 | tf_op jit(solution)/shard_map/ppermute | solution.py:46
  22.4 0.0 collective-permute-done.9.refs_11_
  22.4 0.1 collective-permute-start.15
  22.5 1.7 %collective-permute-done.6.refs_8_ = bf16[272,128]{1,0:T(8,128)(2,1)S(1)} collective-permute-done((bf16[272,128]{1,0:T(8,128)(2,1)S(1)}, bf16[272,128]{1,0:T(8,128)(2,1)S(1)}, u32[]{:S(2)}, u32[]{:S(2)}) %collective-permute-start.6) | collective-permute-done | bytes 69664 | tf_op jit(solution)/shard_map/ppermute | solution.py:46
  24.2 0.0 collective-permute-start.11
  24.2 0.0 collective-permute-done.5.refs_7_
  24.2 0.5 %collective-permute-start.7 = (bf16[272,128]{1,0:T(8,128)(2,1)S(1)}, bf16[272,128]{1,0:T(8,128)(2,1)S(1)}, u32[]{:S(2)}, u32[]{:S(2)}) collective-permute-start(bf16[272,128]{1,0:T(8,128)(2,1)S(1)} %collective-permute-done.6.refs_8_), channel_id=1, source_target_pairs={{0,2},{2,0},{4,6},{6,4},{8,10},{10,8},{12,14},{14,12},{16,18},{18,... | collective-permute-start | bytes 208904 | tf_op jit(solution)/shard_map/ppermute | solution.py:46
  24.7 0.0 collective-permute-done.3.refs_5_
  24.7 0.0 collective-permute-done.15.refs_17_
  24.7 0.7 %collective-permute-done.11.refs_13_ = bf16[272,128]{1,0:T(8,128)(2,1)S(1)} collective-permute-done((bf16[272,128]{1,0:T(8,128)(2,1)S(1)}, bf16[272,128]{1,0:T(8,128)(2,1)S(1)}, u32[]{:S(2)}, u32[]{:S(2)}) %collective-permute-start.11) | collective-permute-done | bytes 69664 | tf_op jit(solution)/shard_map/ppermute | solution.py:46
  25.4 0.2 collective-permute-done.7.refs_9_
  25.6 0.0 collective-permute-done.refs_1_
  25.6 0.0 copy-done.2
  25.6 0.0 copy-done.3
  25.6 0.0 copy-done.4
  25.6 0.0 copy-done.5
  25.6 0.0 copy-start
  25.6 1.0 %copy-done = bf16[256,768]{1,0:T(8,128)(2,1)S(1)} copy-done((bf16[256,768]{1,0:T(8,128)(2,1)S(1)}, bf16[256,768]{1,0:T(8,128)(2,1)}, u32[]{:S(2)}) %copy-start) | copy-done | bytes 393240
  26.6 0.0 copy-start.1
  26.6 0.9 %copy-done.1 = bf16[272,128]{1,0:T(8,128)(2,1)S(1)} copy-done((bf16[272,128]{1,0:T(8,128)(2,1)S(1)}, bf16[272,128]{1,0:T(8,128)(2,1)}, u32[]{:S(2)}) %copy-start.1) | copy-done | bytes 69656
  27.5 4.4 %operator.1 = f32[128,1536]{1,0:T(8,128)} custom-call(s32[4,24]{1,0:T(4,128)S(1)} %copy-done.3, s32[4]{0:T(128)S(1)} %copy-done.4, s32[1,48]{1,0:T(1,128)S(1)} %copy-done.5, bf16[128,256]{1,0:T(8,128)(2,1)S(1)} %copy-done.2, bf16[256,768]{1,0:T(8,128)(2,1)S(1)} %copy-done, bf16[256,768]{1,0:T(8,128)(2,1)S(1)} %collective-permute-done.refs_1_, ...), custom_call_target="tpu_custom_call" | custom-call | tf_op jit(solution)/shard_map/operator/pallas_call | solution.py:170
Async XLA Ops:
  0.0 25.6 %collective-permute-start = (bf16[256,768]{1,0:T(8,128)(2,1)}, bf16[256,768]{1,0:T(8,128)(2,1)S(1)}, u32[]{:S(2)}, u32[]{:S(2)}) collective-permute-start(bf16[256,768]{1,0:T(8,128)(2,1)} %refs_0_.1), channel_id=1, source_target_pairs={{0,1},{1,0},{2,3},{3,2},{4,5},{5,4},{6,7},{7,6},{8,9},{9,8},{10,11... | collective-permute-start | bytes 1179656 | tf_op jit(solution)/shard_map/ppermute | solution.py:46
  4.3 21.3 %copy-start.2 = (bf16[128,256]{1,0:T(8,128)(2,1)S(1)}, bf16[128,256]{1,0:T(8,128)(2,1)}, u32[]{:S(2)}) copy-start(bf16[128,256]{1,0:T(8,128)(2,1)} %restrict_ref.1) | copy-start | bytes 196612
  4.3 21.3 %copy-start.3 = (s32[4,24]{1,0:T(4,128)S(1)}, s32[4,24]{1,0:T(4,128)}, u32[]{:S(2)}) copy-start(s32[4,24]{1,0:T(4,128)} %columns_ref.2) | copy-start | bytes 1156
  4.3 21.3 %copy-start.4 = (s32[4]{0:T(128)S(1)}, s32[4]{0:T(128)}, u32[]{:S(2)}) copy-start(s32[4]{0:T(128)} %counts_ref.1) | copy-start | bytes 52
  4.3 21.3 %copy-start.5 = (s32[1,48]{1,0:T(1,128)S(1)}, s32[1,48]{1,0:T(1,128)}, u32[]{:S(2)}) copy-start(s32[1,48]{1,0:T(1,128)} %pattern_ref.1) | copy-start | bytes 580
  5.9 7.2 %collective-permute-start.12 = (bf16[272,128]{1,0:T(8,128)(2,1)}, bf16[272,128]{1,0:T(8,128)(2,1)S(1)}, u32[]{:S(2)}, u32[]{:S(2)}) collective-permute-start(bf16[272,128]{1,0:T(8,128)(2,1)} %pack.1.refs_2_), channel_id=1, source_target_pairs={{0,24},{2,26},{4,28},{6,30},{8,16},{10,18},{12,20},{14,22},{16,8},... | collective-permute-start | bytes 208904 | tf_op jit(solution)/shard_map/ppermute | solution.py:46
  9.5 5.9 %collective-permute-start.8 = (bf16[272,128]{1,0:T(8,128)(2,1)}, bf16[272,128]{1,0:T(8,128)(2,1)S(1)}, u32[]{:S(2)}, u32[]{:S(2)}) collective-permute-start(bf16[272,128]{1,0:T(8,128)(2,1)} %pack.1.refs_2_), channel_id=1, source_target_pairs={{0,16},{2,18},{4,20},{6,22},{8,24},{10,26},{12,28},{14,30},{16,0},... | collective-permute-start | bytes 208904 | tf_op jit(solution)/shard_map/ppermute | solution.py:46
  9.5 7.4 %collective-permute-start.4 = (bf16[272,128]{1,0:T(8,128)(2,1)}, bf16[272,128]{1,0:T(8,128)(2,1)S(1)}, u32[]{:S(2)}, u32[]{:S(2)}) collective-permute-start(bf16[272,128]{1,0:T(8,128)(2,1)} %pack.1.refs_2_), channel_id=1, source_target_pairs={{0,8},{2,10},{4,12},{6,14},{8,0},{10,2},{12,4},{14,6},{16,24},{18,... | collective-permute-start | bytes 208904 | tf_op jit(solution)/shard_map/ppermute | solution.py:46
  10.3 6.6 %collective-permute-start.2 = (bf16[272,128]{1,0:T(8,128)(2,1)}, bf16[272,128]{1,0:T(8,128)(2,1)S(1)}, u32[]{:S(2)}, u32[]{:S(2)}) collective-permute-start(bf16[272,128]{1,0:T(8,128)(2,1)} %pack.1.refs_2_), channel_id=1, source_target_pairs={{0,4},{2,6},{4,0},{6,2},{8,12},{10,14},{12,8},{14,10},{16,20},{18,... | collective-permute-start | bytes 208904 | tf_op jit(solution)/shard_map/ppermute | solution.py:46
  13.0 4.4 %collective-permute-start.1 = (bf16[272,128]{1,0:T(8,128)(2,1)}, bf16[272,128]{1,0:T(8,128)(2,1)S(1)}, u32[]{:S(2)}, u32[]{:S(2)}) collective-permute-start(bf16[272,128]{1,0:T(8,128)(2,1)} %pack.1.refs_2_), channel_id=1, source_target_pairs={{0,2},{2,0},{4,6},{6,4},{8,10},{10,8},{12,14},{14,12},{16,18},{18,... | collective-permute-start | bytes 208904 | tf_op jit(solution)/shard_map/ppermute | solution.py:46
  15.4 4.3 %collective-permute-start.14 = (bf16[272,128]{1,0:T(8,128)(2,1)S(1)}, bf16[272,128]{1,0:T(8,128)(2,1)S(1)}, u32[]{:S(2)}, u32[]{:S(2)}) collective-permute-start(bf16[272,128]{1,0:T(8,128)(2,1)S(1)} %collective-permute-done.12.refs_14_), channel_id=1, source_target_pairs={{0,4},{2,6},{4,0},{6,2},{8,12},{10,14},{12,8},{14,10},{16,20},{18,... | collective-permute-start | bytes 208904 | tf_op jit(solution)/shard_map/ppermute | solution.py:46
  16.9 5.0 %collective-permute-start.13 = (bf16[272,128]{1,0:T(8,128)(2,1)S(1)}, bf16[272,128]{1,0:T(8,128)(2,1)S(1)}, u32[]{:S(2)}, u32[]{:S(2)}) collective-permute-start(bf16[272,128]{1,0:T(8,128)(2,1)S(1)} %collective-permute-done.12.refs_14_), channel_id=1, source_target_pairs={{0,2},{2,0},{4,6},{6,4},{8,10},{10,8},{12,14},{14,12},{16,18},{18,... | collective-permute-start | bytes 208904 | tf_op jit(solution)/shard_map/ppermute | solution.py:46
  16.9 5.1 %collective-permute-start.10 = (bf16[272,128]{1,0:T(8,128)(2,1)S(1)}, bf16[272,128]{1,0:T(8,128)(2,1)S(1)}, u32[]{:S(2)}, u32[]{:S(2)}) collective-permute-start(bf16[272,128]{1,0:T(8,128)(2,1)S(1)} %collective-permute-done.8.refs_10_), channel_id=1, source_target_pairs={{0,4},{2,6},{4,0},{6,2},{8,12},{10,14},{12,8},{14,10},{16,20},{18,... | collective-permute-start | bytes 208904 | tf_op jit(solution)/shard_map/ppermute | solution.py:46
  17.5 4.9 %collective-permute-start.9 = (bf16[272,128]{1,0:T(8,128)(2,1)S(1)}, bf16[272,128]{1,0:T(8,128)(2,1)S(1)}, u32[]{:S(2)}, u32[]{:S(2)}) collective-permute-start(bf16[272,128]{1,0:T(8,128)(2,1)S(1)} %collective-permute-done.8.refs_10_), channel_id=1, source_target_pairs={{0,2},{2,0},{4,6},{6,4},{8,10},{10,8},{12,14},{14,12},{16,18},{18,... | collective-permute-start | bytes 208904 | tf_op jit(solution)/shard_map/ppermute | solution.py:46
  19.7 4.5 %collective-permute-start.6 = (bf16[272,128]{1,0:T(8,128)(2,1)S(1)}, bf16[272,128]{1,0:T(8,128)(2,1)S(1)}, u32[]{:S(2)}, u32[]{:S(2)}) collective-permute-start(bf16[272,128]{1,0:T(8,128)(2,1)S(1)} %collective-permute-done.4.refs_6_), channel_id=1, source_target_pairs={{0,4},{2,6},{4,0},{6,2},{8,12},{10,14},{12,8},{14,10},{16,20},{18,... | collective-permute-start | bytes 208904 | tf_op jit(solution)/shard_map/ppermute | solution.py:46
  21.9 2.3 %collective-permute-start.5 = (bf16[272,128]{1,0:T(8,128)(2,1)S(1)}, bf16[272,128]{1,0:T(8,128)(2,1)S(1)}, u32[]{:S(2)}, u32[]{:S(2)}) collective-permute-start(bf16[272,128]{1,0:T(8,128)(2,1)S(1)} %collective-permute-done.4.refs_6_), channel_id=1, source_target_pairs={{0,2},{2,0},{4,6},{6,4},{8,10},{10,8},{12,14},{14,12},{16,18},{18,... | collective-permute-start | bytes 208904 | tf_op jit(solution)/shard_map/ppermute | solution.py:46
  21.9 2.7 %collective-permute-start.3 = (bf16[272,128]{1,0:T(8,128)(2,1)S(1)}, bf16[272,128]{1,0:T(8,128)(2,1)S(1)}, u32[]{:S(2)}, u32[]{:S(2)}) collective-permute-start(bf16[272,128]{1,0:T(8,128)(2,1)S(1)} %collective-permute-done.2.refs_4_), channel_id=1, source_target_pairs={{0,2},{2,0},{4,6},{6,4},{8,10},{10,8},{12,14},{14,12},{16,18},{18,... | collective-permute-start | bytes 208904 | tf_op jit(solution)/shard_map/ppermute | solution.py:46
  22.4 2.3 %collective-permute-start.15 = (bf16[272,128]{1,0:T(8,128)(2,1)S(1)}, bf16[272,128]{1,0:T(8,128)(2,1)S(1)}, u32[]{:S(2)}, u32[]{:S(2)}) collective-permute-start(bf16[272,128]{1,0:T(8,128)(2,1)S(1)} %collective-permute-done.14.refs_16_), channel_id=1, source_target_pairs={{0,2},{2,0},{4,6},{6,4},{8,10},{10,8},{12,14},{14,12},{16,18},{18,... | collective-permute-start | bytes 208904 | tf_op jit(solution)/shard_map/ppermute | solution.py:46
  24.2 1.3 %collective-permute-start.11 = (bf16[272,128]{1,0:T(8,128)(2,1)S(1)}, bf16[272,128]{1,0:T(8,128)(2,1)S(1)}, u32[]{:S(2)}, u32[]{:S(2)}) collective-permute-start(bf16[272,128]{1,0:T(8,128)(2,1)S(1)} %collective-permute-done.10.refs_12_), channel_id=1, source_target_pairs={{0,2},{2,0},{4,6},{6,4},{8,10},{10,8},{12,14},{14,12},{16,18},{18,... | collective-permute-start | bytes 208904 | tf_op jit(solution)/shard_map/ppermute | solution.py:46
  24.2 1.4 %collective-permute-start.7 = (bf16[272,128]{1,0:T(8,128)(2,1)S(1)}, bf16[272,128]{1,0:T(8,128)(2,1)S(1)}, u32[]{:S(2)}, u32[]{:S(2)}) collective-permute-start(bf16[272,128]{1,0:T(8,128)(2,1)S(1)} %collective-permute-done.6.refs_8_), channel_id=1, source_target_pairs={{0,2},{2,0},{4,6},{6,4},{8,10},{10,8},{12,14},{14,12},{16,18},{18,... | collective-permute-start | bytes 208904 | tf_op jit(solution)/shard_map/ppermute | solution.py:46
  25.6 1.0 %copy-start = (bf16[256,768]{1,0:T(8,128)(2,1)S(1)}, bf16[256,768]{1,0:T(8,128)(2,1)}, u32[]{:S(2)}) copy-start(bf16[256,768]{1,0:T(8,128)(2,1)} %refs_0_.1) | copy-start | bytes 1179652
  26.6 0.9 %copy-start.1 = (bf16[272,128]{1,0:T(8,128)(2,1)S(1)}, bf16[272,128]{1,0:T(8,128)(2,1)}, u32[]{:S(2)}) copy-start(bf16[272,128]{1,0:T(8,128)(2,1)} %pack.1.refs_2_) | copy-start | bytes 208900

commit v2 on v1

--- a/solution.py
+++ b/solution.py
@@ -20,9 +20,9 @@
     row = lax.broadcasted_iota(jnp.int32, (EXTRA, LANES), 0)
     lane = lax.broadcasted_iota(jnp.int32, (EXTRA, LANES), 1)
     digits = jnp.zeros((EXTRA, LANES), jnp.int32)
-    for brick in range(columns_ref.shape[0]):
+    for brick in range(columns_ref.shape[1]):
         for q in range(P_SLOTS):
-            value = columns_ref[brick, q]
+            value = columns_ref[q, brick]
             here = lane == brick * P_SLOTS + q
             digits = jnp.where(here & (row == 0), value % DIGIT, digits)
             digits = jnp.where(here & (row == 1), value // DIGIT, digits)
@@ -32,37 +32,48 @@
 def pack(prolong, prolong_columns):
     return pl.pallas_call(
         pack_kernel,
-        out_shape=jax.ShapeDtypeStruct((prolong.shape[0] + EXTRA, LANES), jnp.bfloat16),
+        out_shape=pltpu.VMEM((prolong.shape[0] + EXTRA, LANES), jnp.bfloat16),
         in_specs=[
             pl.BlockSpec(memory_space=pltpu.SMEM),
             pl.BlockSpec(memory_space=pltpu.VMEM),
         ],
         out_specs=pl.BlockSpec(memory_space=pltpu.VMEM),
         name="pack",
-    )(prolong_columns, prolong)
+    )(prolong_columns.T, prolong)
 
 
 def swap(block, axis, size, mask):
     return lax.ppermute(block, axis, [(i, i ^ mask) for i in range(size)])
 
 
-def gather_row(packed, size):
-    if size & (size - 1) or size < 8 or size > 32:
-        return [lax.all_gather(packed, "row", axis=0, tiled=True)], False
-    pieces = {0: packed}
-    for mask in (8, 12, 4, 16, 20, 24, 28):
-        if mask < size:
-            pieces[mask] = swap(packed, "row", size, mask)
-    for mask in sorted(pieces):
-        pieces[mask | 2] = swap(pieces[mask], "row", size, 2)
-    for mask in sorted(pieces):
-        pieces[mask | 1] = swap(pieces[mask], "row", size, 1)
-    return [pieces[mask] for mask in range(size)], True
+def gather_row(packed, size, fine_other):
+    if size != 16:
+        return [lax.all_gather(packed, "row", axis=0, tiled=True)], None, fine_other
+    got = {0: packed}
+    for mask, source, hop in (
+        (2, 0, 2),
+        (8, 0, 8),
+        (12, 0, 12),
+        (4, 0, 4),
+        (6, 2, 4),
+        (10, 8, 2),
+        (14, 12, 2),
+    ):
+        got[mask] = swap(got[source], "row", size, hop)
+    arrays, masks = list(got.values()), [[mask] for mask in got]
+    for group in ((0, 2, 4, 6), (8, 12), (10, 14)):
+        both = jnp.concatenate([got[mask] for mask in group])
+        if group[0] == 10:
+            both, fine_other = lax.optimization_barrier((both, fine_other))
+        arrays.append(swap(both, "row", size, 1))
+        masks.append([mask | 1 for mask in group])
+    return arrays, masks, fine_other
 
 
 def operator_kernel(
-    slabs, by_xor, columns_ref, counts_ref, pattern_ref, restrict_ref, *refs, cols, parts
+    slabs, masks, columns_ref, counts_ref, pattern_ref, restrict_ref, *refs, cols
 ):
+    parts = len(masks) if masks else 1
     fines = refs[:cols]
     pieces = refs[cols : cols + parts]
     out_ref, held_ref, seen_ref, reached_ref, slot_ref, sums_ref, sem = refs[cols + parts :]
@@ -74,8 +85,9 @@
     col_index = lax.axis_index("col")
 
     if parts > 1:
-        for at, piece in enumerate(pieces):
-            held_ref[at * rows : (at + 1) * rows, :] = piece[...]
+        for piece, inside in zip(pieces, masks):
+            for at, mask in enumerate(inside):
+                held_ref[mask * rows : (mask + 1) * rows, :] = piece[at * rows : (at + 1) * rows, :]
         source = held_ref
     else:
         source = pieces[0]
@@ -106,7 +118,7 @@
                     brick = columns_ref[i, k]
                     slab = lax.div(brick, bricks)
                     inner = brick - slab * bricks
-                    if by_xor:
+                    if masks:
                         slab = slab ^ row_index
                     start = pl.multiple_of(slab * rows + inner * BRICK, 16)
                     blocks.append(source[pl.ds(start, BRICK), :])
@@ -161,14 +173,15 @@
     owned = coarse_pattern.shape[1] // cols
     coarse = restrict_rows.shape[0] // BRICK * slabs
     packed = pack(prolong, prolong_columns)
-    pieces, by_xor = gather_row(packed, slabs)
-    fines = [fine_matrix] + [swap(fine_matrix, "col", cols, d) for d in range(1, cols)]
+    others = [swap(fine_matrix, "col", cols, d) for d in range(1, cols)]
+    pieces, masks, others = gather_row(packed, slabs, others)
+    fines = [pltpu.with_memory_space_constraint(fine_matrix, pltpu.VMEM)] + others
     rows = packed.shape[0]
     smem = pl.BlockSpec(memory_space=pltpu.SMEM)
     vmem = pl.BlockSpec(memory_space=pltpu.VMEM)
     held_rows = slabs * rows if len(pieces) > 1 else 16
     return pl.pallas_call(
-        functools.partial(operator_kernel, slabs, by_xor, cols=cols, parts=len(pieces)),
+        functools.partial(operator_kernel, slabs, masks, cols=cols),
         out_shape=jax.ShapeDtypeStruct((restrict_rows.shape[0], owned * BRICK), jnp.float32),
         in_specs=[smem] * 3 + [vmem] * (1 + cols + len(pieces)),
         out_specs=vmem,

time: 32.2 us -> 25.6 us (0.80)
  local copies, waits for them, and re-layouts: 3.21 us -> 0.03 us
  starting transfers between devices: 14.4 us -> 11.8 us
  Pallas kernels: 6.04 us -> 5.38 us
    unnamed x13 -> x10, local copies, waits for them, and re-layouts: 3.21 us -> 0.03 us
    ppermute x16 -> x11, starting transfers between devices: 14.4 us -> 11.8 us  [swap(): return lax.ppermute(block, axis, [(i, i ^ mask) for i in range(size)])]
    pallas_call x2, Pallas kernels: 6.04 us -> 5.38 us  [the longest x1 4.48 us: local(): pl.pallas_call(functools.partial(operator_kernel, slabs, masks, cols=cols...]
    ppermute x16 -> x11, waiting for transfers between devices: 8.3 us -> 7.99 us  [swap(): return lax.ppermute(block, axis, [(i, i ^ mask) for i in range(size)])]
  transfers between devices with their start and end apart: 16 -> 11, of which waited for: 7 -> 6; matrix products, arithmetic and copies ran while one was open for 4% -> 0% of each run, Pallas kernels for 5% -> 0%
where the time goes in v2:
time: 25.6 us; the launch traced here: 25.4 us
  starting transfers between devices  11.8 us (46%)
  waiting for transfers between devices  7.99 us (31%)
  Pallas kernels  5.38 us (21%)
    ppermute x11, starting transfers between devices, swap(): return lax.ppermute(block, axis, [(i, i ^ mask) for i in range(size)])  11.8 us
    ppermute x11, waiting for transfers between devices, swap(): return lax.ppermute(block, axis, [(i, i ^ mask) for i in range(size)])  7.99 us
    pallas_call x1, Pallas kernels, local(): pl.pallas_call(functools.partial(operator_kernel, slabs, masks, cols=cols...  4.48 us
    pallas_call x1, Pallas kernels, pack(): pl.pallas_call(pack_kernel, out_shape=pltpu.VMEM((prolong.shape[0] + EXTR...  0.9 us
  transfers between devices with their start and end apart: 11, of which 6 were waited for; matrix products, arithmetic and copies ran while one was open for 0% of the time, Pallas kernels for 0%

profile of v2, /device:TPU:0, one launch (start us, length us, event | category | flops | bytes accessed | tf_op | source)
XLA Modules:
  0.0 25.4 jit_solution(308716384669407707)
XLA Ops:
  0.0 0.9 %pack.1.refs_2_ = bf16[272,128]{1,0:T(8,128)(2,1)S(1)} custom-call(s32[2,4]{1,0:T(2,128)} %bitcast.1, bf16[256,128]{1,0:T(8,128)(2,1)} %prolong_ref.1), custom_call_target="tpu_custom_call" | custom-call | tf_op jit(solution)/shard_map/pack/pallas_call | solution.py:33
  0.9 3.0 %collective-permute-start.5 = (bf16[272,128]{1,0:T(8,128)(2,1)S(1)}, bf16[272,128]{1,0:T(8,128)(2,1)S(1)}, u32[]{:S(2)}, u32[]{:S(2)}) collective-permute-start(bf16[272,128]{1,0:T(8,128)(2,1)S(1)} %pack.1.refs_2_), channel_id=1, source_target_pairs={{0,4},{2,6},{4,0},{6,2},{8,12},{10,14},{12,8},{14,10},{16,20},{18,... | collective-permute-start | bytes 208904 | tf_op jit(solution)/shard_map/ppermute | solution.py:46
  3.9 3.6 %collective-permute-start.2 = (bf16[272,128]{1,0:T(8,128)(2,1)S(1)}, bf16[272,128]{1,0:T(8,128)(2,1)S(1)}, u32[]{:S(2)}, u32[]{:S(2)}) collective-permute-start(bf16[272,128]{1,0:T(8,128)(2,1)S(1)} %pack.1.refs_2_), channel_id=1, source_target_pairs={{0,24},{2,26},{4,28},{6,30},{8,16},{10,18},{12,20},{14,22},{16,8},... | collective-permute-start | bytes 208904 | tf_op jit(solution)/shard_map/ppermute | solution.py:46
  7.5 0.0 collective-permute-start
  7.5 0.8 %collective-permute-start.6 = (bf16[272,128]{1,0:T(8,128)(2,1)S(1)}, bf16[272,128]{1,0:T(8,128)(2,1)S(1)}, u32[]{:S(2)}, u32[]{:S(2)}) collective-permute-start(bf16[272,128]{1,0:T(8,128)(2,1)S(1)} %pack.1.refs_2_), channel_id=1, source_target_pairs={{0,8},{2,10},{4,12},{6,14},{8,0},{10,2},{12,4},{14,6},{16,24},{18,... | collective-permute-start | bytes 208904 | tf_op jit(solution)/shard_map/ppermute | solution.py:46
  8.3 0.0 collective-permute-done.5.refs_3_
  8.3 1.2 %collective-permute-start.7 = (bf16[272,128]{1,0:T(8,128)(2,1)S(1)}, bf16[272,128]{1,0:T(8,128)(2,1)S(1)}, u32[]{:S(2)}, u32[]{:S(2)}) collective-permute-start(bf16[272,128]{1,0:T(8,128)(2,1)S(1)} %collective-permute-done.5.refs_3_), channel_id=1, source_target_pairs={{0,8},{2,10},{4,12},{6,14},{8,0},{10,2},{12,4},{14,6},{16,24},{18,... | collective-permute-start | bytes 208904 | tf_op jit(solution)/shard_map/ppermute | solution.py:46
  9.6 1.5 %collective-permute-start.4 = (bf16[256,768]{1,0:T(8,128)(2,1)}, bf16[256,768]{1,0:T(8,128)(2,1)S(1)}, u32[]{:S(2)}, u32[]{:S(2)}) collective-permute-start(bf16[256,768]{1,0:T(8,128)(2,1)} %refs_0_.1), channel_id=1, source_target_pairs={{0,1},{1,0},{2,3},{3,2},{4,5},{5,4},{6,7},{7,6},{8,9},{9,8},{10,11... | collective-permute-start | bytes 1179656 | tf_op jit(solution)/shard_map/ppermute | solution.py:46
  11.1 0.0 collective-permute-done.2.refs_5_
  11.1 0.5 %collective-permute-start.3 = (bf16[272,128]{1,0:T(8,128)(2,1)S(1)}, bf16[272,128]{1,0:T(8,128)(2,1)S(1)}, u32[]{:S(2)}, u32[]{:S(2)}) collective-permute-start(bf16[272,128]{1,0:T(8,128)(2,1)S(1)} %collective-permute-done.2.refs_5_), channel_id=1, source_target_pairs={{0,4},{2,6},{4,0},{6,2},{8,12},{10,14},{12,8},{14,10},{16,20},{18,... | collective-permute-start | bytes 208904 | tf_op jit(solution)/shard_map/ppermute | solution.py:46
  11.6 1.6 %collective-permute-done.refs_4_ = bf16[272,128]{1,0:T(8,128)(2,1)S(1)} collective-permute-done((bf16[272,128]{1,0:T(8,128)(2,1)S(1)}, bf16[272,128]{1,0:T(8,128)(2,1)S(1)}, u32[]{:S(2)}, u32[]{:S(2)}) %collective-permute-start) | collective-permute-done | bytes 69664 | tf_op jit(solution)/shard_map/ppermute | solution.py:46
  13.2 0.6 %collective-permute-start.1 = (bf16[272,128]{1,0:T(8,128)(2,1)S(1)}, bf16[272,128]{1,0:T(8,128)(2,1)S(1)}, u32[]{:S(2)}, u32[]{:S(2)}) collective-permute-start(bf16[272,128]{1,0:T(8,128)(2,1)S(1)} %collective-permute-done.refs_4_), channel_id=1, source_target_pairs={{0,4},{2,6},{4,0},{6,2},{8,12},{10,14},{12,8},{14,10},{16,20},{18,... | collective-permute-start | bytes 208904 | tf_op jit(solution)/shard_map/ppermute | solution.py:46
  13.8 0.1 collective-permute-done.6.refs_6_
  13.9 0.7 %collective-permute-done.7.refs_7_ = bf16[272,128]{1,0:T(8,128)(2,1)S(1)} collective-permute-done((bf16[272,128]{1,0:T(8,128)(2,1)S(1)}, bf16[272,128]{1,0:T(8,128)(2,1)S(1)}, u32[]{:S(2)}, u32[]{:S(2)}) %collective-permute-start.7) | collective-permute-done | bytes 69664 | tf_op jit(solution)/shard_map/ppermute | solution.py:46
  14.7 0.0 copy-start
  14.7 0.1 collective-permute-start.8
  14.8 0.0 copy-start.1
  14.8 0.0 copy-start.2
  14.8 0.0 copy-start.3
  14.8 0.0 copy-start.4
  14.8 0.6 %collective-permute-start.9 = (bf16[544,128]{1,0:T(8,128)(2,1)S(1)}, bf16[544,128]{1,0:T(8,128)(2,1)S(1)}, u32[]{:S(2)}, u32[]{:S(2)}) collective-permute-start(bf16[544,128]{1,0:T(8,128)(2,1)S(1)} %pad_maximum_fusion.2), channel_id=1, source_target_pairs={{0,2},{2,0},{4,6},{6,4},{8,10},{10,8},{12,14},{14,12},{16,18},{18,... | collective-permute-start | bytes 417800 | tf_op jit(solution)/shard_map/ppermute | solution.py:46
  15.4 0.0 collective-permute-done.3.refs_9_
  15.4 2.2 %collective-permute-done.1.refs_8_ = bf16[272,128]{1,0:T(8,128)(2,1)S(1)} collective-permute-done((bf16[272,128]{1,0:T(8,128)(2,1)S(1)}, bf16[272,128]{1,0:T(8,128)(2,1)S(1)}, u32[]{:S(2)}, u32[]{:S(2)}) %collective-permute-start.1) | collective-permute-done | bytes 69664 | tf_op jit(solution)/shard_map/ppermute | solution.py:46
  17.5 2.0 %collective-permute-done.4.refs_1_ = bf16[256,768]{1,0:T(8,128)(2,1)S(1)} collective-permute-done((bf16[256,768]{1,0:T(8,128)(2,1)}, bf16[256,768]{1,0:T(8,128)(2,1)S(1)}, u32[]{:S(2)}, u32[]{:S(2)}) %collective-permute-start.4) | collective-permute-done | bytes 393248 | tf_op jit(solution)/shard_map/ppermute | solution.py:46
  19.5 0.0 collective-permute-start.10
  19.5 0.0 collective-permute-done.9.refs_11_
  19.5 0.0 collective-permute-done.8.refs_10_
  19.5 1.3 %collective-permute-done.10.refs_12_ = bf16[544,128]{1,0:T(8,128)(2,1)S(1)} collective-permute-done((bf16[544,128]{1,0:T(8,128)(2,1)S(1)}, bf16[544,128]{1,0:T(8,128)(2,1)S(1)}, u32[]{:S(2)}, u32[]{:S(2)}) %collective-permute-start.10) | collective-permute-done | bytes 139296 | tf_op jit(solution)/shard_map/ppermute | solution.py:46
  20.9 0.0 copy-done
  20.9 0.0 copy-done.1
  20.9 0.0 copy-done.2
  20.9 0.0 copy-done.3
  20.9 0.0 copy-done.4
  20.9 4.5 %operator.1 = f32[128,1536]{1,0:T(8,128)} custom-call(s32[4,24]{1,0:T(4,128)S(1)} %copy-done.2, s32[4]{0:T(128)S(1)} %copy-done.3, s32[1,48]{1,0:T(1,128)S(1)} %copy-done.4, bf16[128,256]{1,0:T(8,128)(2,1)S(1)} %copy-done.1, bf16[256,768]{1,0:T(8,128)(2,1)S(1)} %copy-done, bf16[256,768]{1,0:T(8,128)(2,1)S(1)} %collective-permute-done.4.refs_1_, ...), custom_call_target="tpu_custom_call" | custom-call | tf_op jit(solution)/shard_map/operator/pallas_call | solution.py:183
  (3 shorter events, 0.0 us)
Async XLA Ops:
  0.9 7.4 %collective-permute-start.5 = (bf16[272,128]{1,0:T(8,128)(2,1)S(1)}, bf16[272,128]{1,0:T(8,128)(2,1)S(1)}, u32[]{:S(2)}, u32[]{:S(2)}) collective-permute-start(bf16[272,128]{1,0:T(8,128)(2,1)S(1)} %pack.1.refs_2_), channel_id=1, source_target_pairs={{0,4},{2,6},{4,0},{6,2},{8,12},{10,14},{12,8},{14,10},{16,20},{18,... | collective-permute-start | bytes 208904 | tf_op jit(solution)/shard_map/ppermute | solution.py:46
  3.9 7.1 %collective-permute-start.2 = (bf16[272,128]{1,0:T(8,128)(2,1)S(1)}, bf16[272,128]{1,0:T(8,128)(2,1)S(1)}, u32[]{:S(2)}, u32[]{:S(2)}) collective-permute-start(bf16[272,128]{1,0:T(8,128)(2,1)S(1)} %pack.1.refs_2_), channel_id=1, source_target_pairs={{0,24},{2,26},{4,28},{6,30},{8,16},{10,18},{12,20},{14,22},{16,8},... | collective-permute-start | bytes 208904 | tf_op jit(solution)/shard_map/ppermute | solution.py:46
  7.5 5.7 %collective-permute-start = (bf16[272,128]{1,0:T(8,128)(2,1)S(1)}, bf16[272,128]{1,0:T(8,128)(2,1)S(1)}, u32[]{:S(2)}, u32[]{:S(2)}) collective-permute-start(bf16[272,128]{1,0:T(8,128)(2,1)S(1)} %pack.1.refs_2_), channel_id=1, source_target_pairs={{0,16},{2,18},{4,20},{6,22},{8,24},{10,26},{12,28},{14,30},{16,0},... | collective-permute-start | bytes 208904 | tf_op jit(solution)/shard_map/ppermute | solution.py:46
  7.5 6.3 %collective-permute-start.6 = (bf16[272,128]{1,0:T(8,128)(2,1)S(1)}, bf16[272,128]{1,0:T(8,128)(2,1)S(1)}, u32[]{:S(2)}, u32[]{:S(2)}) collective-permute-start(bf16[272,128]{1,0:T(8,128)(2,1)S(1)} %pack.1.refs_2_), channel_id=1, source_target_pairs={{0,8},{2,10},{4,12},{6,14},{8,0},{10,2},{12,4},{14,6},{16,24},{18,... | collective-permute-start | bytes 208904 | tf_op jit(solution)/shard_map/ppermute | solution.py:46
  8.3 6.3 %collective-permute-start.7 = (bf16[272,128]{1,0:T(8,128)(2,1)S(1)}, bf16[272,128]{1,0:T(8,128)(2,1)S(1)}, u32[]{:S(2)}, u32[]{:S(2)}) collective-permute-start(bf16[272,128]{1,0:T(8,128)(2,1)S(1)} %collective-permute-done.5.refs_3_), channel_id=1, source_target_pairs={{0,8},{2,10},{4,12},{6,14},{8,0},{10,2},{12,4},{14,6},{16,24},{18,... | collective-permute-start | bytes 208904 | tf_op jit(solution)/shard_map/ppermute | solution.py:46
  9.6 9.9 %collective-permute-start.4 = (bf16[256,768]{1,0:T(8,128)(2,1)}, bf16[256,768]{1,0:T(8,128)(2,1)S(1)}, u32[]{:S(2)}, u32[]{:S(2)}) collective-permute-start(bf16[256,768]{1,0:T(8,128)(2,1)} %refs_0_.1), channel_id=1, source_target_pairs={{0,1},{1,0},{2,3},{3,2},{4,5},{5,4},{6,7},{7,6},{8,9},{9,8},{10,11... | collective-permute-start | bytes 1179656 | tf_op jit(solution)/shard_map/ppermute | solution.py:46
  11.1 4.3 %collective-permute-start.3 = (bf16[272,128]{1,0:T(8,128)(2,1)S(1)}, bf16[272,128]{1,0:T(8,128)(2,1)S(1)}, u32[]{:S(2)}, u32[]{:S(2)}) collective-permute-start(bf16[272,128]{1,0:T(8,128)(2,1)S(1)} %collective-permute-done.2.refs_5_), channel_id=1, source_target_pairs={{0,4},{2,6},{4,0},{6,2},{8,12},{10,14},{12,8},{14,10},{16,20},{18,... | collective-permute-start | bytes 208904 | tf_op jit(solution)/shard_map/ppermute | solution.py:46
  13.2 4.3 %collective-permute-start.1 = (bf16[272,128]{1,0:T(8,128)(2,1)S(1)}, bf16[272,128]{1,0:T(8,128)(2,1)S(1)}, u32[]{:S(2)}, u32[]{:S(2)}) collective-permute-start(bf16[272,128]{1,0:T(8,128)(2,1)S(1)} %collective-permute-done.refs_4_), channel_id=1, source_target_pairs={{0,4},{2,6},{4,0},{6,2},{8,12},{10,14},{12,8},{14,10},{16,20},{18,... | collective-permute-start | bytes 208904 | tf_op jit(solution)/shard_map/ppermute | solution.py:46
  14.7 6.2 %copy-start = (bf16[256,768]{1,0:T(8,128)(2,1)S(1)}, bf16[256,768]{1,0:T(8,128)(2,1)}, u32[]{:S(2)}) copy-start(bf16[256,768]{1,0:T(8,128)(2,1)} %refs_0_.1) | copy-start | bytes 1179652
  14.7 4.9 %collective-permute-start.8 = (bf16[1088,128]{1,0:T(8,128)(2,1)S(1)}, bf16[1088,128]{1,0:T(8,128)(2,1)S(1)}, u32[]{:S(2)}, u32[]{:S(2)}) collective-permute-start(bf16[1088,128]{1,0:T(8,128)(2,1)S(1)} %pad_maximum_fusion), channel_id=1, source_target_pairs={{0,2},{2,0},{4,6},{6,4},{8,10},{10,8},{12,14},{14,12},{16,18},{18,... | collective-permute-start | bytes 835592 | tf_op jit(solution)/shard_map/ppermute | solution.py:46
  14.8 6.1 %copy-start.1 = (bf16[128,256]{1,0:T(8,128)(2,1)S(1)}, bf16[128,256]{1,0:T(8,128)(2,1)}, u32[]{:S(2)}) copy-start(bf16[128,256]{1,0:T(8,128)(2,1)} %restrict_ref.1) | copy-start | bytes 196612
  14.8 6.1 %copy-start.2 = (s32[4,24]{1,0:T(4,128)S(1)}, s32[4,24]{1,0:T(4,128)}, u32[]{:S(2)}) copy-start(s32[4,24]{1,0:T(4,128)} %columns_ref.1) | copy-start | bytes 1156
  14.8 6.1 %copy-start.3 = (s32[4]{0:T(128)S(1)}, s32[4]{0:T(128)}, u32[]{:S(2)}) copy-start(s32[4]{0:T(128)} %counts_ref.1) | copy-start | bytes 52
  14.8 6.1 %copy-start.4 = (s32[1,48]{1,0:T(1,128)S(1)}, s32[1,48]{1,0:T(1,128)}, u32[]{:S(2)}) copy-start(s32[1,48]{1,0:T(1,128)} %pattern_ref.1) | copy-start | bytes 580
  14.8 4.7 %collective-permute-start.9 = (bf16[544,128]{1,0:T(8,128)(2,1)S(1)}, bf16[544,128]{1,0:T(8,128)(2,1)S(1)}, u32[]{:S(2)}, u32[]{:S(2)}) collective-permute-start(bf16[544,128]{1,0:T(8,128)(2,1)S(1)} %pad_maximum_fusion.2), channel_id=1, source_target_pairs={{0,2},{2,0},{4,6},{6,4},{8,10},{10,8},{12,14},{14,12},{16,18},{18,... | collective-permute-start | bytes 417800 | tf_op jit(solution)/shard_map/ppermute | solution.py:46
  19.5 1.4 %collective-permute-start.10 = (bf16[544,128]{1,0:T(8,128)(2,1)S(1)}, bf16[544,128]{1,0:T(8,128)(2,1)S(1)}, u32[]{:S(2)}, u32[]{:S(2)}) collective-permute-start(bf16[544,128]{1,0:T(8,128)(2,1)S(1)} %pad_maximum_fusion.1), channel_id=1, source_target_pairs={{0,2},{2,0},{4,6},{6,4},{8,10},{10,8},{12,14},{14,12},{16,18},{18,... | collective-permute-start | bytes 417800 | tf_op jit(solution)/shard_map/ppermute | solution.py:46

commit v3 on v2

v3 whole, which is shorter than its diff:
```python
import functools

import jax
import jax.numpy as jnp
from jax import lax
from jax.experimental import pallas as pl
from jax.experimental.pallas import tpu as pltpu
from jax.sharding import PartitionSpec as P

BRICK = 64
P_SLOTS = 2
DIGIT = 128
LANES = 128
EXTRA = 16


def pack_kernel(columns_ref, prolong_ref, packed_ref):
    rows = prolong_ref.shape[0]
    packed_ref[:rows, :] = prolong_ref[...]
    row = lax.broadcasted_iota(jnp.int32, (EXTRA, LANES), 0)
    lane = lax.broadcasted_iota(jnp.int32, (EXTRA, LANES), 1)
    digits = jnp.zeros((EXTRA, LANES), jnp.int32)
    for brick in range(columns_ref.shape[1]):
        for q in range(P_SLOTS):
            value = columns_ref[q, brick] + 1
            here = lane == brick
            digits = jnp.where(here & (row == 2 * q), lax.rem(value, DIGIT), digits)
            digits = jnp.where(here & (row == 2 * q + 1), lax.div(value, DIGIT), digits)
    packed_ref[rows:, :] = digits.astype(jnp.float32).astype(jnp.bfloat16)


def pack(prolong, prolong_columns):
    return pl.pallas_call(
        pack_kernel,
        out_shape=pltpu.VMEM((prolong.shape[0] + EXTRA, LANES), jnp.bfloat16),
        in_specs=[
            pl.BlockSpec(memory_space=pltpu.SMEM),
            pl.BlockSpec(memory_space=pltpu.VMEM),
        ],
        out_specs=pl.BlockSpec(memory_space=pltpu.VMEM),
        name="pack",
    )(prolong_columns.T, prolong)


def swap(block, axis, size, mask):
    return lax.ppermute(block, axis, [(i, i ^ mask) for i in range(size)])


def gather_row(packed, size, fine_other):
    if size != 16:
        return [lax.all_gather(packed, "row", axis=0, tiled=True)], None, fine_other
    got = {(0,): packed}
    for mask in (4, 8, 12):
        got[(mask,)] = swap(packed, "row", size, mask)
    across = {}
    for group in ((0, 4), (8,), (12,)):
        both = jnp.concatenate([got[(mask,)] for mask in group])
        across[tuple(mask | 2 for mask in group)] = swap(both, "row", size, 2)
    pieces = {**got, **across}
    for half in (got, across):
        both = jnp.concatenate(list(half.values()))
        if half is across:
            both, fine_other = lax.optimization_barrier((both, fine_other))
        group = tuple(mask | 1 for inside in half for mask in inside)
        pieces[group] = swap(both, "row", size, 1)
    return list(pieces.values()), list(pieces), fine_other


def index_kernel(by_xor, slabs, cols, columns_ref, counts_ref, pattern_ref, start_ref, pick_ref, own_ref):
    bricks, slots = columns_ref.shape
    share = slots // cols
    owned = pattern_ref.shape[1] // cols
    rows = bricks * BRICK + EXTRA
    row_index = lax.axis_index("row")
    col_index = lax.axis_index("col")
    lane = lax.broadcasted_iota(jnp.int32, (8, LANES), 1)
    slab_of = jnp.zeros((8, LANES), jnp.int32)
    inner_of = jnp.zeros((8, LANES), jnp.int32)
    live_of = jnp.zeros((8, LANES), jnp.int32)
    for i in range(bricks):
        for part in range(cols):
            first = (col_index ^ part) * share if cols > 1 else 0
            for pos in range(share):
                brick = columns_ref[i, first + pos]
                slab = lax.div(brick, bricks)
                inner = brick - slab * bricks
                if by_xor:
                    slab = slab ^ row_index
                here = lane == i * slots + part * share + pos
                slab_of = jnp.where(here, slab, slab_of)
                inner_of = jnp.where(here, inner, inner_of)
                live_of = jnp.where(here, (first + pos < counts_ref[i]).astype(jnp.int32), live_of)
    start_ref[...] = slab_of * rows + inner_of * BRICK
    place = jnp.where(live_of == 1, slab_of * bricks + inner_of, -1)[0:1, :]
    row = lax.broadcasted_iota(jnp.int32, pick_ref.shape, 0)
    pick_ref[...] = (row == place).astype(jnp.float32).astype(jnp.bfloat16)
    own = jnp.full(own_ref.shape, -1, jnp.int32)
    row = lax.broadcasted_iota(jnp.int32, own_ref.shape, 0)
    for s in range(owned):
        wanted = pattern_ref[0, col_index * owned + s]
        own = jnp.where(row == s, jnp.where(wanted < 0, -1, wanted + 1), own)
    own_ref[...] = own.astype(jnp.float32)


def make_index(by_xor, slabs, cols, fine_columns, fine_counts, coarse_pattern):
    bricks = fine_counts.shape[0]
    owned = coarse_pattern.shape[1] // cols
    up = lambda n, to: -(-n // to) * to
    return pl.pallas_call(
        functools.partial(index_kernel, by_xor, slabs, cols),
        out_shape=(
            pltpu.VMEM((8, LANES), jnp.int32),
            pltpu.VMEM((up(slabs * bricks, LANES), LANES), jnp.bfloat16),
            pltpu.VMEM((up(owned, 8), LANES), jnp.float32),
        ),
        in_specs=[pl.BlockSpec(memory_space=pltpu.SMEM)] * 3,
        out_specs=(pl.BlockSpec(memory_space=pltpu.VMEM),) * 3,
        name="index",
    )(fine_columns, fine_counts, coarse_pattern)


def operator_kernel(slabs, masks, bricks, slots, owned, start_ref, pick_ref, own_ref, restrict_ref, *refs, cols):
    parts = len(masks) if masks else 1
    fines, refs = refs[:cols], refs[cols:]
    pieces, refs = refs[:parts], refs[parts:]
    out_ref, held_ref, slot_ref, begin_ref, goal_ref, result_ref = refs[:6]
    sums, (begin_sem, goal_sem, out_sem) = refs[6 : 6 + bricks], refs[6 + bricks :]
    share = slots // cols
    rows = bricks * BRICK + EXTRA

    to_begin = pltpu.make_async_copy(start_ref, begin_ref, begin_sem)
    to_begin.start()
    table = [jnp.zeros((EXTRA, LANES), jnp.float32) for _ in range(pick_ref.shape[0] // LANES)]
    for piece, inside in zip(pieces, masks if masks else [range(slabs)]):
        for at, slab in enumerate(inside):
            first = at * rows + bricks * BRICK
            digits = piece[first : first + EXTRA, :].astype(jnp.float32)
            tile, shift = slab * bricks // LANES, slab * bricks % LANES
            table[tile] += pltpu.roll(digits, shift, 1) if shift else digits
    reached = jnp.dot(
        jnp.concatenate(table, axis=1).astype(jnp.bfloat16),
        pick_ref[...],
        preferred_element_type=jnp.float32,
    )
    own = own_ref[...]
    offset = lax.broadcasted_iota(jnp.int32, own.shape, 0).astype(jnp.float32) - owned
    for q in range(P_SLOTS):
        coarse = reached[2 * q : 2 * q + 1, :] + DIGIT * reached[2 * q + 1 : 2 * q + 2, :]
        slot = owned + jnp.sum(jnp.where(own == coarse, offset, 0.0), axis=0, keepdims=True)
        slot_ref[q : q + 1, :] = slot.astype(jnp.int32)
    to_goal = pltpu.make_async_copy(slot_ref, goal_ref, goal_sem)
    to_goal.start()

    source = pieces[0]
    if masks:
        source = held_ref
        for piece, inside in zip(pieces, masks):
            for at, slab in enumerate(inside):
                held_ref[slab * rows : (slab + 1) * rows, :] = piece[at * rows : (at + 1) * rows, :]
    for total in sums:
        total[...] = jnp.zeros_like(total)
    left = lax.broadcasted_iota(jnp.int32, (BRICK, LANES), 1) < BRICK
    nothing = jnp.zeros((BRICK, LANES), jnp.bfloat16)

    to_begin.wait()
    to_goal.wait()

    for part in range(cols):
        for pair in range(share // 2):
            for i in range(bricks):
                blocks, where_to = [], []
                for half in range(2):
                    at = i * slots + part * share + pair * 2 + half
                    start = pl.multiple_of(begin_ref[0, at], 16)
                    blocks.append(source[pl.ds(start, BRICK), :])
                    where_to += [goal_ref[q, at] for q in range(P_SLOTS)]
                right = jnp.concatenate(
                    [
                        jnp.concatenate([blocks[0], nothing], axis=1),
                        jnp.concatenate([nothing, blocks[1]], axis=1),
                    ],
                    axis=0,
                )
                a = fines[part][i * BRICK : (i + 1) * BRICK, pair * LANES : (pair + 1) * LANES]
                product = jnp.dot(a, right, preferred_element_type=jnp.float32)
                for half in range(2):
                    block = product[:, half * LANES : (half + 1) * LANES]
                    sums[i][where_to[half * 2]] += jnp.where(left, block, 0.0)
                    sums[i][where_to[half * 2 + 1]] += jnp.where(left, 0.0, block)

    restrict = restrict_ref[...]
    group = 4 if owned % 4 == 0 else 2
    width = group * BRICK
    leaving = []
    for at in range(owned // group):
        high, low = [], []
        for i in range(bricks):
            tops, rests = [], []
            for even in range(at * group, (at + 1) * group, 2):
                first, second = sums[i][even], sums[i][even + 1]
                total = jnp.where(left, first, second) + pltpu.roll(
                    jnp.where(left, second, first), BRICK, 1
                )
                tops.append(total.astype(jnp.bfloat16))
                rests.append((total - tops[-1].astype(jnp.float32)).astype(jnp.bfloat16))
            high.append(jnp.concatenate(tops, axis=1))
            low.append(jnp.concatenate(rests, axis=1))
        high = jnp.concatenate(high, axis=0)
        low = jnp.concatenate(low, axis=0)
        here = pl.ds(at * width, width)
        result_ref[:, here] = jnp.dot(restrict, high, preferred_element_type=jnp.float32) + jnp.dot(
            restrict, low, preferred_element_type=jnp.float32
        )
        move = pltpu.make_async_copy(result_ref.at[:, here], out_ref.at[:, here], out_sem.at[at])
        move.start()
        leaving.append(move)
    for move in leaving:
        move.wait()


def operate(slabs, cols, bricks, slots, owned, index, restrict_rows, fines, pieces, masks):
    rows = bricks * BRICK + EXTRA
    vmem = pl.BlockSpec(memory_space=pltpu.VMEM)
    held_rows = slabs * rows if masks else 16
    shape = (restrict_rows.shape[0], owned * BRICK)
    return pl.pallas_call(
        functools.partial(operator_kernel, slabs, masks, bricks, slots, owned, cols=cols),
        out_shape=jax.ShapeDtypeStruct(shape, jnp.float32),
        in_specs=[vmem] * (4 + cols + len(pieces)),
        out_specs=pl.BlockSpec(memory_space=pl.ANY),
        scratch_shapes=[
            pltpu.VMEM((held_rows, LANES), jnp.bfloat16),
            pltpu.VMEM((8, LANES), jnp.int32),
            pltpu.SMEM((8, LANES), jnp.int32),
            pltpu.SMEM((8, LANES), jnp.int32),
            pltpu.VMEM(shape, jnp.float32),
        ]
        + [pltpu.VMEM((owned + 1, BRICK, LANES), jnp.float32)] * bricks
        + [
            pltpu.SemaphoreType.DMA,
            pltpu.SemaphoreType.DMA,
            pltpu.SemaphoreType.DMA((owned // 2,)),
        ],
        compiler_params=pltpu.CompilerParams(vmem_limit_bytes=32 * 1024 * 1024),
        name="operator",
    )(*index, restrict_rows, *fines, *pieces)


def local(
    slabs,
    cols,
    fine_matrix,
    fine_columns,
    fine_counts,
    prolong,
    prolong_columns,
    restrict_rows,
    coarse_pattern,
):
    bricks, slots = fine_columns.shape
    owned = coarse_pattern.shape[1] // cols
    packed = pack(prolong, prolong_columns)
    others = [swap(fine_matrix, "col", cols, d) for d in range(1, cols)]
    pieces, masks, others = gather_row(packed, slabs, others)
    fines = [pltpu.with_memory_space_constraint(fine_matrix, pltpu.VMEM)] + others
    if masks:
        fine_columns, pieces[1] = lax.optimization_barrier((fine_columns, pieces[1]))
    index = make_index(masks is not None, slabs, cols, fine_columns, fine_counts, coarse_pattern)
    return operate(slabs, cols, bricks, slots, owned, index, restrict_rows, fines, pieces, masks)


def solution(mesh):
    return jax.shard_map(
        functools.partial(local, mesh.shape["row"], mesh.shape["col"]),
        mesh=mesh,
        in_specs=(
            P("row", "col"),
            P("row", None),
            P("row"),
            P("row", None),
            P("row", None),
            P("row", None),
            P("row", None),
        ),
        out_specs=P("row", "col"),
        check_vma=False,
    )
```

time: 25.6 us -> 22.9 us (0.89)
  waiting for transfers between devices: 7.99 us -> 4.89 us
  Pallas kernels: 5.38 us -> 5.78 us
    ppermute x11 -> x9, waiting for transfers between devices: 7.99 us -> 4.89 us  [swap(): return lax.ppermute(block, axis, [(i, i ^ mask) for i in range(size)])]
    pallas_call x1 -> x2, Pallas kernels: 4.48 us -> 4.9 us  [the longest x1 3.57 us: operate(): pl.pallas_call(functools.partial(operator_kernel, slabs, masks, bricks, s...]
    ppermute x11 -> x9, starting transfers between devices: 11.8 us -> 11.9 us  [swap(): return lax.ppermute(block, axis, [(i, i ^ mask) for i in range(size)])]
  transfers between devices with their start and end apart: 11 -> 9, of which waited for: 6 -> 5; matrix products, arithmetic and copies ran while one was open for 0% -> 0% of each run, Pallas kernels for 0% -> 6%
where the time goes in v3:
time: 22.9 us; the launch traced here: 22.8 us
  starting transfers between devices  11.9 us (52%)
  Pallas kernels  5.78 us (25%)
  waiting for transfers between devices  4.89 us (21%)
    ppermute x9, starting transfers between devices, swap(): return lax.ppermute(block, axis, [(i, i ^ mask) for i in range(size)])  11.9 us
    ppermute x9, waiting for transfers between devices, swap(): return lax.ppermute(block, axis, [(i, i ^ mask) for i in range(size)])  4.89 us
    pallas_call x1, Pallas kernels, operate(): pl.pallas_call(functools.partial(operator_kernel, slabs, masks, bricks, s...  3.57 us
    pallas_call x1, Pallas kernels, make_index(): pl.pallas_call(functools.partial(index_kernel, by_xor, slabs, cols), out_...  1.33 us
    pallas_call x1, Pallas kernels, pack(): pl.pallas_call(pack_kernel, out_shape=pltpu.VMEM((prolong.shape[0] + EXTR...  0.88 us
  transfers between devices with their start and end apart: 9, of which 5 were waited for; matrix products, arithmetic and copies ran while one was open for 0% of the time, Pallas kernels for 6%

profile of v3, /device:TPU:0, one launch (start us, length us, event | category | flops | bytes accessed | tf_op | source)
XLA Modules:
  0.0 22.8 jit_solution(3268320152172667213)
XLA Ops:
  0.0 0.9 %pack.1.refs_2_ = bf16[272,128]{1,0:T(8,128)(2,1)S(1)} custom-call(s32[2,4]{1,0:T(2,128)} %bitcast.1, bf16[256,128]{1,0:T(8,128)(2,1)} %prolong_ref.1), custom_call_target="tpu_custom_call" | custom-call | tf_op jit(solution)/shard_map/pack/pallas_call | solution.py:33
  0.9 3.1 %collective-permute-start = (bf16[272,128]{1,0:T(8,128)(2,1)S(1)}, bf16[272,128]{1,0:T(8,128)(2,1)S(1)}, u32[]{:S(2)}, u32[]{:S(2)}) collective-permute-start(bf16[272,128]{1,0:T(8,128)(2,1)S(1)} %pack.1.refs_2_), channel_id=1, source_target_pairs={{0,8},{2,10},{4,12},{6,14},{8,0},{10,2},{12,4},{14,6},{16,24},{18,... | collective-permute-start | bytes 208904 | tf_op jit(solution)/shard_map/ppermute | solution.py:46
  4.0 2.5 %collective-permute-start.4 = (bf16[272,128]{1,0:T(8,128)(2,1)S(1)}, bf16[272,128]{1,0:T(8,128)(2,1)S(1)}, u32[]{:S(2)}, u32[]{:S(2)}) collective-permute-start(bf16[272,128]{1,0:T(8,128)(2,1)S(1)} %pack.1.refs_2_), channel_id=1, source_target_pairs={{0,24},{2,26},{4,28},{6,30},{8,16},{10,18},{12,20},{14,22},{16,8},... | collective-permute-start | bytes 208904 | tf_op jit(solution)/shard_map/ppermute | solution.py:46
  6.5 0.1 collective-permute-start.2
  6.6 1.5 %collective-permute-start.6 = (bf16[256,768]{1,0:T(8,128)(2,1)}, bf16[256,768]{1,0:T(8,128)(2,1)S(1)}, u32[]{:S(2)}, u32[]{:S(2)}) collective-permute-start(bf16[256,768]{1,0:T(8,128)(2,1)} %refs_0_.1), channel_id=1, source_target_pairs={{0,1},{1,0},{2,3},{3,2},{4,5},{5,4},{6,7},{7,6},{8,9},{9,8},{10,11... | collective-permute-start | bytes 1179656 | tf_op jit(solution)/shard_map/ppermute | solution.py:46
  8.1 0.0 collective-permute-done.refs_3_
  8.1 1.6 %collective-permute-start.1 = (bf16[544,128]{1,0:T(8,128)(2,1)S(1)}, bf16[544,128]{1,0:T(8,128)(2,1)S(1)}, u32[]{:S(2)}, u32[]{:S(2)}) collective-permute-start(bf16[544,128]{1,0:T(8,128)(2,1)S(1)} %pad_maximum_fusion.2), channel_id=1, source_target_pairs={{0,4},{2,6},{4,0},{6,2},{8,12},{10,14},{12,8},{14,10},{16,20},{18,... | collective-permute-start | bytes 417800 | tf_op jit(solution)/shard_map/ppermute | solution.py:46
  9.7 1.3 %collective-permute-done.4.refs_5_ = bf16[272,128]{1,0:T(8,128)(2,1)S(1)} collective-permute-done((bf16[272,128]{1,0:T(8,128)(2,1)S(1)}, bf16[272,128]{1,0:T(8,128)(2,1)S(1)}, u32[]{:S(2)}, u32[]{:S(2)}) %collective-permute-start.4) | collective-permute-done | bytes 69664 | tf_op jit(solution)/shard_map/ppermute | solution.py:46
  11.0 1.5 %collective-permute-start.5 = (bf16[272,128]{1,0:T(8,128)(2,1)S(1)}, bf16[272,128]{1,0:T(8,128)(2,1)S(1)}, u32[]{:S(2)}, u32[]{:S(2)}) collective-permute-start(bf16[272,128]{1,0:T(8,128)(2,1)S(1)} %collective-permute-done.4.refs_5_), channel_id=1, source_target_pairs={{0,4},{2,6},{4,0},{6,2},{8,12},{10,14},{12,8},{14,10},{16,20},{18,... | collective-permute-start | bytes 208904 | tf_op jit(solution)/shard_map/ppermute | solution.py:46
  12.5 0.7 %collective-permute-done.2.refs_4_ = bf16[272,128]{1,0:T(8,128)(2,1)S(1)} collective-permute-done((bf16[272,128]{1,0:T(8,128)(2,1)S(1)}, bf16[272,128]{1,0:T(8,128)(2,1)S(1)}, u32[]{:S(2)}, u32[]{:S(2)}) %collective-permute-start.2) | collective-permute-done | bytes 69664 | tf_op jit(solution)/shard_map/ppermute | solution.py:46
  13.2 1.5 %collective-permute-start.3 = (bf16[272,128]{1,0:T(8,128)(2,1)S(1)}, bf16[272,128]{1,0:T(8,128)(2,1)S(1)}, u32[]{:S(2)}, u32[]{:S(2)}) collective-permute-start(bf16[272,128]{1,0:T(8,128)(2,1)S(1)} %collective-permute-done.2.refs_4_), channel_id=1, source_target_pairs={{0,4},{2,6},{4,0},{6,2},{8,12},{10,14},{12,8},{14,10},{16,20},{18,... | collective-permute-start | bytes 208904 | tf_op jit(solution)/shard_map/ppermute | solution.py:46
  14.7 0.0 copy-start
  14.8 0.0 copy-start.1
  14.8 0.1 collective-permute-start.7
  14.8 0.5 %collective-permute-done.5.refs_8_ = bf16[272,128]{1,0:T(8,128)(2,1)S(1)} collective-permute-done((bf16[272,128]{1,0:T(8,128)(2,1)S(1)}, bf16[272,128]{1,0:T(8,128)(2,1)S(1)}, u32[]{:S(2)}, u32[]{:S(2)}) %collective-permute-start.5) | collective-permute-done | bytes 69664 | tf_op jit(solution)/shard_map/ppermute | solution.py:46
  15.3 2.2 %collective-permute-done.3.refs_7_ = bf16[272,128]{1,0:T(8,128)(2,1)S(1)} collective-permute-done((bf16[272,128]{1,0:T(8,128)(2,1)S(1)}, bf16[272,128]{1,0:T(8,128)(2,1)S(1)}, u32[]{:S(2)}, u32[]{:S(2)}) %collective-permute-start.3) | collective-permute-done | bytes 69664 | tf_op jit(solution)/shard_map/ppermute | solution.py:46
  17.5 0.0 collective-permute-done.1.refs_6_
  17.5 0.0 collective-permute-done.6.refs_1_
  17.6 0.1 collective-permute-start.8
  17.6 1.3 %index.1 = (s32[8,128]{1,0:T(8,128)S(1)}, bf16[128,128]{1,0:T(8,128)(2,1)S(1)}, f32[24,128]{1,0:T(8,128)S(1)}) custom-call(s32[4,24]{1,0:T(4,128)} %columns_ref, s32[4]{0:T(128)} %counts_ref.1, s32[1,48]{1,0:T(1,128)} %pattern_ref.1), custom_call_target="tpu_custom_call" | custom-call | tf_op jit(solution)/shard_map/index/pallas_call | solution.py:109
  19.0 0.0 collective-permute-done.7.refs_9_
  19.0 0.2 collective-permute-done.8.refs_10_
  19.2 0.0 copy-done
  19.2 0.0 copy-done.1
  19.2 3.6 %operator.1 = f32[128,1536]{1,0:T(8,128)} custom-call(s32[8,128]{1,0:T(8,128)S(1)} %get-tuple-element.13.start_ref, bf16[128,128]{1,0:T(8,128)(2,1)S(1)} %get-tuple-element.14.pick_ref, f32[24,128]{1,0:T(8,128)S(1)} %get-tuple-element.15.own_ref, bf16[128,256]{1,0:T(8,128)(2,1)S(1)} %copy-done.1, bf16[256,768]{1,0:T(8,128)(2,1)S(1)} %copy-done, ...), custom_call_target="tpu_custom_call" | custom-call | tf_op jit(solution)/shard_map/operator/pallas_call | solution.py:226
  (3 shorter events, 0.0 us)
Async XLA Ops:
  0.9 7.2 %collective-permute-start = (bf16[272,128]{1,0:T(8,128)(2,1)S(1)}, bf16[272,128]{1,0:T(8,128)(2,1)S(1)}, u32[]{:S(2)}, u32[]{:S(2)}) collective-permute-start(bf16[272,128]{1,0:T(8,128)(2,1)S(1)} %pack.1.refs_2_), channel_id=1, source_target_pairs={{0,8},{2,10},{4,12},{6,14},{8,0},{10,2},{12,4},{14,6},{16,24},{18,... | collective-permute-start | bytes 208904 | tf_op jit(solution)/shard_map/ppermute | solution.py:46
  4.0 7.0 %collective-permute-start.4 = (bf16[272,128]{1,0:T(8,128)(2,1)S(1)}, bf16[272,128]{1,0:T(8,128)(2,1)S(1)}, u32[]{:S(2)}, u32[]{:S(2)}) collective-permute-start(bf16[272,128]{1,0:T(8,128)(2,1)S(1)} %pack.1.refs_2_), channel_id=1, source_target_pairs={{0,24},{2,26},{4,28},{6,30},{8,16},{10,18},{12,20},{14,22},{16,8},... | collective-permute-start | bytes 208904 | tf_op jit(solution)/shard_map/ppermute | solution.py:46
  6.5 6.8 %collective-permute-start.2 = (bf16[272,128]{1,0:T(8,128)(2,1)S(1)}, bf16[272,128]{1,0:T(8,128)(2,1)S(1)}, u32[]{:S(2)}, u32[]{:S(2)}) collective-permute-start(bf16[272,128]{1,0:T(8,128)(2,1)S(1)} %pack.1.refs_2_), channel_id=1, source_target_pairs={{0,16},{2,18},{4,20},{6,22},{8,24},{10,26},{12,28},{14,30},{16,0},... | collective-permute-start | bytes 208904 | tf_op jit(solution)/shard_map/ppermute | solution.py:46
  6.6 11.0 %collective-permute-start.6 = (bf16[256,768]{1,0:T(8,128)(2,1)}, bf16[256,768]{1,0:T(8,128)(2,1)S(1)}, u32[]{:S(2)}, u32[]{:S(2)}) collective-permute-start(bf16[256,768]{1,0:T(8,128)(2,1)} %refs_0_.1), channel_id=1, source_target_pairs={{0,1},{1,0},{2,3},{3,2},{4,5},{5,4},{6,7},{7,6},{8,9},{9,8},{10,11... | collective-permute-start | bytes 1179656 | tf_op jit(solution)/shard_map/ppermute | solution.py:46
  8.1 9.4 %collective-permute-start.1 = (bf16[544,128]{1,0:T(8,128)(2,1)S(1)}, bf16[544,128]{1,0:T(8,128)(2,1)S(1)}, u32[]{:S(2)}, u32[]{:S(2)}) collective-permute-start(bf16[544,128]{1,0:T(8,128)(2,1)S(1)} %pad_maximum_fusion.2), channel_id=1, source_target_pairs={{0,4},{2,6},{4,0},{6,2},{8,12},{10,14},{12,8},{14,10},{16,20},{18,... | collective-permute-start | bytes 417800 | tf_op jit(solution)/shard_map/ppermute | solution.py:46
  11.0 4.3 %collective-permute-start.5 = (bf16[272,128]{1,0:T(8,128)(2,1)S(1)}, bf16[272,128]{1,0:T(8,128)(2,1)S(1)}, u32[]{:S(2)}, u32[]{:S(2)}) collective-permute-start(bf16[272,128]{1,0:T(8,128)(2,1)S(1)} %collective-permute-done.4.refs_5_), channel_id=1, source_target_pairs={{0,4},{2,6},{4,0},{6,2},{8,12},{10,14},{12,8},{14,10},{16,20},{18,... | collective-permute-start | bytes 208904 | tf_op jit(solution)/shard_map/ppermute | solution.py:46
  13.2 4.3 %collective-permute-start.3 = (bf16[272,128]{1,0:T(8,128)(2,1)S(1)}, bf16[272,128]{1,0:T(8,128)(2,1)S(1)}, u32[]{:S(2)}, u32[]{:S(2)}) collective-permute-start(bf16[272,128]{1,0:T(8,128)(2,1)S(1)} %collective-permute-done.2.refs_4_), channel_id=1, source_target_pairs={{0,4},{2,6},{4,0},{6,2},{8,12},{10,14},{12,8},{14,10},{16,20},{18,... | collective-permute-start | bytes 208904 | tf_op jit(solution)/shard_map/ppermute | solution.py:46
  14.7 4.4 %copy-start = (bf16[256,768]{1,0:T(8,128)(2,1)S(1)}, bf16[256,768]{1,0:T(8,128)(2,1)}, u32[]{:S(2)}) copy-start(bf16[256,768]{1,0:T(8,128)(2,1)} %refs_0_.1) | copy-start | bytes 1179652
  14.8 4.4 %copy-start.1 = (bf16[128,256]{1,0:T(8,128)(2,1)S(1)}, bf16[128,256]{1,0:T(8,128)(2,1)}, u32[]{:S(2)}) copy-start(bf16[128,256]{1,0:T(8,128)(2,1)} %restrict_ref.1) | copy-start | bytes 196612
  14.8 4.2 %collective-permute-start.7 = (bf16[1088,128]{1,0:T(8,128)(2,1)S(1)}, bf16[1088,128]{1,0:T(8,128)(2,1)S(1)}, u32[]{:S(2)}, u32[]{:S(2)}) collective-permute-start(bf16[1088,128]{1,0:T(8,128)(2,1)S(1)} %pad_maximum_fusion.1), channel_id=1, source_target_pairs={{0,2},{2,0},{4,6},{6,4},{8,10},{10,8},{12,14},{14,12},{16,18},{18,... | collective-permute-start | bytes 835592 | tf_op jit(solution)/shard_map/ppermute | solution.py:46
  17.6 1.6 %collective-permute-start.8 = (bf16[1088,128]{1,0:T(8,128)(2,1)S(1)}, bf16[1088,128]{1,0:T(8,128)(2,1)S(1)}, u32[]{:S(2)}, u32[]{:S(2)}) collective-permute-start(bf16[1088,128]{1,0:T(8,128)(2,1)S(1)} %pad_maximum_fusion), channel_id=1, source_target_pairs={{0,2},{2,0},{4,6},{6,4},{8,10},{10,8},{12,14},{14,12},{16,18},{18,... | collective-permute-start | bytes 835592 | tf_op jit(solution)/shard_map/ppermute | solution.py:46

commit v4 on v3

--- a/solution.py
+++ b/solution.py
@@ -12,6 +12,7 @@
 DIGIT = 128
 LANES = 128
 EXTRA = 16
+SMALL = 8 * 1024 * 1024
 
 
 def pack_kernel(columns_ref, prolong_ref, packed_ref):
@@ -46,9 +47,9 @@
     return lax.ppermute(block, axis, [(i, i ^ mask) for i in range(size)])
 
 
-def gather_row(packed, size, fine_other):
+def gather_row(packed, size, fine_other, make):
     if size != 16:
-        return [lax.all_gather(packed, "row", axis=0, tiled=True)], None, fine_other
+        return [lax.all_gather(packed, "row", axis=0, tiled=True)], None, fine_other, make(packed)
     got = {(0,): packed}
     for mask in (4, 8, 12):
         got[(mask,)] = swap(packed, "row", size, mask)
@@ -56,17 +57,18 @@
     for group in ((0, 4), (8,), (12,)):
         both = jnp.concatenate([got[(mask,)] for mask in group])
         across[tuple(mask | 2 for mask in group)] = swap(both, "row", size, 2)
+    index = list(make(got[(4,)]))
     pieces = {**got, **across}
     for half in (got, across):
         both = jnp.concatenate(list(half.values()))
         if half is across:
-            both, fine_other = lax.optimization_barrier((both, fine_other))
+            both, fine_other, index[1] = lax.optimization_barrier((both, fine_other, index[1]))
         group = tuple(mask | 1 for inside in half for mask in inside)
         pieces[group] = swap(both, "row", size, 1)
-    return list(pieces.values()), list(pieces), fine_other
-
-
-def index_kernel(by_xor, slabs, cols, columns_ref, counts_ref, pattern_ref, start_ref, pick_ref, own_ref):
+    return list(pieces.values()), list(pieces), fine_other, index
+
+
+def index_kernel(by_xor, slabs, cols, columns_ref, counts_ref, pattern_ref, start_ref, pick_ref, own_ref, *sums):
     bricks, slots = columns_ref.shape
     share = slots // cols
     owned = pattern_ref.shape[1] // cols
@@ -86,11 +88,11 @@
                 inner = brick - slab * bricks
                 if by_xor:
                     slab = slab ^ row_index
+                start_ref[0, i * slots + part * share + pos] = slab * rows + inner * BRICK
                 here = lane == i * slots + part * share + pos
                 slab_of = jnp.where(here, slab, slab_of)
                 inner_of = jnp.where(here, inner, inner_of)
                 live_of = jnp.where(here, (first + pos < counts_ref[i]).astype(jnp.int32), live_of)
-    start_ref[...] = slab_of * rows + inner_of * BRICK
     place = jnp.where(live_of == 1, slab_of * bricks + inner_of, -1)[0:1, :]
     row = lax.broadcasted_iota(jnp.int32, pick_ref.shape, 0)
     pick_ref[...] = (row == place).astype(jnp.float32).astype(jnp.bfloat16)
@@ -100,21 +102,26 @@
         wanted = pattern_ref[0, col_index * owned + s]
         own = jnp.where(row == s, jnp.where(wanted < 0, -1, wanted + 1), own)
     own_ref[...] = own.astype(jnp.float32)
+    for total in sums:
+        total[...] = jnp.zeros_like(total)
 
 
 def make_index(by_xor, slabs, cols, fine_columns, fine_counts, coarse_pattern):
     bricks = fine_counts.shape[0]
     owned = coarse_pattern.shape[1] // cols
+    slots = fine_columns.shape[1]
     up = lambda n, to: -(-n // to) * to
     return pl.pallas_call(
         functools.partial(index_kernel, by_xor, slabs, cols),
         out_shape=(
-            pltpu.VMEM((8, LANES), jnp.int32),
+            pltpu.SMEM((1, bricks * slots), jnp.int32),
             pltpu.VMEM((up(slabs * bricks, LANES), LANES), jnp.bfloat16),
             pltpu.VMEM((up(owned, 8), LANES), jnp.float32),
-        ),
+        )
+        + (pltpu.VMEM((owned + 1, BRICK, LANES), jnp.float32),) * (bricks * P_SLOTS),
         in_specs=[pl.BlockSpec(memory_space=pltpu.SMEM)] * 3,
-        out_specs=(pl.BlockSpec(memory_space=pltpu.VMEM),) * 3,
+        out_specs=(pl.BlockSpec(memory_space=pltpu.SMEM),) + (pl.BlockSpec(memory_space=pltpu.VMEM),) * (2 + bricks * P_SLOTS),
+        compiler_params=pltpu.CompilerParams(vmem_limit_bytes=SMALL),
         name="index",
     )(fine_columns, fine_counts, coarse_pattern)
 
@@ -123,13 +130,13 @@
     parts = len(masks) if masks else 1
     fines, refs = refs[:cols], refs[cols:]
     pieces, refs = refs[:parts], refs[parts:]
-    out_ref, held_ref, slot_ref, begin_ref, goal_ref, result_ref = refs[:6]
-    sums, (begin_sem, goal_sem, out_sem) = refs[6 : 6 + bricks], refs[6 + bricks :]
+    refs = refs[bricks * P_SLOTS :]
+    out_ref, refs = refs[0], refs[1:]
+    sums, refs = refs[: bricks * P_SLOTS], refs[bricks * P_SLOTS :]
+    held_ref, result_ref, out_sem = refs
     share = slots // cols
     rows = bricks * BRICK + EXTRA
 
-    to_begin = pltpu.make_async_copy(start_ref, begin_ref, begin_sem)
-    to_begin.start()
     table = [jnp.zeros((EXTRA, LANES), jnp.float32) for _ in range(pick_ref.shape[0] // LANES)]
     for piece, inside in zip(pieces, masks if masks else [range(slabs)]):
         for at, slab in enumerate(inside):
@@ -143,13 +150,12 @@
         preferred_element_type=jnp.float32,
     )
     own = own_ref[...]
+    slots_v = []
     offset = lax.broadcasted_iota(jnp.int32, own.shape, 0).astype(jnp.float32) - owned
     for q in range(P_SLOTS):
         coarse = reached[2 * q : 2 * q + 1, :] + DIGIT * reached[2 * q + 1 : 2 * q + 2, :]
         slot = owned + jnp.sum(jnp.where(own == coarse, offset, 0.0), axis=0, keepdims=True)
-        slot_ref[q : q + 1, :] = slot.astype(jnp.int32)
-    to_goal = pltpu.make_async_copy(slot_ref, goal_ref, goal_sem)
-    to_goal.start()
+        slots_v.append(slot.astype(jnp.int32))
 
     source = pieces[0]
     if masks:
@@ -157,13 +163,9 @@
         for piece, inside in zip(pieces, masks):
             for at, slab in enumerate(inside):
                 held_ref[slab * rows : (slab + 1) * rows, :] = piece[at * rows : (at + 1) * rows, :]
-    for total in sums:
-        total[...] = jnp.zeros_like(total)
     left = lax.broadcasted_iota(jnp.int32, (BRICK, LANES), 1) < BRICK
     nothing = jnp.zeros((BRICK, LANES), jnp.bfloat16)
 
-    to_begin.wait()
-    to_goal.wait()
 
     for part in range(cols):
         for pair in range(share // 2):
@@ -171,9 +173,9 @@
                 blocks, where_to = [], []
                 for half in range(2):
                     at = i * slots + part * share + pair * 2 + half
-                    start = pl.multiple_of(begin_ref[0, at], 16)
+                    start = pl.multiple_of(start_ref[0, at], 16)
                     blocks.append(source[pl.ds(start, BRICK), :])
-                    where_to += [goal_ref[q, at] for q in range(P_SLOTS)]
+                    where_to += [slots_v[q][0, at] for q in range(P_SLOTS)]
                 right = jnp.concatenate(
                     [
                         jnp.concatenate([blocks[0], nothing], axis=1),
@@ -185,8 +187,8 @@
                 product = jnp.dot(a, right, preferred_element_type=jnp.float32)
                 for half in range(2):
                     block = product[:, half * LANES : (half + 1) * LANES]
-                    sums[i][where_to[half * 2]] += jnp.where(left, block, 0.0)
-                    sums[i][where_to[half * 2 + 1]] += jnp.where(left, 0.0, block)
+                    sums[i*2+0+2*0][where_to[half * 2]] += block
+                    sums[i*2+1+2*0][where_to[half * 2 + 1]] += block
 
     restrict = restrict_ref[...]
     group = 4 if owned % 4 == 0 else 2
@@ -197,9 +199,9 @@
         for i in range(bricks):
             tops, rests = [], []
             for even in range(at * group, (at + 1) * group, 2):
-                first, second = sums[i][even], sums[i][even + 1]
-                total = jnp.where(left, first, second) + pltpu.roll(
-                    jnp.where(left, second, first), BRICK, 1
+                f0, f1, s0, s1 = sums[2*i][even], sums[2*i+1][even], sums[2*i][even + 1], sums[2*i+1][even+1]
+                total = jnp.where(left, f0, s1) + pltpu.roll(
+                    jnp.where(left, s0, f1), BRICK, 1
                 )
                 tops.append(total.astype(jnp.bfloat16))
                 rests.append((total - tops[-1].astype(jnp.float32)).astype(jnp.bfloat16))
@@ -221,29 +223,27 @@
 def operate(slabs, cols, bricks, slots, owned, index, restrict_rows, fines, pieces, masks):
     rows = bricks * BRICK + EXTRA
     vmem = pl.BlockSpec(memory_space=pltpu.VMEM)
+    smem = pl.BlockSpec(memory_space=pltpu.SMEM)
     held_rows = slabs * rows if masks else 16
     shape = (restrict_rows.shape[0], owned * BRICK)
+    starts, pick, own, *sums = index
+    starts = pltpu.with_memory_space_constraint(starts, pltpu.SMEM)
+    given = (starts, pick, own, restrict_rows, *fines, *pieces)
     return pl.pallas_call(
         functools.partial(operator_kernel, slabs, masks, bricks, slots, owned, cols=cols),
-        out_shape=jax.ShapeDtypeStruct(shape, jnp.float32),
-        in_specs=[vmem] * (4 + cols + len(pieces)),
-        out_specs=pl.BlockSpec(memory_space=pl.ANY),
+        out_shape=[jax.ShapeDtypeStruct(shape, jnp.float32)]
+        + [pltpu.VMEM(each.shape, jnp.float32) for each in sums],
+        in_specs=[smem] + [vmem] * (len(given) - 1 + len(sums)),
+        out_specs=[pl.BlockSpec(memory_space=pl.ANY)] + [vmem] * len(sums),
+        input_output_aliases={len(given) + at: 1 + at for at in range(len(sums))},
         scratch_shapes=[
             pltpu.VMEM((held_rows, LANES), jnp.bfloat16),
-            pltpu.VMEM((8, LANES), jnp.int32),
-            pltpu.SMEM((8, LANES), jnp.int32),
-            pltpu.SMEM((8, LANES), jnp.int32),
             pltpu.VMEM(shape, jnp.float32),
-        ]
-        + [pltpu.VMEM((owned + 1, BRICK, LANES), jnp.float32)] * bricks
-        + [
-            pltpu.SemaphoreType.DMA,
-            pltpu.SemaphoreType.DMA,
             pltpu.SemaphoreType.DMA((owned // 2,)),
         ],
         compiler_params=pltpu.CompilerParams(vmem_limit_bytes=32 * 1024 * 1024),
         name="operator",
-    )(*index, restrict_rows, *fines, *pieces)
+    )(*given, *sums)[0]
 
 
 def local(
@@ -261,11 +261,13 @@
     owned = coarse_pattern.shape[1] // cols
     packed = pack(prolong, prolong_columns)
     others = [swap(fine_matrix, "col", cols, d) for d in range(1, cols)]
-    pieces, masks, others = gather_row(packed, slabs, others)
+
+    def make(after):
+        columns, _ = lax.optimization_barrier((fine_columns, after))
+        return make_index(slabs == 16, slabs, cols, columns, fine_counts, coarse_pattern)
+
+    pieces, masks, others, index = gather_row(packed, slabs, others, make)
     fines = [pltpu.with_memory_space_constraint(fine_matrix, pltpu.VMEM)] + others
-    if masks:
-        fine_columns, pieces[1] = lax.optimization_barrier((fine_columns, pieces[1]))
-    index = make_index(masks is not None, slabs, cols, fine_columns, fine_counts, coarse_pattern)
     return operate(slabs, cols, bricks, slots, owned, index, restrict_rows, fines, pieces, masks)
 
 

time: 22.9 us -> 22 us (0.961)
  Pallas kernels: 5.78 us -> 5.21 us
  waiting for transfers between devices: 4.89 us -> 4.49 us
    pallas_call x1, Pallas kernels: 3.57 us -> 2.66 us  [operate(): pl.pallas_call(functools.partial(operator_kernel, slabs, masks, bricks, s...]
    ppermute x9, waiting for transfers between devices: 4.89 us -> 4.49 us  [swap(): return lax.ppermute(block, axis, [(i, i ^ mask) for i in range(size)])]
    pallas_call x1, Pallas kernels: 1.33 us -> 1.67 us  [make_index(): pl.pallas_call(functools.partial(index_kernel, by_xor, slabs, cols), out_...]
  transfers between devices with their start and end apart: 9 -> 9, of which waited for: 5 -> 4; matrix products, arithmetic and copies ran while one was open for 0% -> 0% of each run, Pallas kernels for 6% -> 8%
where the time goes in v4:
time: 22 us; the launch traced here: 21.8 us
  starting transfers between devices  11.9 us (54%)
  Pallas kernels  5.21 us (24%)
  waiting for transfers between devices  4.49 us (20%)
    ppermute x9, starting transfers between devices, swap(): return lax.ppermute(block, axis, [(i, i ^ mask) for i in range(size)])  11.9 us
    ppermute x9, waiting for transfers between devices, swap(): return lax.ppermute(block, axis, [(i, i ^ mask) for i in range(size)])  4.49 us
    pallas_call x1, Pallas kernels, operate(): pl.pallas_call(functools.partial(operator_kernel, slabs, masks, bricks, s...  2.66 us
    pallas_call x1, Pallas kernels, make_index(): pl.pallas_call(functools.partial(index_kernel, by_xor, slabs, cols), out_...  1.67 us
    pallas_call x1, Pallas kernels, pack(): pl.pallas_call(pack_kernel, out_shape=pltpu.VMEM((prolong.shape[0] + EXTR...  0.88 us
  transfers between devices with their start and end apart: 9, of which 4 were waited for; matrix products, arithmetic and copies ran while one was open for 0% of the time, Pallas kernels for 8%

profile of v4, /device:TPU:0, one launch (start us, length us, event | category | flops | bytes accessed | tf_op | source)
XLA Modules:
  0.0 21.8 jit_solution(691992332582466576)
XLA Ops:
  0.0 0.9 %pack.1.refs_2_ = bf16[272,128]{1,0:T(8,128)(2,1)S(1)} custom-call(s32[2,4]{1,0:T(2,128)} %bitcast.1, bf16[256,128]{1,0:T(8,128)(2,1)} %prolong_ref.1), custom_call_target="tpu_custom_call" | custom-call | tf_op jit(solution)/shard_map/pack/pallas_call | solution.py:34
  0.9 3.1 %collective-permute-start = (bf16[272,128]{1,0:T(8,128)(2,1)S(1)}, bf16[272,128]{1,0:T(8,128)(2,1)S(1)}, u32[]{:S(2)}, u32[]{:S(2)}) collective-permute-start(bf16[272,128]{1,0:T(8,128)(2,1)S(1)} %pack.1.refs_2_), channel_id=1, source_target_pairs={{0,8},{2,10},{4,12},{6,14},{8,0},{10,2},{12,4},{14,6},{16,24},{18,... | collective-permute-start | bytes 208904 | tf_op jit(solution)/shard_map/ppermute | solution.py:47
  4.0 2.5 %collective-permute-start.4 = (bf16[272,128]{1,0:T(8,128)(2,1)S(1)}, bf16[272,128]{1,0:T(8,128)(2,1)S(1)}, u32[]{:S(2)}, u32[]{:S(2)}) collective-permute-start(bf16[272,128]{1,0:T(8,128)(2,1)S(1)} %pack.1.refs_2_), channel_id=1, source_target_pairs={{0,24},{2,26},{4,28},{6,30},{8,16},{10,18},{12,20},{14,22},{16,8},... | collective-permute-start | bytes 208904 | tf_op jit(solution)/shard_map/ppermute | solution.py:47
  6.5 0.1 collective-permute-start.2
  6.6 1.5 %collective-permute-start.6 = (bf16[256,768]{1,0:T(8,128)(2,1)}, bf16[256,768]{1,0:T(8,128)(2,1)S(1)}, u32[]{:S(2)}, u32[]{:S(2)}) collective-permute-start(bf16[256,768]{1,0:T(8,128)(2,1)} %refs_0_.1), channel_id=1, source_target_pairs={{0,1},{1,0},{2,3},{3,2},{4,5},{5,4},{6,7},{7,6},{8,9},{9,8},{10,11... | collective-permute-start | bytes 1179656 | tf_op jit(solution)/shard_map/ppermute | solution.py:47
  8.1 0.0 collective-permute-done.refs_3_
  8.1 0.0 copy-start.2
  8.1 0.0 copy-start.3
  8.1 0.0 copy-start.4
  8.1 1.6 %collective-permute-start.1 = (bf16[544,128]{1,0:T(8,128)(2,1)S(1)}, bf16[544,128]{1,0:T(8,128)(2,1)S(1)}, u32[]{:S(2)}, u32[]{:S(2)}) collective-permute-start(bf16[544,128]{1,0:T(8,128)(2,1)S(1)} %pad_maximum_fusion.2), channel_id=1, source_target_pairs={{0,4},{2,6},{4,0},{6,2},{8,12},{10,14},{12,8},{14,10},{16,20},{18,... | collective-permute-start | bytes 417800 | tf_op jit(solution)/shard_map/ppermute | solution.py:47
  9.7 1.3 %collective-permute-done.4.refs_5_ = bf16[272,128]{1,0:T(8,128)(2,1)S(1)} collective-permute-done((bf16[272,128]{1,0:T(8,128)(2,1)S(1)}, bf16[272,128]{1,0:T(8,128)(2,1)S(1)}, u32[]{:S(2)}, u32[]{:S(2)}) %collective-permute-start.4) | collective-permute-done | bytes 69664 | tf_op jit(solution)/shard_map/ppermute | solution.py:47
  11.0 1.5 %collective-permute-start.5 = (bf16[272,128]{1,0:T(8,128)(2,1)S(1)}, bf16[272,128]{1,0:T(8,128)(2,1)S(1)}, u32[]{:S(2)}, u32[]{:S(2)}) collective-permute-start(bf16[272,128]{1,0:T(8,128)(2,1)S(1)} %collective-permute-done.4.refs_5_), channel_id=1, source_target_pairs={{0,4},{2,6},{4,0},{6,2},{8,12},{10,14},{12,8},{14,10},{16,20},{18,... | collective-permute-start | bytes 208904 | tf_op jit(solution)/shard_map/ppermute | solution.py:47
  12.5 0.7 %collective-permute-done.2.refs_4_ = bf16[272,128]{1,0:T(8,128)(2,1)S(1)} collective-permute-done((bf16[272,128]{1,0:T(8,128)(2,1)S(1)}, bf16[272,128]{1,0:T(8,128)(2,1)S(1)}, u32[]{:S(2)}, u32[]{:S(2)}) %collective-permute-start.2) | collective-permute-done | bytes 69664 | tf_op jit(solution)/shard_map/ppermute | solution.py:47
  13.2 1.5 %collective-permute-start.3 = (bf16[272,128]{1,0:T(8,128)(2,1)S(1)}, bf16[272,128]{1,0:T(8,128)(2,1)S(1)}, u32[]{:S(2)}, u32[]{:S(2)}) collective-permute-start(bf16[272,128]{1,0:T(8,128)(2,1)S(1)} %collective-permute-done.2.refs_4_), channel_id=1, source_target_pairs={{0,4},{2,6},{4,0},{6,2},{8,12},{10,14},{12,8},{14,10},{16,20},{18,... | collective-permute-start | bytes 208904 | tf_op jit(solution)/shard_map/ppermute | solution.py:47
  14.7 0.0 copy-start
  14.8 0.1 collective-permute-start.7
  14.8 0.0 copy-done.2
  14.8 0.0 copy-done.3
  14.9 0.0 copy-done.4
  14.9 1.7 %index.1 = (s32[1,96]{1,0:T(1,128)S(4)}, bf16[128,128]{1,0:T(8,128)(2,1)S(1)}, f32[24,128]{1,0:T(8,128)S(1)}, f32[25,64,128]{2,1,0:T(8,128)S(1)}, f32[25,64,128]...) custom-call(s32[4,24]{1,0:T(4,128)S(1)} %copy-done.2, ...), custom_call_target="tpu_custom_call" | custom-call | tf_op jit(solution)/shard_map/index/pallas_call | solution.py:114
  16.5 0.0 collective-permute-done.5.refs_8_
  16.6 1.0 %collective-permute-done.3.refs_7_ = bf16[272,128]{1,0:T(8,128)(2,1)S(1)} collective-permute-done((bf16[272,128]{1,0:T(8,128)(2,1)S(1)}, bf16[272,128]{1,0:T(8,128)(2,1)S(1)}, u32[]{:S(2)}, u32[]{:S(2)}) %collective-permute-start.3) | collective-permute-done | bytes 69664 | tf_op jit(solution)/shard_map/ppermute | solution.py:47
  17.5 0.0 collective-permute-done.1.refs_6_
  17.5 0.0 copy-start.1
  17.5 0.0 collective-permute-done.6.refs_1_
  17.6 0.1 collective-permute-start.8
  17.6 0.0 collective-permute-done.7.refs_9_
  17.6 1.5 %collective-permute-done.8.refs_10_ = bf16[1088,128]{1,0:T(8,128)(2,1)S(1)} collective-permute-done((bf16[1088,128]{1,0:T(8,128)(2,1)S(1)}, bf16[1088,128]{1,0:T(8,128)(2,1)S(1)}, u32[]{:S(2)}, u32[]{:S(2)}) %collective-permute-start.8) | collective-permute-done | bytes 278560 | tf_op jit(solution)/shard_map/ppermute | solution.py:47
  19.2 0.0 copy-done
  19.2 0.0 copy-done.1
  19.2 2.7 %operator.1 = (f32[128,1536]{1,0:T(8,128)}, f32[25,64,128]{2,1,0:T(8,128)S(1)}, f32[25,64,128]{2,1,0:T(8,128)S(1)}, f32[25,64,128]{2,1,0:T(8,128)S(1)}, f32[25,6...) custom-call(s32[1,96]{1,0:T(1,128)S(4)} %get-tuple-element.22.start_, ...), custom_call_target="tpu_custom_call", output_to_operand_aliasing={{1}: (15, {}), {2}: (16, {}), {3}: (17, {}), {4}: (18, {}),... | custom-call | tf_op jit(solution)/shard_map/operator/pallas_call | solution.py:232
  (3 shorter events, 0.0 us)
Async XLA Ops:
  0.9 7.2 %collective-permute-start = (bf16[272,128]{1,0:T(8,128)(2,1)S(1)}, bf16[272,128]{1,0:T(8,128)(2,1)S(1)}, u32[]{:S(2)}, u32[]{:S(2)}) collective-permute-start(bf16[272,128]{1,0:T(8,128)(2,1)S(1)} %pack.1.refs_2_), channel_id=1, source_target_pairs={{0,8},{2,10},{4,12},{6,14},{8,0},{10,2},{12,4},{14,6},{16,24},{18,... | collective-permute-start | bytes 208904 | tf_op jit(solution)/shard_map/ppermute | solution.py:47
  4.0 7.0 %collective-permute-start.4 = (bf16[272,128]{1,0:T(8,128)(2,1)S(1)}, bf16[272,128]{1,0:T(8,128)(2,1)S(1)}, u32[]{:S(2)}, u32[]{:S(2)}) collective-permute-start(bf16[272,128]{1,0:T(8,128)(2,1)S(1)} %pack.1.refs_2_), channel_id=1, source_target_pairs={{0,24},{2,26},{4,28},{6,30},{8,16},{10,18},{12,20},{14,22},{16,8},... | collective-permute-start | bytes 208904 | tf_op jit(solution)/shard_map/ppermute | solution.py:47
  6.5 6.8 %collective-permute-start.2 = (bf16[272,128]{1,0:T(8,128)(2,1)S(1)}, bf16[272,128]{1,0:T(8,128)(2,1)S(1)}, u32[]{:S(2)}, u32[]{:S(2)}) collective-permute-start(bf16[272,128]{1,0:T(8,128)(2,1)S(1)} %pack.1.refs_2_), channel_id=1, source_target_pairs={{0,16},{2,18},{4,20},{6,22},{8,24},{10,26},{12,28},{14,30},{16,0},... | collective-permute-start | bytes 208904 | tf_op jit(solution)/shard_map/ppermute | solution.py:47
  6.6 11.0 %collective-permute-start.6 = (bf16[256,768]{1,0:T(8,128)(2,1)}, bf16[256,768]{1,0:T(8,128)(2,1)S(1)}, u32[]{:S(2)}, u32[]{:S(2)}) collective-permute-start(bf16[256,768]{1,0:T(8,128)(2,1)} %refs_0_.1), channel_id=1, source_target_pairs={{0,1},{1,0},{2,3},{3,2},{4,5},{5,4},{6,7},{7,6},{8,9},{9,8},{10,11... | collective-permute-start | bytes 1179656 | tf_op jit(solution)/shard_map/ppermute | solution.py:47
  8.1 6.8 %copy-start.2 = (s32[4,24]{1,0:T(4,128)S(1)}, s32[4,24]{1,0:T(4,128)}, u32[]{:S(2)}) copy-start(s32[4,24]{1,0:T(4,128)} %columns_ref) | copy-start | bytes 1156
  8.1 6.8 %copy-start.3 = (s32[4]{0:T(128)S(1)}, s32[4]{0:T(128)}, u32[]{:S(2)}) copy-start(s32[4]{0:T(128)} %counts_ref.1) | copy-start | bytes 52
  8.1 6.8 %copy-start.4 = (s32[1,48]{1,0:T(1,128)S(1)}, s32[1,48]{1,0:T(1,128)}, u32[]{:S(2)}) copy-start(s32[1,48]{1,0:T(1,128)} %pattern_ref.1) | copy-start | bytes 580
  8.1 9.4 %collective-permute-start.1 = (bf16[544,128]{1,0:T(8,128)(2,1)S(1)}, bf16[544,128]{1,0:T(8,128)(2,1)S(1)}, u32[]{:S(2)}, u32[]{:S(2)}) collective-permute-start(bf16[544,128]{1,0:T(8,128)(2,1)S(1)} %pad_maximum_fusion.2), channel_id=1, source_target_pairs={{0,4},{2,6},{4,0},{6,2},{8,12},{10,14},{12,8},{14,10},{16,20},{18,... | collective-permute-start | bytes 417800 | tf_op jit(solution)/shard_map/ppermute | solution.py:47
  11.0 5.5 %collective-permute-start.5 = (bf16[272,128]{1,0:T(8,128)(2,1)S(1)}, bf16[272,128]{1,0:T(8,128)(2,1)S(1)}, u32[]{:S(2)}, u32[]{:S(2)}) collective-permute-start(bf16[272,128]{1,0:T(8,128)(2,1)S(1)} %collective-permute-done.4.refs_5_), channel_id=1, source_target_pairs={{0,4},{2,6},{4,0},{6,2},{8,12},{10,14},{12,8},{14,10},{16,20},{18,... | collective-permute-start | bytes 208904 | tf_op jit(solution)/shard_map/ppermute | solution.py:47
  13.2 4.3 %collective-permute-start.3 = (bf16[272,128]{1,0:T(8,128)(2,1)S(1)}, bf16[272,128]{1,0:T(8,128)(2,1)S(1)}, u32[]{:S(2)}, u32[]{:S(2)}) collective-permute-start(bf16[272,128]{1,0:T(8,128)(2,1)S(1)} %collective-permute-done.2.refs_4_), channel_id=1, source_target_pairs={{0,4},{2,6},{4,0},{6,2},{8,12},{10,14},{12,8},{14,10},{16,20},{18,... | collective-permute-start | bytes 208904 | tf_op jit(solution)/shard_map/ppermute | solution.py:47
  14.7 4.4 %copy-start = (bf16[256,768]{1,0:T(8,128)(2,1)S(1)}, bf16[256,768]{1,0:T(8,128)(2,1)}, u32[]{:S(2)}) copy-start(bf16[256,768]{1,0:T(8,128)(2,1)} %refs_0_.1) | copy-start | bytes 1179652
  14.8 2.9 %collective-permute-start.7 = (bf16[1088,128]{1,0:T(8,128)(2,1)S(1)}, bf16[1088,128]{1,0:T(8,128)(2,1)S(1)}, u32[]{:S(2)}, u32[]{:S(2)}) collective-permute-start(bf16[1088,128]{1,0:T(8,128)(2,1)S(1)} %pad_maximum_fusion.1), channel_id=1, source_target_pairs={{0,2},{2,0},{4,6},{6,4},{8,10},{10,8},{12,14},{14,12},{16,18},{18,... | collective-permute-start | bytes 835592 | tf_op jit(solution)/shard_map/ppermute | solution.py:47
  17.5 1.7 %copy-start.1 = (bf16[128,256]{1,0:T(8,128)(2,1)S(1)}, bf16[128,256]{1,0:T(8,128)(2,1)}, u32[]{:S(2)}) copy-start(bf16[128,256]{1,0:T(8,128)(2,1)} %restrict_ref.1) | copy-start | bytes 196612
  17.6 1.6 %collective-permute-start.8 = (bf16[1088,128]{1,0:T(8,128)(2,1)S(1)}, bf16[1088,128]{1,0:T(8,128)(2,1)S(1)}, u32[]{:S(2)}, u32[]{:S(2)}) collective-permute-start(bf16[1088,128]{1,0:T(8,128)(2,1)S(1)} %pad_maximum_fusion), channel_id=1, source_target_pairs={{0,2},{2,0},{4,6},{6,4},{8,10},{10,8},{12,14},{14,12},{16,18},{18,... | collective-permute-start | bytes 835592 | tf_op jit(solution)/shard_map/ppermute | solution.py:47

commit v5 on v4

--- a/solution.py
+++ b/solution.py
@@ -47,25 +47,25 @@
     return lax.ppermute(block, axis, [(i, i ^ mask) for i in range(size)])
 
 
-def gather_row(packed, size, fine_other, make):
+def gather_row(packed, size, make):
     if size != 16:
-        return [lax.all_gather(packed, "row", axis=0, tiled=True)], None, fine_other, make(packed)
+        return [lax.all_gather(packed, "row", axis=0, tiled=True)], None, make(packed)
     got = {(0,): packed}
-    for mask in (4, 8, 12):
+    for mask in (4, 12, 8):
         got[(mask,)] = swap(packed, "row", size, mask)
     across = {}
-    for group in ((0, 4), (8,), (12,)):
+    for group in ((12,), (0,), (4,), (8,)):
         both = jnp.concatenate([got[(mask,)] for mask in group])
         across[tuple(mask | 2 for mask in group)] = swap(both, "row", size, 2)
-    index = list(make(got[(4,)]))
+    index = list(make(got[(8,)]))
     pieces = {**got, **across}
-    for half in (got, across):
-        both = jnp.concatenate(list(half.values()))
-        if half is across:
-            both, fine_other, index[1] = lax.optimization_barrier((both, fine_other, index[1]))
+    for half in (((12,), (4,), (8,), (0,)), ((6,), (14,), (2,), (10,))):
+        both = jnp.concatenate([pieces[inside] for inside in half])
+        if half[0] in across:
+            both, index[1] = lax.optimization_barrier((both, index[1]))
         group = tuple(mask | 1 for inside in half for mask in inside)
         pieces[group] = swap(both, "row", size, 1)
-    return list(pieces.values()), list(pieces), fine_other, index
+    return list(pieces.values()), list(pieces), index
 
 
 def index_kernel(by_xor, slabs, cols, columns_ref, counts_ref, pattern_ref, start_ref, pick_ref, own_ref, *sums):
@@ -156,6 +156,7 @@
         coarse = reached[2 * q : 2 * q + 1, :] + DIGIT * reached[2 * q + 1 : 2 * q + 2, :]
         slot = owned + jnp.sum(jnp.where(own == coarse, offset, 0.0), axis=0, keepdims=True)
         slots_v.append(slot.astype(jnp.int32))
+    goals = slots_v[0] + 256 * slots_v[1]
 
     source = pieces[0]
     if masks:
@@ -175,7 +176,8 @@
                     at = i * slots + part * share + pair * 2 + half
                     start = pl.multiple_of(start_ref[0, at], 16)
                     blocks.append(source[pl.ds(start, BRICK), :])
-                    where_to += [slots_v[q][0, at] for q in range(P_SLOTS)]
+                    goal = goals[0, at]
+                    where_to += [goal & 255, goal >> 8]
                 right = jnp.concatenate(
                     [
                         jnp.concatenate([blocks[0], nothing], axis=1),
@@ -191,7 +193,7 @@
                     sums[i*2+1+2*0][where_to[half * 2 + 1]] += block
 
     restrict = restrict_ref[...]
-    group = 4 if owned % 4 == 0 else 2
+    group = 2
     width = group * BRICK
     leaving = []
     for at in range(owned // group):
@@ -266,7 +268,7 @@
         columns, _ = lax.optimization_barrier((fine_columns, after))
         return make_index(slabs == 16, slabs, cols, columns, fine_counts, coarse_pattern)
 
-    pieces, masks, others, index = gather_row(packed, slabs, others, make)
+    pieces, masks, index = gather_row(packed, slabs, make)
     fines = [pltpu.with_memory_space_constraint(fine_matrix, pltpu.VMEM)] + others
     return operate(slabs, cols, bricks, slots, owned, index, restrict_rows, fines, pieces, masks)
 

time: 22 us -> 21.2 us (0.964)
  waiting for transfers between devices: 4.49 us -> 3.59 us
  starting transfers between devices: 11.9 us -> 12.2 us
    ppermute x9 -> x10, waiting for transfers between devices: 4.49 us -> 3.59 us  [swap(): return lax.ppermute(block, axis, [(i, i ^ mask) for i in range(size)])]
    ppermute x9 -> x10, starting transfers between devices: 11.9 us -> 12.2 us  [swap(): return lax.ppermute(block, axis, [(i, i ^ mask) for i in range(size)])]
  transfers between devices with their start and end apart: 9 -> 10, of which waited for: 4 -> 5; matrix products, arithmetic and copies ran while one was open for 0% -> 0% of each run, Pallas kernels for 8% -> 8%
where the time goes in v5:
time: 21.2 us; the launch traced here: 21 us
  starting transfers between devices  12.2 us (58%)
  Pallas kernels  5.07 us (24%)
  waiting for transfers between devices  3.59 us (17%)
    ppermute x10, starting transfers between devices, swap(): return lax.ppermute(block, axis, [(i, i ^ mask) for i in range(size)])  12.2 us
    ppermute x10, waiting for transfers between devices, swap(): return lax.ppermute(block, axis, [(i, i ^ mask) for i in range(size)])  3.59 us
    pallas_call x1, Pallas kernels, operate(): pl.pallas_call(functools.partial(operator_kernel, slabs, masks, bricks, s...  2.53 us
    pallas_call x1, Pallas kernels, make_index(): pl.pallas_call(functools.partial(index_kernel, by_xor, slabs, cols), out_...  1.67 us
    pallas_call x1, Pallas kernels, pack(): pl.pallas_call(pack_kernel, out_shape=pltpu.VMEM((prolong.shape[0] + EXTR...  0.88 us
  transfers between devices with their start and end apart: 10, of which 5 were waited for; matrix products, arithmetic and copies ran while one was open for 0% of the time, Pallas kernels for 8%

profile of v5, /device:TPU:0, one launch (start us, length us, event | category | flops | bytes accessed | tf_op | source)
XLA Modules:
  0.0 21.0 jit_solution(4942717639866482559)
XLA Ops:
  0.0 0.9 %pack.1.refs_2_ = bf16[272,128]{1,0:T(8,128)(2,1)S(1)} custom-call(s32[2,4]{1,0:T(2,128)} %bitcast.1, bf16[256,128]{1,0:T(8,128)(2,1)} %prolong_ref.1), custom_call_target="tpu_custom_call" | custom-call | tf_op jit(solution)/shard_map/pack/pallas_call | solution.py:34
  0.9 0.0 copy-start.2
  0.9 0.0 copy-start.3
  0.9 0.0 copy-start.4
  0.9 5.1 %collective-permute-start.3 = (bf16[272,128]{1,0:T(8,128)(2,1)S(1)}, bf16[272,128]{1,0:T(8,128)(2,1)S(1)}, u32[]{:S(2)}, u32[]{:S(2)}) collective-permute-start(bf16[272,128]{1,0:T(8,128)(2,1)S(1)} %pack.1.refs_2_), channel_id=1, source_target_pairs={{0,24},{2,26},{4,28},{6,30},{8,16},{10,18},{12,20},{14,22},{16,8},... | collective-permute-start | bytes 208904 | tf_op jit(solution)/shard_map/ppermute | solution.py:47
  6.0 0.0 collective-permute-start.1
  6.0 0.6 %collective-permute-start = (bf16[272,128]{1,0:T(8,128)(2,1)S(1)}, bf16[272,128]{1,0:T(8,128)(2,1)S(1)}, u32[]{:S(2)}, u32[]{:S(2)}) collective-permute-start(bf16[272,128]{1,0:T(8,128)(2,1)S(1)} %pack.1.refs_2_), channel_id=1, source_target_pairs={{0,16},{2,18},{4,20},{6,22},{8,24},{10,26},{12,28},{14,30},{16,0},... | collective-permute-start | bytes 208904 | tf_op jit(solution)/shard_map/ppermute | solution.py:47
  6.7 1.7 %collective-permute-start.5 = (bf16[272,128]{1,0:T(8,128)(2,1)S(1)}, bf16[272,128]{1,0:T(8,128)(2,1)S(1)}, u32[]{:S(2)}, u32[]{:S(2)}) collective-permute-start(bf16[272,128]{1,0:T(8,128)(2,1)S(1)} %pack.1.refs_2_), channel_id=1, source_target_pairs={{0,4},{2,6},{4,0},{6,2},{8,12},{10,14},{12,8},{14,10},{16,20},{18,... | collective-permute-start | bytes 208904 | tf_op jit(solution)/shard_map/ppermute | solution.py:47
  8.3 1.5 %collective-permute-start.7 = (bf16[256,768]{1,0:T(8,128)(2,1)}, bf16[256,768]{1,0:T(8,128)(2,1)S(1)}, u32[]{:S(2)}, u32[]{:S(2)}) collective-permute-start(bf16[256,768]{1,0:T(8,128)(2,1)} %refs_0_.1), channel_id=1, source_target_pairs={{0,1},{1,0},{2,3},{3,2},{4,5},{5,4},{6,7},{7,6},{8,9},{9,8},{10,11... | collective-permute-start | bytes 1179656 | tf_op jit(solution)/shard_map/ppermute | solution.py:47
  9.8 0.0 collective-permute-done.3.refs_4_
  9.8 0.8 %collective-permute-start.4 = (bf16[272,128]{1,0:T(8,128)(2,1)S(1)}, bf16[272,128]{1,0:T(8,128)(2,1)S(1)}, u32[]{:S(2)}, u32[]{:S(2)}) collective-permute-start(bf16[272,128]{1,0:T(8,128)(2,1)S(1)} %collective-permute-done.3.refs_4_), channel_id=1, source_target_pairs={{0,4},{2,6},{4,0},{6,2},{8,12},{10,14},{12,8},{14,10},{16,20},{18,... | collective-permute-start | bytes 208904 | tf_op jit(solution)/shard_map/ppermute | solution.py:47
  10.6 0.3 %collective-permute-done.1.refs_3_ = bf16[272,128]{1,0:T(8,128)(2,1)S(1)} collective-permute-done((bf16[272,128]{1,0:T(8,128)(2,1)S(1)}, bf16[272,128]{1,0:T(8,128)(2,1)S(1)}, u32[]{:S(2)}, u32[]{:S(2)}) %collective-permute-start.1) | collective-permute-done | bytes 69664 | tf_op jit(solution)/shard_map/ppermute | solution.py:47
  10.9 1.7 %collective-permute-start.2 = (bf16[272,128]{1,0:T(8,128)(2,1)S(1)}, bf16[272,128]{1,0:T(8,128)(2,1)S(1)}, u32[]{:S(2)}, u32[]{:S(2)}) collective-permute-start(bf16[272,128]{1,0:T(8,128)(2,1)S(1)} %collective-permute-done.1.refs_3_), channel_id=1, source_target_pairs={{0,4},{2,6},{4,0},{6,2},{8,12},{10,14},{12,8},{14,10},{16,20},{18,... | collective-permute-start | bytes 208904 | tf_op jit(solution)/shard_map/ppermute | solution.py:47
  12.5 0.0 collective-permute-done.refs_5_
  12.6 0.7 %collective-permute-start.6 = (bf16[272,128]{1,0:T(8,128)(2,1)S(1)}, bf16[272,128]{1,0:T(8,128)(2,1)S(1)}, u32[]{:S(2)}, u32[]{:S(2)}) collective-permute-start(bf16[272,128]{1,0:T(8,128)(2,1)S(1)} %collective-permute-done.refs_5_), channel_id=1, source_target_pairs={{0,4},{2,6},{4,0},{6,2},{8,12},{10,14},{12,8},{14,10},{16,20},{18,... | collective-permute-start | bytes 208904 | tf_op jit(solution)/shard_map/ppermute | solution.py:47
  13.3 0.0 copy-done.2
  13.3 0.0 copy-done.3
  13.3 0.0 copy-done.4
  13.3 0.0 copy-start
  13.3 1.7 %index.1 = (s32[1,96]{1,0:T(1,128)S(4)}, bf16[128,128]{1,0:T(8,128)(2,1)S(1)}, f32[24,128]{1,0:T(8,128)S(1)}, f32[25,64,128]{2,1,0:T(8,128)S(1)}, f32[25,64,128]...) custom-call(s32[4,24]{1,0:T(4,128)S(1)} %copy-done.2, ...), custom_call_target="tpu_custom_call" | custom-call | tf_op jit(solution)/shard_map/index/pallas_call | solution.py:114
  15.0 0.0 collective-permute-done.5.refs_7_
  15.0 0.1 collective-permute-start.8
  15.1 0.0 collective-permute-done.4.refs_6_
  15.1 0.9 %collective-permute-done.2.refs_8_ = bf16[272,128]{1,0:T(8,128)(2,1)S(1)} collective-permute-done((bf16[272,128]{1,0:T(8,128)(2,1)S(1)}, bf16[272,128]{1,0:T(8,128)(2,1)S(1)}, u32[]{:S(2)}, u32[]{:S(2)}) %collective-permute-start.2) | collective-permute-done | bytes 69664 | tf_op jit(solution)/shard_map/ppermute | solution.py:47
  16.0 0.9 %collective-permute-done.6.refs_9_ = bf16[272,128]{1,0:T(8,128)(2,1)S(1)} collective-permute-done((bf16[272,128]{1,0:T(8,128)(2,1)S(1)}, bf16[272,128]{1,0:T(8,128)(2,1)S(1)}, u32[]{:S(2)}, u32[]{:S(2)}) %collective-permute-start.6) | collective-permute-done | bytes 69664 | tf_op jit(solution)/shard_map/ppermute | solution.py:47
  16.9 0.0 copy-start.1
  16.9 0.1 collective-permute-start.9
  17.0 0.0 collective-permute-done.8.refs_10_
  17.0 1.4 %collective-permute-done.7.refs_1_ = bf16[256,768]{1,0:T(8,128)(2,1)S(1)} collective-permute-done((bf16[256,768]{1,0:T(8,128)(2,1)}, bf16[256,768]{1,0:T(8,128)(2,1)S(1)}, u32[]{:S(2)}, u32[]{:S(2)}) %collective-permute-start.7) | collective-permute-done | bytes 393248 | tf_op jit(solution)/shard_map/ppermute | solution.py:47
  18.4 0.1 collective-permute-done.9.refs_11_
  18.5 0.0 copy-done
  18.5 0.0 copy-done.1
  18.5 2.5 %operator.1 = (f32[128,1536]{1,0:T(8,128)}, f32[25,64,128]{2,1,0:T(8,128)S(1)}, f32[25,64,128]{2,1,0:T(8,128)S(1)}, f32[25,64,128]{2,1,0:T(8,128)S(1)}, f32[25,6...) custom-call(s32[1,96]{1,0:T(1,128)S(4)} %get-tuple-element.21.start_, ...), custom_call_target="tpu_custom_call", output_to_operand_aliasing={{1}: (16, {}), {2}: (17, {}), {3}: (18, {}), {4}: (19, {}),... | custom-call | tf_op jit(solution)/shard_map/operator/pallas_call | solution.py:234
  (2 shorter events, 0.0 us)
Async XLA Ops:
  0.9 12.4 %copy-start.2 = (s32[4,24]{1,0:T(4,128)S(1)}, s32[4,24]{1,0:T(4,128)}, u32[]{:S(2)}) copy-start(s32[4,24]{1,0:T(4,128)} %columns_ref) | copy-start | bytes 1156
  0.9 12.4 %copy-start.3 = (s32[4]{0:T(128)S(1)}, s32[4]{0:T(128)}, u32[]{:S(2)}) copy-start(s32[4]{0:T(128)} %counts_ref.1) | copy-start | bytes 52
  0.9 12.4 %copy-start.4 = (s32[1,48]{1,0:T(1,128)S(1)}, s32[1,48]{1,0:T(1,128)}, u32[]{:S(2)}) copy-start(s32[1,48]{1,0:T(1,128)} %pattern_ref.1) | copy-start | bytes 580
  0.9 8.9 %collective-permute-start.3 = (bf16[272,128]{1,0:T(8,128)(2,1)S(1)}, bf16[272,128]{1,0:T(8,128)(2,1)S(1)}, u32[]{:S(2)}, u32[]{:S(2)}) collective-permute-start(bf16[272,128]{1,0:T(8,128)(2,1)S(1)} %pack.1.refs_2_), channel_id=1, source_target_pairs={{0,24},{2,26},{4,28},{6,30},{8,16},{10,18},{12,20},{14,22},{16,8},... | collective-permute-start | bytes 208904 | tf_op jit(solution)/shard_map/ppermute | solution.py:47
  6.0 4.9 %collective-permute-start.1 = (bf16[272,128]{1,0:T(8,128)(2,1)S(1)}, bf16[272,128]{1,0:T(8,128)(2,1)S(1)}, u32[]{:S(2)}, u32[]{:S(2)}) collective-permute-start(bf16[272,128]{1,0:T(8,128)(2,1)S(1)} %pack.1.refs_2_), channel_id=1, source_target_pairs={{0,8},{2,10},{4,12},{6,14},{8,0},{10,2},{12,4},{14,6},{16,24},{18,... | collective-permute-start | bytes 208904 | tf_op jit(solution)/shard_map/ppermute | solution.py:47
  6.0 6.5 %collective-permute-start = (bf16[272,128]{1,0:T(8,128)(2,1)S(1)}, bf16[272,128]{1,0:T(8,128)(2,1)S(1)}, u32[]{:S(2)}, u32[]{:S(2)}) collective-permute-start(bf16[272,128]{1,0:T(8,128)(2,1)S(1)} %pack.1.refs_2_), channel_id=1, source_target_pairs={{0,16},{2,18},{4,20},{6,22},{8,24},{10,26},{12,28},{14,30},{16,0},... | collective-permute-start | bytes 208904 | tf_op jit(solution)/shard_map/ppermute | solution.py:47
  6.7 8.3 %collective-permute-start.5 = (bf16[272,128]{1,0:T(8,128)(2,1)S(1)}, bf16[272,128]{1,0:T(8,128)(2,1)S(1)}, u32[]{:S(2)}, u32[]{:S(2)}) collective-permute-start(bf16[272,128]{1,0:T(8,128)(2,1)S(1)} %pack.1.refs_2_), channel_id=1, source_target_pairs={{0,4},{2,6},{4,0},{6,2},{8,12},{10,14},{12,8},{14,10},{16,20},{18,... | collective-permute-start | bytes 208904 | tf_op jit(solution)/shard_map/ppermute | solution.py:47
  8.3 10.1 %collective-permute-start.7 = (bf16[256,768]{1,0:T(8,128)(2,1)}, bf16[256,768]{1,0:T(8,128)(2,1)S(1)}, u32[]{:S(2)}, u32[]{:S(2)}) collective-permute-start(bf16[256,768]{1,0:T(8,128)(2,1)} %refs_0_.1), channel_id=1, source_target_pairs={{0,1},{1,0},{2,3},{3,2},{4,5},{5,4},{6,7},{7,6},{8,9},{9,8},{10,11... | collective-permute-start | bytes 1179656 | tf_op jit(solution)/shard_map/ppermute | solution.py:47
  9.8 5.3 %collective-permute-start.4 = (bf16[272,128]{1,0:T(8,128)(2,1)S(1)}, bf16[272,128]{1,0:T(8,128)(2,1)S(1)}, u32[]{:S(2)}, u32[]{:S(2)}) collective-permute-start(bf16[272,128]{1,0:T(8,128)(2,1)S(1)} %collective-permute-done.3.refs_4_), channel_id=1, source_target_pairs={{0,4},{2,6},{4,0},{6,2},{8,12},{10,14},{12,8},{14,10},{16,20},{18,... | collective-permute-start | bytes 208904 | tf_op jit(solution)/shard_map/ppermute | solution.py:47
  10.9 5.1 %collective-permute-start.2 = (bf16[272,128]{1,0:T(8,128)(2,1)S(1)}, bf16[272,128]{1,0:T(8,128)(2,1)S(1)}, u32[]{:S(2)}, u32[]{:S(2)}) collective-permute-start(bf16[272,128]{1,0:T(8,128)(2,1)S(1)} %collective-permute-done.1.refs_3_), channel_id=1, source_target_pairs={{0,4},{2,6},{4,0},{6,2},{8,12},{10,14},{12,8},{14,10},{16,20},{18,... | collective-permute-start | bytes 208904 | tf_op jit(solution)/shard_map/ppermute | solution.py:47
  12.6 4.3 %collective-permute-start.6 = (bf16[272,128]{1,0:T(8,128)(2,1)S(1)}, bf16[272,128]{1,0:T(8,128)(2,1)S(1)}, u32[]{:S(2)}, u32[]{:S(2)}) collective-permute-start(bf16[272,128]{1,0:T(8,128)(2,1)S(1)} %collective-permute-done.refs_5_), channel_id=1, source_target_pairs={{0,4},{2,6},{4,0},{6,2},{8,12},{10,14},{12,8},{14,10},{16,20},{18,... | collective-permute-start | bytes 208904 | tf_op jit(solution)/shard_map/ppermute | solution.py:47
  13.3 5.2 %copy-start = (bf16[256,768]{1,0:T(8,128)(2,1)S(1)}, bf16[256,768]{1,0:T(8,128)(2,1)}, u32[]{:S(2)}) copy-start(bf16[256,768]{1,0:T(8,128)(2,1)} %refs_0_.1) | copy-start | bytes 1179652
  15.0 1.9 %collective-permute-start.8 = (bf16[1088,128]{1,0:T(8,128)(2,1)S(1)}, bf16[1088,128]{1,0:T(8,128)(2,1)S(1)}, u32[]{:S(2)}, u32[]{:S(2)}) collective-permute-start(bf16[1088,128]{1,0:T(8,128)(2,1)S(1)} %pad_maximum_fusion.1), channel_id=1, source_target_pairs={{0,2},{2,0},{4,6},{6,4},{8,10},{10,8},{12,14},{14,12},{16,18},{18,... | collective-permute-start | bytes 835592 | tf_op jit(solution)/shard_map/ppermute | solution.py:47
  16.9 1.7 %copy-start.1 = (bf16[128,256]{1,0:T(8,128)(2,1)S(1)}, bf16[128,256]{1,0:T(8,128)(2,1)}, u32[]{:S(2)}) copy-start(bf16[128,256]{1,0:T(8,128)(2,1)} %restrict_ref.1) | copy-start | bytes 196612
  16.9 1.6 %collective-permute-start.9 = (bf16[1088,128]{1,0:T(8,128)(2,1)S(1)}, bf16[1088,128]{1,0:T(8,128)(2,1)S(1)}, u32[]{:S(2)}, u32[]{:S(2)}) collective-permute-start(bf16[1088,128]{1,0:T(8,128)(2,1)S(1)} %pad_maximum_fusion), channel_id=1, source_target_pairs={{0,2},{2,0},{4,6},{6,4},{8,10},{10,8},{12,14},{14,12},{16,18},{18,... | collective-permute-start | bytes 835592 | tf_op jit(solution)/shard_map/ppermute | solution.py:47

commit v6 on v5

--- a/solution.py
+++ b/solution.py
@@ -12,6 +12,8 @@
 DIGIT = 128
 LANES = 128
 EXTRA = 16
+GOAL_BITS = 8
+GOAL = 1 << GOAL_BITS
 SMALL = 8 * 1024 * 1024
 
 
@@ -51,7 +53,7 @@
     if size != 16:
         return [lax.all_gather(packed, "row", axis=0, tiled=True)], None, make(packed)
     got = {(0,): packed}
-    for mask in (4, 12, 8):
+    for mask in (8, 12, 4):
         got[(mask,)] = swap(packed, "row", size, mask)
     across = {}
     for group in ((12,), (0,), (4,), (8,)):
@@ -59,7 +61,7 @@
         across[tuple(mask | 2 for mask in group)] = swap(both, "row", size, 2)
     index = list(make(got[(8,)]))
     pieces = {**got, **across}
-    for half in (((12,), (4,), (8,), (0,)), ((6,), (14,), (2,), (10,))):
+    for half in (((0,), (8,), (4,), (12,)), ((6,), (14,), (2,), (10,))):
         both = jnp.concatenate([pieces[inside] for inside in half])
         if half[0] in across:
             both, index[1] = lax.optimization_barrier((both, index[1]))
@@ -68,7 +70,9 @@
     return list(pieces.values()), list(pieces), index
 
 
-def index_kernel(by_xor, slabs, cols, columns_ref, counts_ref, pattern_ref, start_ref, pick_ref, own_ref, *sums):
+def index_kernel(
+    by_xor, slabs, cols, columns_ref, counts_ref, pattern_ref, start_ref, pick_ref, own_ref, *sums
+):
     bricks, slots = columns_ref.shape
     share = slots // cols
     owned = pattern_ref.shape[1] // cols
@@ -120,13 +124,16 @@
         )
         + (pltpu.VMEM((owned + 1, BRICK, LANES), jnp.float32),) * (bricks * P_SLOTS),
         in_specs=[pl.BlockSpec(memory_space=pltpu.SMEM)] * 3,
-        out_specs=(pl.BlockSpec(memory_space=pltpu.SMEM),) + (pl.BlockSpec(memory_space=pltpu.VMEM),) * (2 + bricks * P_SLOTS),
+        out_specs=(pl.BlockSpec(memory_space=pltpu.SMEM),)
+        + (pl.BlockSpec(memory_space=pltpu.VMEM),) * (2 + bricks * P_SLOTS),
         compiler_params=pltpu.CompilerParams(vmem_limit_bytes=SMALL),
         name="index",
     )(fine_columns, fine_counts, coarse_pattern)
 
 
-def operator_kernel(slabs, masks, bricks, slots, owned, start_ref, pick_ref, own_ref, restrict_ref, *refs, cols):
+def operator_kernel(
+    slabs, masks, bricks, slots, owned, start_ref, pick_ref, own_ref, restrict_ref, *refs, cols
+):
     parts = len(masks) if masks else 1
     fines, refs = refs[:cols], refs[cols:]
     pieces, refs = refs[:parts], refs[parts:]
@@ -150,13 +157,13 @@
         preferred_element_type=jnp.float32,
     )
     own = own_ref[...]
-    slots_v = []
+    found = []
     offset = lax.broadcasted_iota(jnp.int32, own.shape, 0).astype(jnp.float32) - owned
     for q in range(P_SLOTS):
         coarse = reached[2 * q : 2 * q + 1, :] + DIGIT * reached[2 * q + 1 : 2 * q + 2, :]
         slot = owned + jnp.sum(jnp.where(own == coarse, offset, 0.0), axis=0, keepdims=True)
-        slots_v.append(slot.astype(jnp.int32))
-    goals = slots_v[0] + 256 * slots_v[1]
+        found.append(slot.astype(jnp.int32))
+    goals = found[0] + GOAL * found[1]
 
     source = pieces[0]
     if masks:
@@ -166,7 +173,6 @@
                 held_ref[slab * rows : (slab + 1) * rows, :] = piece[at * rows : (at + 1) * rows, :]
     left = lax.broadcasted_iota(jnp.int32, (BRICK, LANES), 1) < BRICK
     nothing = jnp.zeros((BRICK, LANES), jnp.bfloat16)
-
 
     for part in range(cols):
         for pair in range(share // 2):
@@ -177,7 +183,7 @@
                     start = pl.multiple_of(start_ref[0, at], 16)
                     blocks.append(source[pl.ds(start, BRICK), :])
                     goal = goals[0, at]
-                    where_to += [goal & 255, goal >> 8]
+                    where_to += [goal & (GOAL - 1), goal >> GOAL_BITS]
                 right = jnp.concatenate(
                     [
                         jnp.concatenate([blocks[0], nothing], axis=1),
@@ -189,29 +195,25 @@
                 product = jnp.dot(a, right, preferred_element_type=jnp.float32)
                 for half in range(2):
                     block = product[:, half * LANES : (half + 1) * LANES]
-                    sums[i*2+0+2*0][where_to[half * 2]] += block
-                    sums[i*2+1+2*0][where_to[half * 2 + 1]] += block
+                    for q in range(P_SLOTS):
+                        sums[i * P_SLOTS + q][where_to[half * P_SLOTS + q]] += block
 
     restrict = restrict_ref[...]
-    group = 2
-    width = group * BRICK
     leaving = []
-    for at in range(owned // group):
+    for at in range(owned // 2):
         high, low = [], []
         for i in range(bricks):
-            tops, rests = [], []
-            for even in range(at * group, (at + 1) * group, 2):
-                f0, f1, s0, s1 = sums[2*i][even], sums[2*i+1][even], sums[2*i][even + 1], sums[2*i+1][even+1]
-                total = jnp.where(left, f0, s1) + pltpu.roll(
-                    jnp.where(left, s0, f1), BRICK, 1
-                )
-                tops.append(total.astype(jnp.bfloat16))
-                rests.append((total - tops[-1].astype(jnp.float32)).astype(jnp.bfloat16))
-            high.append(jnp.concatenate(tops, axis=1))
-            low.append(jnp.concatenate(rests, axis=1))
+            even, odd = (
+                [sums[i * P_SLOTS + q][2 * at + side] for q in range(P_SLOTS)] for side in range(2)
+            )
+            total = jnp.where(left, even[0], odd[1]) + pltpu.roll(
+                jnp.where(left, odd[0], even[1]), BRICK, 1
+            )
+            high.append(total.astype(jnp.bfloat16))
+            low.append((total - high[-1].astype(jnp.float32)).astype(jnp.bfloat16))
         high = jnp.concatenate(high, axis=0)
         low = jnp.concatenate(low, axis=0)
-        here = pl.ds(at * width, width)
+        here = pl.ds(at * LANES, LANES)
         result_ref[:, here] = jnp.dot(restrict, high, preferred_element_type=jnp.float32) + jnp.dot(
             restrict, low, preferred_element_type=jnp.float32
         )

time: 21.2 us -> 21.2 us (level)
  no operation moved by 1% of the time
where the time goes in v6:
time: 21.2 us; the launch traced here: 21 us
  starting transfers between devices  12.2 us (58%)
  Pallas kernels  5.07 us (24%)
  waiting for transfers between devices  3.59 us (17%)
    ppermute x10, starting transfers between devices, swap(): return lax.ppermute(block, axis, [(i, i ^ mask) for i in range(size)])  12.2 us
    ppermute x10, waiting for transfers between devices, swap(): return lax.ppermute(block, axis, [(i, i ^ mask) for i in range(size)])  3.59 us
    pallas_call x1, Pallas kernels, operate(): pl.pallas_call(functools.partial(operator_kernel, slabs, masks, bricks, s...  2.52 us
    pallas_call x1, Pallas kernels, make_index(): pl.pallas_call(functools.partial(index_kernel, by_xor, slabs, cols), out_...  1.67 us
    pallas_call x1, Pallas kernels, pack(): pl.pallas_call(pack_kernel, out_shape=pltpu.VMEM((prolong.shape[0] + EXTR...  0.88 us
  transfers between devices with their start and end apart: 10, of which 5 were waited for; matrix products, arithmetic and copies ran while one was open for 0% of the time, Pallas kernels for 8%

profile of v6, /device:TPU:0, one launch (start us, length us, event | category | flops | bytes accessed | tf_op | source)
XLA Modules:
  0.0 21.0 jit_solution(12143521237551826164)
XLA Ops:
  0.0 0.9 %pack.1.refs_2_ = bf16[272,128]{1,0:T(8,128)(2,1)S(1)} custom-call(s32[2,4]{1,0:T(2,128)} %bitcast.1, bf16[256,128]{1,0:T(8,128)(2,1)} %prolong_ref.1), custom_call_target="tpu_custom_call" | custom-call | tf_op jit(solution)/shard_map/pack/pallas_call | solution.py:36
  0.9 0.0 copy-start.2
  0.9 0.0 copy-start.3
  0.9 0.0 copy-start.4
  0.9 5.1 %collective-permute-start.3 = (bf16[272,128]{1,0:T(8,128)(2,1)S(1)}, bf16[272,128]{1,0:T(8,128)(2,1)S(1)}, u32[]{:S(2)}, u32[]{:S(2)}) collective-permute-start(bf16[272,128]{1,0:T(8,128)(2,1)S(1)} %pack.1.refs_2_), channel_id=1, source_target_pairs={{0,24},{2,26},{4,28},{6,30},{8,16},{10,18},{12,20},{14,22},{16,8},... | collective-permute-start | bytes 208904 | tf_op jit(solution)/shard_map/ppermute | solution.py:49
  6.0 0.0 collective-permute-start.1
  6.0 0.6 %collective-permute-start = (bf16[272,128]{1,0:T(8,128)(2,1)S(1)}, bf16[272,128]{1,0:T(8,128)(2,1)S(1)}, u32[]{:S(2)}, u32[]{:S(2)}) collective-permute-start(bf16[272,128]{1,0:T(8,128)(2,1)S(1)} %pack.1.refs_2_), channel_id=1, source_target_pairs={{0,16},{2,18},{4,20},{6,22},{8,24},{10,26},{12,28},{14,30},{16,0},... | collective-permute-start | bytes 208904 | tf_op jit(solution)/shard_map/ppermute | solution.py:49
  6.7 1.7 %collective-permute-start.5 = (bf16[272,128]{1,0:T(8,128)(2,1)S(1)}, bf16[272,128]{1,0:T(8,128)(2,1)S(1)}, u32[]{:S(2)}, u32[]{:S(2)}) collective-permute-start(bf16[272,128]{1,0:T(8,128)(2,1)S(1)} %pack.1.refs_2_), channel_id=1, source_target_pairs={{0,4},{2,6},{4,0},{6,2},{8,12},{10,14},{12,8},{14,10},{16,20},{18,... | collective-permute-start | bytes 208904 | tf_op jit(solution)/shard_map/ppermute | solution.py:49
  8.3 1.5 %collective-permute-start.7 = (bf16[256,768]{1,0:T(8,128)(2,1)}, bf16[256,768]{1,0:T(8,128)(2,1)S(1)}, u32[]{:S(2)}, u32[]{:S(2)}) collective-permute-start(bf16[256,768]{1,0:T(8,128)(2,1)} %refs_0_.1), channel_id=1, source_target_pairs={{0,1},{1,0},{2,3},{3,2},{4,5},{5,4},{6,7},{7,6},{8,9},{9,8},{10,11... | collective-permute-start | bytes 1179656 | tf_op jit(solution)/shard_map/ppermute | solution.py:49
  9.8 0.0 collective-permute-done.3.refs_4_
  9.8 0.8 %collective-permute-start.4 = (bf16[272,128]{1,0:T(8,128)(2,1)S(1)}, bf16[272,128]{1,0:T(8,128)(2,1)S(1)}, u32[]{:S(2)}, u32[]{:S(2)}) collective-permute-start(bf16[272,128]{1,0:T(8,128)(2,1)S(1)} %collective-permute-done.3.refs_4_), channel_id=1, source_target_pairs={{0,4},{2,6},{4,0},{6,2},{8,12},{10,14},{12,8},{14,10},{16,20},{18,... | collective-permute-start | bytes 208904 | tf_op jit(solution)/shard_map/ppermute | solution.py:49
  10.6 0.3 %collective-permute-done.1.refs_5_ = bf16[272,128]{1,0:T(8,128)(2,1)S(1)} collective-permute-done((bf16[272,128]{1,0:T(8,128)(2,1)S(1)}, bf16[272,128]{1,0:T(8,128)(2,1)S(1)}, u32[]{:S(2)}, u32[]{:S(2)}) %collective-permute-start.1) | collective-permute-done | bytes 69664 | tf_op jit(solution)/shard_map/ppermute | solution.py:49
  10.9 1.7 %collective-permute-start.2 = (bf16[272,128]{1,0:T(8,128)(2,1)S(1)}, bf16[272,128]{1,0:T(8,128)(2,1)S(1)}, u32[]{:S(2)}, u32[]{:S(2)}) collective-permute-start(bf16[272,128]{1,0:T(8,128)(2,1)S(1)} %collective-permute-done.1.refs_5_), channel_id=1, source_target_pairs={{0,4},{2,6},{4,0},{6,2},{8,12},{10,14},{12,8},{14,10},{16,20},{18,... | collective-permute-start | bytes 208904 | tf_op jit(solution)/shard_map/ppermute | solution.py:49
  12.5 0.0 collective-permute-done.refs_3_
  12.6 0.7 %collective-permute-start.6 = (bf16[272,128]{1,0:T(8,128)(2,1)S(1)}, bf16[272,128]{1,0:T(8,128)(2,1)S(1)}, u32[]{:S(2)}, u32[]{:S(2)}) collective-permute-start(bf16[272,128]{1,0:T(8,128)(2,1)S(1)} %collective-permute-done.refs_3_), channel_id=1, source_target_pairs={{0,4},{2,6},{4,0},{6,2},{8,12},{10,14},{12,8},{14,10},{16,20},{18,... | collective-permute-start | bytes 208904 | tf_op jit(solution)/shard_map/ppermute | solution.py:49
  13.3 0.0 copy-done.2
  13.3 0.0 copy-done.3
  13.3 0.0 copy-done.4
  13.3 0.0 copy-start
  13.3 1.7 %index.1 = (s32[1,96]{1,0:T(1,128)S(4)}, bf16[128,128]{1,0:T(8,128)(2,1)S(1)}, f32[24,128]{1,0:T(8,128)S(1)}, f32[25,64,128]{2,1,0:T(8,128)S(1)}, f32[25,64,128]...) custom-call(s32[4,24]{1,0:T(4,128)S(1)} %copy-done.2, ...), custom_call_target="tpu_custom_call" | custom-call | tf_op jit(solution)/shard_map/index/pallas_call | solution.py:118
  15.0 0.0 collective-permute-done.5.refs_7_
  15.0 0.1 collective-permute-start.8
  15.1 0.0 collective-permute-done.4.refs_6_
  15.1 0.9 %collective-permute-done.2.refs_8_ = bf16[272,128]{1,0:T(8,128)(2,1)S(1)} collective-permute-done((bf16[272,128]{1,0:T(8,128)(2,1)S(1)}, bf16[272,128]{1,0:T(8,128)(2,1)S(1)}, u32[]{:S(2)}, u32[]{:S(2)}) %collective-permute-start.2) | collective-permute-done | bytes 69664 | tf_op jit(solution)/shard_map/ppermute | solution.py:49
  16.0 0.9 %collective-permute-done.6.refs_9_ = bf16[272,128]{1,0:T(8,128)(2,1)S(1)} collective-permute-done((bf16[272,128]{1,0:T(8,128)(2,1)S(1)}, bf16[272,128]{1,0:T(8,128)(2,1)S(1)}, u32[]{:S(2)}, u32[]{:S(2)}) %collective-permute-start.6) | collective-permute-done | bytes 69664 | tf_op jit(solution)/shard_map/ppermute | solution.py:49
  16.9 0.0 copy-start.1
  16.9 0.1 collective-permute-start.9
  17.0 0.0 collective-permute-done.8.refs_10_
  17.0 1.4 %collective-permute-done.7.refs_1_ = bf16[256,768]{1,0:T(8,128)(2,1)S(1)} collective-permute-done((bf16[256,768]{1,0:T(8,128)(2,1)}, bf16[256,768]{1,0:T(8,128)(2,1)S(1)}, u32[]{:S(2)}, u32[]{:S(2)}) %collective-permute-start.7) | collective-permute-done | bytes 393248 | tf_op jit(solution)/shard_map/ppermute | solution.py:49
  18.4 0.1 collective-permute-done.9.refs_11_
  18.5 0.0 copy-done
  18.5 0.0 copy-done.1
  18.5 2.5 %operator.1 = (f32[128,1536]{1,0:T(8,128)}, f32[25,64,128]{2,1,0:T(8,128)S(1)}, f32[25,64,128]{2,1,0:T(8,128)S(1)}, f32[25,64,128]{2,1,0:T(8,128)S(1)}, f32[25,6...) custom-call(s32[1,96]{1,0:T(1,128)S(4)} %get-tuple-element.21.start_, ...), custom_call_target="tpu_custom_call", output_to_operand_aliasing={{1}: (16, {}), {2}: (17, {}), {3}: (18, {}), {4}: (19, {}),... | custom-call | tf_op jit(solution)/shard_map/operator/pallas_call | solution.py:236
  (2 shorter events, 0.0 us)
Async XLA Ops:
  0.9 12.4 %copy-start.2 = (s32[4,24]{1,0:T(4,128)S(1)}, s32[4,24]{1,0:T(4,128)}, u32[]{:S(2)}) copy-start(s32[4,24]{1,0:T(4,128)} %columns_ref) | copy-start | bytes 1156
  0.9 12.4 %copy-start.3 = (s32[4]{0:T(128)S(1)}, s32[4]{0:T(128)}, u32[]{:S(2)}) copy-start(s32[4]{0:T(128)} %counts_ref.1) | copy-start | bytes 52
  0.9 12.4 %copy-start.4 = (s32[1,48]{1,0:T(1,128)S(1)}, s32[1,48]{1,0:T(1,128)}, u32[]{:S(2)}) copy-start(s32[1,48]{1,0:T(1,128)} %pattern_ref.1) | copy-start | bytes 580
  0.9 8.9 %collective-permute-start.3 = (bf16[272,128]{1,0:T(8,128)(2,1)S(1)}, bf16[272,128]{1,0:T(8,128)(2,1)S(1)}, u32[]{:S(2)}, u32[]{:S(2)}) collective-permute-start(bf16[272,128]{1,0:T(8,128)(2,1)S(1)} %pack.1.refs_2_), channel_id=1, source_target_pairs={{0,24},{2,26},{4,28},{6,30},{8,16},{10,18},{12,20},{14,22},{16,8},... | collective-permute-start | bytes 208904 | tf_op jit(solution)/shard_map/ppermute | solution.py:49
  6.0 4.9 %collective-permute-start.1 = (bf16[272,128]{1,0:T(8,128)(2,1)S(1)}, bf16[272,128]{1,0:T(8,128)(2,1)S(1)}, u32[]{:S(2)}, u32[]{:S(2)}) collective-permute-start(bf16[272,128]{1,0:T(8,128)(2,1)S(1)} %pack.1.refs_2_), channel_id=1, source_target_pairs={{0,8},{2,10},{4,12},{6,14},{8,0},{10,2},{12,4},{14,6},{16,24},{18,... | collective-permute-start | bytes 208904 | tf_op jit(solution)/shard_map/ppermute | solution.py:49
  6.0 6.5 %collective-permute-start = (bf16[272,128]{1,0:T(8,128)(2,1)S(1)}, bf16[272,128]{1,0:T(8,128)(2,1)S(1)}, u32[]{:S(2)}, u32[]{:S(2)}) collective-permute-start(bf16[272,128]{1,0:T(8,128)(2,1)S(1)} %pack.1.refs_2_), channel_id=1, source_target_pairs={{0,16},{2,18},{4,20},{6,22},{8,24},{10,26},{12,28},{14,30},{16,0},... | collective-permute-start | bytes 208904 | tf_op jit(solution)/shard_map/ppermute | solution.py:49
  6.7 8.3 %collective-permute-start.5 = (bf16[272,128]{1,0:T(8,128)(2,1)S(1)}, bf16[272,128]{1,0:T(8,128)(2,1)S(1)}, u32[]{:S(2)}, u32[]{:S(2)}) collective-permute-start(bf16[272,128]{1,0:T(8,128)(2,1)S(1)} %pack.1.refs_2_), channel_id=1, source_target_pairs={{0,4},{2,6},{4,0},{6,2},{8,12},{10,14},{12,8},{14,10},{16,20},{18,... | collective-permute-start | bytes 208904 | tf_op jit(solution)/shard_map/ppermute | solution.py:49
  8.3 10.1 %collective-permute-start.7 = (bf16[256,768]{1,0:T(8,128)(2,1)}, bf16[256,768]{1,0:T(8,128)(2,1)S(1)}, u32[]{:S(2)}, u32[]{:S(2)}) collective-permute-start(bf16[256,768]{1,0:T(8,128)(2,1)} %refs_0_.1), channel_id=1, source_target_pairs={{0,1},{1,0},{2,3},{3,2},{4,5},{5,4},{6,7},{7,6},{8,9},{9,8},{10,11... | collective-permute-start | bytes 1179656 | tf_op jit(solution)/shard_map/ppermute | solution.py:49
  9.8 5.3 %collective-permute-start.4 = (bf16[272,128]{1,0:T(8,128)(2,1)S(1)}, bf16[272,128]{1,0:T(8,128)(2,1)S(1)}, u32[]{:S(2)}, u32[]{:S(2)}) collective-permute-start(bf16[272,128]{1,0:T(8,128)(2,1)S(1)} %collective-permute-done.3.refs_4_), channel_id=1, source_target_pairs={{0,4},{2,6},{4,0},{6,2},{8,12},{10,14},{12,8},{14,10},{16,20},{18,... | collective-permute-start | bytes 208904 | tf_op jit(solution)/shard_map/ppermute | solution.py:49
  10.9 5.1 %collective-permute-start.2 = (bf16[272,128]{1,0:T(8,128)(2,1)S(1)}, bf16[272,128]{1,0:T(8,128)(2,1)S(1)}, u32[]{:S(2)}, u32[]{:S(2)}) collective-permute-start(bf16[272,128]{1,0:T(8,128)(2,1)S(1)} %collective-permute-done.1.refs_5_), channel_id=1, source_target_pairs={{0,4},{2,6},{4,0},{6,2},{8,12},{10,14},{12,8},{14,10},{16,20},{18,... | collective-permute-start | bytes 208904 | tf_op jit(solution)/shard_map/ppermute | solution.py:49
  12.6 4.3 %collective-permute-start.6 = (bf16[272,128]{1,0:T(8,128)(2,1)S(1)}, bf16[272,128]{1,0:T(8,128)(2,1)S(1)}, u32[]{:S(2)}, u32[]{:S(2)}) collective-permute-start(bf16[272,128]{1,0:T(8,128)(2,1)S(1)} %collective-permute-done.refs_3_), channel_id=1, source_target_pairs={{0,4},{2,6},{4,0},{6,2},{8,12},{10,14},{12,8},{14,10},{16,20},{18,... | collective-permute-start | bytes 208904 | tf_op jit(solution)/shard_map/ppermute | solution.py:49
  13.3 5.2 %copy-start = (bf16[256,768]{1,0:T(8,128)(2,1)S(1)}, bf16[256,768]{1,0:T(8,128)(2,1)}, u32[]{:S(2)}) copy-start(bf16[256,768]{1,0:T(8,128)(2,1)} %refs_0_.1) | copy-start | bytes 1179652
  15.0 1.9 %collective-permute-start.8 = (bf16[1088,128]{1,0:T(8,128)(2,1)S(1)}, bf16[1088,128]{1,0:T(8,128)(2,1)S(1)}, u32[]{:S(2)}, u32[]{:S(2)}) collective-permute-start(bf16[1088,128]{1,0:T(8,128)(2,1)S(1)} %pad_maximum_fusion.1), channel_id=1, source_target_pairs={{0,2},{2,0},{4,6},{6,4},{8,10},{10,8},{12,14},{14,12},{16,18},{18,... | collective-permute-start | bytes 835592 | tf_op jit(solution)/shard_map/ppermute | solution.py:49
  16.9 1.7 %copy-start.1 = (bf16[128,256]{1,0:T(8,128)(2,1)S(1)}, bf16[128,256]{1,0:T(8,128)(2,1)}, u32[]{:S(2)}) copy-start(bf16[128,256]{1,0:T(8,128)(2,1)} %restrict_ref.1) | copy-start | bytes 196612
  16.9 1.6 %collective-permute-start.9 = (bf16[1088,128]{1,0:T(8,128)(2,1)S(1)}, bf16[1088,128]{1,0:T(8,128)(2,1)S(1)}, u32[]{:S(2)}, u32[]{:S(2)}) collective-permute-start(bf16[1088,128]{1,0:T(8,128)(2,1)S(1)} %pad_maximum_fusion), channel_id=1, source_target_pairs={{0,2},{2,0},{4,6},{6,4},{8,10},{10,8},{12,14},{14,12},{16,18},{18,... | collective-permute-start | bytes 835592 | tf_op jit(solution)/shard_map/ppermute | solution.py:49

commit v7 on v6

--- a/solution.py
+++ b/solution.py
@@ -15,6 +15,8 @@
 GOAL_BITS = 8
 GOAL = 1 << GOAL_BITS
 SMALL = 8 * 1024 * 1024
+LIMIT = 32 * 1024 * 1024
+LATE = 1
 
 
 def pack_kernel(columns_ref, prolong_ref, packed_ref):
@@ -128,29 +130,64 @@
         + (pl.BlockSpec(memory_space=pltpu.VMEM),) * (2 + bricks * P_SLOTS),
         compiler_params=pltpu.CompilerParams(vmem_limit_bytes=SMALL),
         name="index",
-    )(fine_columns, fine_counts, coarse_pattern)
+    )(*(pltpu.with_memory_space_constraint(each, pltpu.HBM) for each in (fine_columns, fine_counts, coarse_pattern)))
+
+
+def take_in(piece, inside, bricks, table, held_ref):
+    rows = bricks * BRICK + EXTRA
+    for at, slab in enumerate(inside):
+        block = piece[at * rows : (at + 1) * rows, :]
+        if held_ref is not None:
+            held_ref[slab * rows : (slab + 1) * rows, :] = block
+        digits = block[bricks * BRICK :, :].astype(jnp.float32)
+        tile, shift = slab * bricks // LANES, slab * bricks % LANES
+        table[tile] += pltpu.roll(digits, shift, 1) if shift else digits
+
+
+def prep_kernel(masks, bricks, *refs):
+    pieces, (held_ref, table_ref) = refs[:-2], refs[-2:]
+    table = [jnp.zeros((EXTRA, LANES), jnp.float32)]
+    for piece, inside in zip(pieces, masks):
+        take_in(piece, inside, bricks, table, held_ref)
+    table_ref[...] = table[0]
+
+
+def make_prep(slabs, bricks, pieces, masks):
+    vmem = pl.BlockSpec(memory_space=pltpu.VMEM)
+    return pl.pallas_call(
+        functools.partial(prep_kernel, masks, bricks),
+        out_shape=[
+            pltpu.VMEM((slabs * (bricks * BRICK + EXTRA), LANES), jnp.bfloat16),
+            pltpu.VMEM((EXTRA, LANES), jnp.float32),
+        ],
+        in_specs=[vmem] * len(pieces),
+        out_specs=[vmem] * 2,
+        compiler_params=pltpu.CompilerParams(vmem_limit_bytes=LIMIT),
+        name="prep",
+    )(*pieces)
 
 
 def operator_kernel(
     slabs, masks, bricks, slots, owned, start_ref, pick_ref, own_ref, restrict_ref, *refs, cols
 ):
-    parts = len(masks) if masks else 1
+    late = len(masks) if masks else 1
     fines, refs = refs[:cols], refs[cols:]
-    pieces, refs = refs[:parts], refs[parts:]
-    refs = refs[bricks * P_SLOTS :]
-    out_ref, refs = refs[0], refs[1:]
-    sums, refs = refs[: bricks * P_SLOTS], refs[bricks * P_SLOTS :]
-    held_ref, result_ref, out_sem = refs
+    given, refs = refs[:late], refs[late:]
+    kept = bricks * P_SLOTS
     share = slots // cols
-    rows = bricks * BRICK + EXTRA
-
-    table = [jnp.zeros((EXTRA, LANES), jnp.float32) for _ in range(pick_ref.shape[0] // LANES)]
-    for piece, inside in zip(pieces, masks if masks else [range(slabs)]):
-        for at, slab in enumerate(inside):
-            first = at * rows + bricks * BRICK
-            digits = piece[first : first + EXTRA, :].astype(jnp.float32)
-            tile, shift = slab * bricks // LANES, slab * bricks % LANES
-            table[tile] += pltpu.roll(digits, shift, 1) if shift else digits
+    if masks:
+        table_ref, refs = refs[0], refs[2 + kept :]
+        out_ref, source, *refs = refs
+        table = [table_ref[...]]
+        for piece, inside in zip(given, masks):
+            take_in(piece, inside, bricks, table, source)
+    else:
+        out_ref, *refs = refs[kept:]
+        source = given[0]
+        table = [jnp.zeros((EXTRA, LANES), jnp.float32) for _ in range(pick_ref.shape[0] // LANES)]
+        take_in(source, range(slabs), bricks, table, None)
+    sums, (result_ref, out_sem) = refs[:kept], refs[kept:]
+
     reached = jnp.dot(
         jnp.concatenate(table, axis=1).astype(jnp.bfloat16),
         pick_ref[...],
@@ -165,12 +202,6 @@
         found.append(slot.astype(jnp.int32))
     goals = found[0] + GOAL * found[1]
 
-    source = pieces[0]
-    if masks:
-        source = held_ref
-        for piece, inside in zip(pieces, masks):
-            for at, slab in enumerate(inside):
-                held_ref[slab * rows : (slab + 1) * rows, :] = piece[at * rows : (at + 1) * rows, :]
     left = lax.broadcasted_iota(jnp.int32, (BRICK, LANES), 1) < BRICK
     nothing = jnp.zeros((BRICK, LANES), jnp.bfloat16)
 
@@ -225,29 +256,32 @@
 
 
 def operate(slabs, cols, bricks, slots, owned, index, restrict_rows, fines, pieces, masks):
-    rows = bricks * BRICK + EXTRA
     vmem = pl.BlockSpec(memory_space=pltpu.VMEM)
     smem = pl.BlockSpec(memory_space=pltpu.SMEM)
-    held_rows = slabs * rows if masks else 16
     shape = (restrict_rows.shape[0], owned * BRICK)
-    starts, pick, own, *sums = index
+    starts, pick, own, *kept = index
     starts = pltpu.with_memory_space_constraint(starts, pltpu.SMEM)
-    given = (starts, pick, own, restrict_rows, *fines, *pieces)
+    given = [starts, pick, own, restrict_rows, *fines, *pieces[-LATE:]]
+    if masks:
+        held, table = make_prep(slabs, bricks, pieces[:-LATE], masks[:-LATE])
+        given.append(table)
+        kept = [held] + kept
     return pl.pallas_call(
-        functools.partial(operator_kernel, slabs, masks, bricks, slots, owned, cols=cols),
+        functools.partial(
+            operator_kernel, slabs, masks[-LATE:] if masks else None, bricks, slots, owned, cols=cols
+        ),
         out_shape=[jax.ShapeDtypeStruct(shape, jnp.float32)]
-        + [pltpu.VMEM(each.shape, jnp.float32) for each in sums],
-        in_specs=[smem] + [vmem] * (len(given) - 1 + len(sums)),
-        out_specs=[pl.BlockSpec(memory_space=pl.ANY)] + [vmem] * len(sums),
-        input_output_aliases={len(given) + at: 1 + at for at in range(len(sums))},
+        + [pltpu.VMEM(each.shape, each.dtype) for each in kept],
+        in_specs=[smem] + [vmem] * (len(given) - 1 + len(kept)),
+        out_specs=[pl.BlockSpec(memory_space=pl.ANY)] + [vmem] * len(kept),
+        input_output_aliases={len(given) + at: 1 + at for at in range(len(kept))},
         scratch_shapes=[
-            pltpu.VMEM((held_rows, LANES), jnp.bfloat16),
             pltpu.VMEM(shape, jnp.float32),
             pltpu.SemaphoreType.DMA((owned // 2,)),
         ],
-        compiler_params=pltpu.CompilerParams(vmem_limit_bytes=32 * 1024 * 1024),
+        compiler_params=pltpu.CompilerParams(vmem_limit_bytes=LIMIT),
         name="operator",
-    )(*given, *sums)[0]
+    )(*given, *kept)[0]
 
 
 def local(

time: 21.2 us -> 21.2 us (level)
  Pallas kernels: 5.07 us -> 5.4 us
  waiting for transfers between devices: 3.59 us -> 3.37 us
    ppermute x10, waiting for transfers between devices: 3.59 us -> 3.37 us  [swap(): return lax.ppermute(block, axis, [(i, i ^ mask) for i in range(size)])]
    pallas_call x1 -> x2, Pallas kernels: 2.52 us -> 2.67 us  [the longest x1 2.54 us: operate(): pl.pallas_call(functools.partial(operator_kernel, slabs, masks[-LATE:] if...]
  transfers between devices with their start and end apart: 10 -> 10, of which waited for: 5 -> 5; matrix products, arithmetic and copies ran while one was open for 0% -> 0% of each run, Pallas kernels for 8% -> 9%
where the time goes in v7:
time: 21.2 us; the launch traced here: 21.1 us
  starting transfers between devices  12.2 us (58%)
  Pallas kernels  5.4 us (25%)
  waiting for transfers between devices  3.37 us (16%)
    ppermute x10, starting transfers between devices, swap(): return lax.ppermute(block, axis, [(i, i ^ mask) for i in range(size)])  12.2 us
    ppermute x10, waiting for transfers between devices, swap(): return lax.ppermute(block, axis, [(i, i ^ mask) for i in range(size)])  3.37 us
    pallas_call x1, Pallas kernels, operate(): pl.pallas_call(functools.partial(operator_kernel, slabs, masks[-LATE:] if...  2.54 us
    pallas_call x1, Pallas kernels, make_index(): pl.pallas_call(functools.partial(index_kernel, by_xor, slabs, cols), out_...  1.8 us
    pallas_call x1, Pallas kernels, pack(): pl.pallas_call(pack_kernel, out_shape=pltpu.VMEM((prolong.shape[0] + EXTR...  0.93 us
  transfers between devices with their start and end apart: 10, of which 5 were waited for; matrix products, arithmetic and copies ran while one was open for 0% of the time, Pallas kernels for 9%

profile of v7, /device:TPU:0, one launch (start us, length us, event | category | flops | bytes accessed | tf_op | source)
XLA Modules:
  0.0 21.1 jit_solution(6345832712104906221)
XLA Ops:
  0.0 0.0 copy-start
  0.0 0.0 copy-start.1
  0.0 0.9 %pack.1.refs_0_ = bf16[272,128]{1,0:T(8,128)(2,1)S(1)} custom-call(s32[2,4]{1,0:T(2,128)} %bitcast.1, bf16[256,128]{1,0:T(8,128)(2,1)} %prolong_ref.1), custom_call_target="tpu_custom_call" | custom-call | tf_op jit(solution)/shard_map/pack/pallas_call | solution.py:38
  0.9 5.1 %collective-permute-start.3 = (bf16[272,128]{1,0:T(8,128)(2,1)S(1)}, bf16[272,128]{1,0:T(8,128)(2,1)S(1)}, u32[]{:S(2)}, u32[]{:S(2)}) collective-permute-start(bf16[272,128]{1,0:T(8,128)(2,1)S(1)} %pack.1.refs_0_), channel_id=1, source_target_pairs={{0,24},{2,26},{4,28},{6,30},{8,16},{10,18},{12,20},{14,22},{16,8},... | collective-permute-start | bytes 208904 | tf_op jit(solution)/shard_map/ppermute | solution.py:51
  6.1 0.0 collective-permute-start.1
  6.1 0.6 %collective-permute-start = (bf16[272,128]{1,0:T(8,128)(2,1)S(1)}, bf16[272,128]{1,0:T(8,128)(2,1)S(1)}, u32[]{:S(2)}, u32[]{:S(2)}) collective-permute-start(bf16[272,128]{1,0:T(8,128)(2,1)S(1)} %pack.1.refs_0_), channel_id=1, source_target_pairs={{0,16},{2,18},{4,20},{6,22},{8,24},{10,26},{12,28},{14,30},{16,0},... | collective-permute-start | bytes 208904 | tf_op jit(solution)/shard_map/ppermute | solution.py:51
  6.7 1.7 %collective-permute-start.5 = (bf16[272,128]{1,0:T(8,128)(2,1)S(1)}, bf16[272,128]{1,0:T(8,128)(2,1)S(1)}, u32[]{:S(2)}, u32[]{:S(2)}) collective-permute-start(bf16[272,128]{1,0:T(8,128)(2,1)S(1)} %pack.1.refs_0_), channel_id=1, source_target_pairs={{0,4},{2,6},{4,0},{6,2},{8,12},{10,14},{12,8},{14,10},{16,20},{18,... | collective-permute-start | bytes 208904 | tf_op jit(solution)/shard_map/ppermute | solution.py:51
  8.4 1.5 %collective-permute-start.7 = (bf16[256,768]{1,0:T(8,128)(2,1)}, bf16[256,768]{1,0:T(8,128)(2,1)S(1)}, u32[]{:S(2)}, u32[]{:S(2)}) collective-permute-start(bf16[256,768]{1,0:T(8,128)(2,1)} %refs_0_.1), channel_id=1, source_target_pairs={{0,1},{1,0},{2,3},{3,2},{4,5},{5,4},{6,7},{7,6},{8,9},{9,8},{10,11... | collective-permute-start | bytes 1179656 | tf_op jit(solution)/shard_map/ppermute | solution.py:51
  9.9 0.0 collective-permute-done.3.refs_2_
  9.9 0.8 %collective-permute-start.4 = (bf16[272,128]{1,0:T(8,128)(2,1)S(1)}, bf16[272,128]{1,0:T(8,128)(2,1)S(1)}, u32[]{:S(2)}, u32[]{:S(2)}) collective-permute-start(bf16[272,128]{1,0:T(8,128)(2,1)S(1)} %collective-permute-done.3.refs_2_), channel_id=1, source_target_pairs={{0,4},{2,6},{4,0},{6,2},{8,12},{10,14},{12,8},{14,10},{16,20},{18,... | collective-permute-start | bytes 208904 | tf_op jit(solution)/shard_map/ppermute | solution.py:51
  10.6 0.3 %collective-permute-done.1.refs_3_ = bf16[272,128]{1,0:T(8,128)(2,1)S(1)} collective-permute-done((bf16[272,128]{1,0:T(8,128)(2,1)S(1)}, bf16[272,128]{1,0:T(8,128)(2,1)S(1)}, u32[]{:S(2)}, u32[]{:S(2)}) %collective-permute-start.1) | collective-permute-done | bytes 69664 | tf_op jit(solution)/shard_map/ppermute | solution.py:51
  10.9 1.7 %collective-permute-start.2 = (bf16[272,128]{1,0:T(8,128)(2,1)S(1)}, bf16[272,128]{1,0:T(8,128)(2,1)S(1)}, u32[]{:S(2)}, u32[]{:S(2)}) collective-permute-start(bf16[272,128]{1,0:T(8,128)(2,1)S(1)} %collective-permute-done.1.refs_3_), channel_id=1, source_target_pairs={{0,4},{2,6},{4,0},{6,2},{8,12},{10,14},{12,8},{14,10},{16,20},{18,... | collective-permute-start | bytes 208904 | tf_op jit(solution)/shard_map/ppermute | solution.py:51
  12.6 0.0 collective-permute-done.refs_1_
  12.6 0.7 %collective-permute-start.6 = (bf16[272,128]{1,0:T(8,128)(2,1)S(1)}, bf16[272,128]{1,0:T(8,128)(2,1)S(1)}, u32[]{:S(2)}, u32[]{:S(2)}) collective-permute-start(bf16[272,128]{1,0:T(8,128)(2,1)S(1)} %collective-permute-done.refs_1_), channel_id=1, source_target_pairs={{0,4},{2,6},{4,0},{6,2},{8,12},{10,14},{12,8},{14,10},{16,20},{18,... | collective-permute-start | bytes 208904 | tf_op jit(solution)/shard_map/ppermute | solution.py:51
  13.3 1.8 %index.1 = (s32[1,96]{1,0:T(1,128)S(4)}, bf16[128,128]{1,0:T(8,128)(2,1)S(1)}, f32[24,128]{1,0:T(8,128)S(1)}, f32[25,64,128]{2,1,0:T(8,128)S(1)}, f32[25,64,128]...) custom-call(s32[4,24]{1,0:T(4,128)} %columns_ref, ...), custom_call_target="tpu_custom_call" | custom-call | tf_op jit(solution)/shard_map/index/pallas_call | solution.py:120
  15.1 0.0 collective-permute-done.5.refs_5_
  15.1 0.1 collective-permute-start.9
  15.2 0.0 collective-permute-done.4.refs_4_
  15.2 0.8 %collective-permute-done.2.refs_6_ = bf16[272,128]{1,0:T(8,128)(2,1)S(1)} collective-permute-done((bf16[272,128]{1,0:T(8,128)(2,1)S(1)}, bf16[272,128]{1,0:T(8,128)(2,1)S(1)}, u32[]{:S(2)}, u32[]{:S(2)}) %collective-permute-start.2) | collective-permute-done | bytes 69664 | tf_op jit(solution)/shard_map/ppermute | solution.py:51
  16.0 0.9 %collective-permute-done.6.refs_7_ = bf16[272,128]{1,0:T(8,128)(2,1)S(1)} collective-permute-done((bf16[272,128]{1,0:T(8,128)(2,1)S(1)}, bf16[272,128]{1,0:T(8,128)(2,1)S(1)}, u32[]{:S(2)}, u32[]{:S(2)}) %collective-permute-start.6) | collective-permute-done | bytes 69664 | tf_op jit(solution)/shard_map/ppermute | solution.py:51
  16.9 0.1 collective-permute-start.8
  17.0 0.0 collective-permute-done.9.refs_8_
  17.0 0.1 prep.1
  17.1 1.3 %collective-permute-done.7.refs_1_ = bf16[256,768]{1,0:T(8,128)(2,1)S(1)} collective-permute-done((bf16[256,768]{1,0:T(8,128)(2,1)}, bf16[256,768]{1,0:T(8,128)(2,1)S(1)}, u32[]{:S(2)}, u32[]{:S(2)}) %collective-permute-start.7) | collective-permute-done | bytes 393248 | tf_op jit(solution)/shard_map/ppermute | solution.py:51
  18.4 0.1 collective-permute-done.8.refs_2_
  18.5 0.0 copy-done
  18.5 0.0 copy-done.1
  18.5 2.5 %operator.1 = (f32[128,1536]{1,0:T(8,128)}, bf16[4352,128]{1,0:T(8,128)(2,1)S(1)}, f32[25,64,128]{2,1,0:T(8,128)S(1)}, f32[25,64,128]{2,1,0:T(8,128)S(1)}, f32[2...) custom-call(s32[1,96]{1,0:T(1,128)S(4)} %get-tuple-element.23.start_, ...), custom_call_target="tpu_custom_call", output_to_operand_aliasing={{1}: (8, {}), {2}: (9, {}), {3}: (10, {}), {4}: (11, {}), {... | custom-call | tf_op jit(solution)/shard_map/operator/pallas_call | solution.py:269
  (2 shorter events, 0.0 us)
Async XLA Ops:
  0.0 18.5 %copy-start = (bf16[256,768]{1,0:T(8,128)(2,1)S(1)}, bf16[256,768]{1,0:T(8,128)(2,1)}, u32[]{:S(2)}) copy-start(bf16[256,768]{1,0:T(8,128)(2,1)} %refs_0_.1) | copy-start | bytes 1179652
  0.0 18.5 %copy-start.1 = (bf16[128,256]{1,0:T(8,128)(2,1)S(1)}, bf16[128,256]{1,0:T(8,128)(2,1)}, u32[]{:S(2)}) copy-start(bf16[128,256]{1,0:T(8,128)(2,1)} %restrict_ref.1) | copy-start | bytes 196612
  0.9 8.9 %collective-permute-start.3 = (bf16[272,128]{1,0:T(8,128)(2,1)S(1)}, bf16[272,128]{1,0:T(8,128)(2,1)S(1)}, u32[]{:S(2)}, u32[]{:S(2)}) collective-permute-start(bf16[272,128]{1,0:T(8,128)(2,1)S(1)} %pack.1.refs_0_), channel_id=1, source_target_pairs={{0,24},{2,26},{4,28},{6,30},{8,16},{10,18},{12,20},{14,22},{16,8},... | collective-permute-start | bytes 208904 | tf_op jit(solution)/shard_map/ppermute | solution.py:51
  6.1 4.9 %collective-permute-start.1 = (bf16[272,128]{1,0:T(8,128)(2,1)S(1)}, bf16[272,128]{1,0:T(8,128)(2,1)S(1)}, u32[]{:S(2)}, u32[]{:S(2)}) collective-permute-start(bf16[272,128]{1,0:T(8,128)(2,1)S(1)} %pack.1.refs_0_), channel_id=1, source_target_pairs={{0,8},{2,10},{4,12},{6,14},{8,0},{10,2},{12,4},{14,6},{16,24},{18,... | collective-permute-start | bytes 208904 | tf_op jit(solution)/shard_map/ppermute | solution.py:51
  6.1 6.5 %collective-permute-start = (bf16[272,128]{1,0:T(8,128)(2,1)S(1)}, bf16[272,128]{1,0:T(8,128)(2,1)S(1)}, u32[]{:S(2)}, u32[]{:S(2)}) collective-permute-start(bf16[272,128]{1,0:T(8,128)(2,1)S(1)} %pack.1.refs_0_), channel_id=1, source_target_pairs={{0,16},{2,18},{4,20},{6,22},{8,24},{10,26},{12,28},{14,30},{16,0},... | collective-permute-start | bytes 208904 | tf_op jit(solution)/shard_map/ppermute | solution.py:51
  6.7 8.4 %collective-permute-start.5 = (bf16[272,128]{1,0:T(8,128)(2,1)S(1)}, bf16[272,128]{1,0:T(8,128)(2,1)S(1)}, u32[]{:S(2)}, u32[]{:S(2)}) collective-permute-start(bf16[272,128]{1,0:T(8,128)(2,1)S(1)} %pack.1.refs_0_), channel_id=1, source_target_pairs={{0,4},{2,6},{4,0},{6,2},{8,12},{10,14},{12,8},{14,10},{16,20},{18,... | collective-permute-start | bytes 208904 | tf_op jit(solution)/shard_map/ppermute | solution.py:51
  8.4 10.1 %collective-permute-start.7 = (bf16[256,768]{1,0:T(8,128)(2,1)}, bf16[256,768]{1,0:T(8,128)(2,1)S(1)}, u32[]{:S(2)}, u32[]{:S(2)}) collective-permute-start(bf16[256,768]{1,0:T(8,128)(2,1)} %refs_0_.1), channel_id=1, source_target_pairs={{0,1},{1,0},{2,3},{3,2},{4,5},{5,4},{6,7},{7,6},{8,9},{9,8},{10,11... | collective-permute-start | bytes 1179656 | tf_op jit(solution)/shard_map/ppermute | solution.py:51
  9.9 5.4 %collective-permute-start.4 = (bf16[272,128]{1,0:T(8,128)(2,1)S(1)}, bf16[272,128]{1,0:T(8,128)(2,1)S(1)}, u32[]{:S(2)}, u32[]{:S(2)}) collective-permute-start(bf16[272,128]{1,0:T(8,128)(2,1)S(1)} %collective-permute-done.3.refs_2_), channel_id=1, source_target_pairs={{0,4},{2,6},{4,0},{6,2},{8,12},{10,14},{12,8},{14,10},{16,20},{18,... | collective-permute-start | bytes 208904 | tf_op jit(solution)/shard_map/ppermute | solution.py:51
  10.9 5.1 %collective-permute-start.2 = (bf16[272,128]{1,0:T(8,128)(2,1)S(1)}, bf16[272,128]{1,0:T(8,128)(2,1)S(1)}, u32[]{:S(2)}, u32[]{:S(2)}) collective-permute-start(bf16[272,128]{1,0:T(8,128)(2,1)S(1)} %collective-permute-done.1.refs_3_), channel_id=1, source_target_pairs={{0,4},{2,6},{4,0},{6,2},{8,12},{10,14},{12,8},{14,10},{16,20},{18,... | collective-permute-start | bytes 208904 | tf_op jit(solution)/shard_map/ppermute | solution.py:51
  12.6 4.3 %collective-permute-start.6 = (bf16[272,128]{1,0:T(8,128)(2,1)S(1)}, bf16[272,128]{1,0:T(8,128)(2,1)S(1)}, u32[]{:S(2)}, u32[]{:S(2)}) collective-permute-start(bf16[272,128]{1,0:T(8,128)(2,1)S(1)} %collective-permute-done.refs_1_), channel_id=1, source_target_pairs={{0,4},{2,6},{4,0},{6,2},{8,12},{10,14},{12,8},{14,10},{16,20},{18,... | collective-permute-start | bytes 208904 | tf_op jit(solution)/shard_map/ppermute | solution.py:51
  15.1 1.8 %collective-permute-start.9 = (bf16[1088,128]{1,0:T(8,128)(2,1)S(1)}, bf16[1088,128]{1,0:T(8,128)(2,1)S(1)}, u32[]{:S(2)}, u32[]{:S(2)}) collective-permute-start(bf16[1088,128]{1,0:T(8,128)(2,1)S(1)} %pad_maximum_fusion.1), channel_id=1, source_target_pairs={{0,2},{2,0},{4,6},{6,4},{8,10},{10,8},{12,14},{14,12},{16,18},{18,... | collective-permute-start | bytes 835592 | tf_op jit(solution)/shard_map/ppermute | solution.py:51
  16.9 1.6 %collective-permute-start.8 = (bf16[1088,128]{1,0:T(8,128)(2,1)S(1)}, bf16[1088,128]{1,0:T(8,128)(2,1)S(1)}, u32[]{:S(2)}, u32[]{:S(2)}) collective-permute-start(bf16[1088,128]{1,0:T(8,128)(2,1)S(1)} %pad_maximum_fusion), channel_id=1, source_target_pairs={{0,2},{2,0},{4,6},{6,4},{8,10},{10,8},{12,14},{14,12},{16,18},{18,... | collective-permute-start | bytes 835592 | tf_op jit(solution)/shard_map/ppermute | solution.py:51
